TPU v7x, 32 devices: a whole 2x2x4 slice. The times are simulated.
32 devices in a mesh: grp: 2 (over x), blk: 8 (over z, y), sub: 2 (over core).
Axes of the slice: x: 2, y: 2, z: 4, core: 2. Of those that a mesh axis runs over, the one named last changes fastest.
Arguments:
- spectra: bfloat16 [16, 2, 256, 2048], P('sub', None, None, ('grp', 'blk')), parts along dimension 3, may hold values from -6 to 6
- direction: int32 [2, 8], P(None, 'blk'), may hold values 0 or 1
Outputs:
- correlations: float32 [2, 16, 64, 128, 128], P(None, ('grp', 'blk'), 'sub'), parts along dimension 1
There are 2 independent parts, one for each index of `grp`. A program takes and returns all parts, laid end to end along the dimension named above; an argument that names none is the same for every part. Nothing has to cross between parts.
Inputs may be any that keep to these rules, and one draw needn't show every extreme that they name: direction[r, b] = 1 puts block b's partner in round r at block b + r + 1, 0 at block b - r - 1, modulo 8.
All inputs are finite; a program needn't handle non-finite values.
Results may differ from a plain program's by a relative error of at most 0.011.
Values may be sent and summed in bfloat16 or wider, within the bound.
No kernel may reach another device: no remote copies, remote signals or barrier semaphores. Data moves between devices by JAX's collectives and lax.ppermute only.
A program may use at most 128 MiB of HBM per device.

v0:
```python
import math

import jax
import jax.numpy as jnp
from jax import lax
from jax.sharding import PartitionSpec as P

LAGS = 64
ROUNDS = 2


def from_behind(x, axis, by):
    size = lax.axis_size(axis)
    return lax.ppermute(x, axis, [(i, (i + by) % size) for i in range(size)])


def make_table(bin_count, windows, lag_count):
    lags = jnp.arange(lag_count, dtype=jnp.int32) - lag_count // 2
    bins = jnp.arange(bin_count, dtype=jnp.int32)
    period = 2 * bin_count
    phase = bins[None, :] * ((lags[:, None] + period) % period) % period
    angle = phase.astype(jnp.float32) * (math.pi / bin_count)
    weight = (bin_count * windows) ** (-0.5)
    return (jnp.stack([jnp.cos(angle), -jnp.sin(angle)], axis=-1) * weight).astype(jnp.bfloat16)


def correlate(local_block, partner, lag_table):
    windows, _, bin_count, channels = local_block.shape
    swapped = jnp.stack([partner[:, 1], -partner[:, 0]], axis=1)
    operand = jnp.concatenate([partner, swapped], axis=-1)
    bin_block = min(128, bin_count)
    summed = jnp.zeros((lag_table.shape[0], channels, channels), jnp.float32)
    for first_bin in range(0, bin_count, bin_block):
        left_part = local_block[:, :, first_bin : first_bin + bin_block]
        right_part = operand[:, :, first_bin : first_bin + bin_block]
        cross_tile = jnp.einsum(
            "scfi,scfj->fij", left_part, right_part, preferred_element_type=jnp.bfloat16
        )
        cross_tile = cross_tile.reshape(bin_block, channels, 2, channels)
        table_part = lag_table[:, first_bin : first_bin + bin_block]
        summed = summed + jnp.einsum(
            "tfk,fikj->tij", table_part, cross_tile, preferred_element_type=jnp.float32
        )
    return summed


def per_device(spectra, direction):
    windows, _, bin_count, channels = spectra.shape
    lag_table = make_table(bin_count, windows * lax.axis_size("sub"), LAGS)
    ahead = spectra
    behind = spectra
    reduced_rounds = []
    for round_index in range(ROUNDS):
        ahead = from_behind(spectra, "blk", -(round_index + 1))
        behind = from_behind(spectra, "blk", round_index + 1)
        partner = jnp.where(direction[round_index, 0] == 1, ahead, behind)
        partial_lags = correlate(spectra, partner, lag_table)
        reduced_rounds.append(
            lax.psum_scatter(
                partial_lags.astype(jnp.bfloat16), "sub", scatter_dimension=0, tiled=True
            ).astype(jnp.float32)
        )
    reduced = jnp.stack(reduced_rounds, axis=0)
    return reduced[:, None]


def solution(mesh):
    return jax.shard_map(
        per_device,
        mesh=mesh,
        in_specs=(P("sub", None, None, ("grp", "blk")), P(None, "blk")),
        out_specs=P(None, ("grp", "blk"), "sub", None, None),
        check_vma=False,
    )
```

profile of v0, /device:TPU:0, one launch (start us, length us, event | category | flops | bytes accessed | tf_op | source)
XLA Modules:
  0.0 180.7 jit_solution(10108547325119340823)
XLA Ops:
  6.5 0.0 reduce-scatter.5.cloned.1.call-start
  6.5 3.0 %copy.3 = bf16[8,2,256,128]{3,0,1,2:T(8,128)(2,1)} copy(bf16[8,2,256,128]{3,2,1,0:T(8,128)(2,1)} %param.2) | data formatting | bytes 2097152 | tf_op args[0]
  9.5 5.0 %collective-permute-start.2 = (bf16[8,2,256,128]{3,0,1,2:T(8,128)(2,1)}, bf16[8,2,256,128]{3,0,1,2:T(8,128)(2,1)S(1)}, u32[]{:S(2)}, u32[]{:S(2)}) collective-permute-start(bf16[8,2,256,128]{3,0,1,2:T(8,128)(2,1)} %copy.3), channel_id=1, source_target_pairs={{0,12},{2,14},{4,0},{6,2},{8,4},{10,6},{12,8},{14,10},{1,13},{3,15... | collective-permute-start | bytes 3145736 | tf_op jit(solution)/shard_map/ppermute | solution.py:14
  14.6 0.0 collective-permute-start.3
  14.6 4.8 %collective-permute-start = (bf16[8,2,256,128]{3,0,1,2:T(8,128)(2,1)}, bf16[8,2,256,128]{3,0,1,2:T(8,128)(2,1)}, u32[]{:S(2)}, u32[]{:S(2)}) collective-permute-start(bf16[8,2,256,128]{3,0,1,2:T(8,128)(2,1)} %copy.3), channel_id=1, source_target_pairs={{0,14},{2,0},{4,2},{6,4},{8,6},{10,8},{12,10},{14,12},{1,15},{3,1}... | collective-permute-start | bytes 3145736 | tf_op jit(solution)/shard_map/ppermute | solution.py:14
  19.3 0.0 collective-permute-start.1
  19.3 0.3 fusion.18
  19.7 0.6 fusion.11
  20.3 1.4 fusion.28
  23.0 1.1 fusion.41
  24.0 1.9 %fusion.39 = bf16[8,2,128,128]{3,0,1,2:T(8,128)(2,1)} fusion(bf16[8,2,256,128]{3,0,1,2:T(8,128)(2,1)} %copy.3), kind=kLoop, calls=%fused_computation.16.clone.2 | loop fusion | bytes 1048576 | tf_op jit(solution)/shard_map/scfi,scfj->fij/dot_general | solution.py:36
  25.9 1.9 %fusion.45 = bf16[8,2,128,128]{3,0,1,2:T(8,128)(2,1)} fusion(bf16[8,2,256,128]{3,0,1,2:T(8,128)(2,1)} %copy.3), kind=kLoop, calls=%fused_computation.19.clone | loop fusion | bytes 1048576 | tf_op jit(solution)/shard_map/scfi,scfj->fij/dot_general | solution.py:36
  27.8 1.9 %fusion.43 = bf16[8,2,128,128]{3,0,1,2:T(8,128)(2,1)} fusion(bf16[8,2,256,128]{3,0,1,2:T(8,128)(2,1)} %copy.3), kind=kLoop, calls=%fused_computation.17.clone | loop fusion | bytes 1048576 | tf_op jit(solution)/shard_map/scfi,scfj->fij/dot_general | solution.py:36
  29.7 8.7 %collective-permute-done.2 = bf16[8,2,256,128]{3,0,1,2:T(8,128)(2,1)S(1)} collective-permute-done((bf16[8,2,256,128]{3,0,1,2:T(8,128)(2,1)}, bf16[8,2,256,128]{3,0,1,2:T(8,128)(2,1)S(1)}, u32[]{:S(2)}, u32[]{:S(2)}) %collective-permute-start.2) | collective-permute-done | bytes 1048608 | tf_op jit(solution)/shard_map/ppermute | solution.py:14
  38.4 23.3 %collective-permute-done.3 = bf16[8,2,256,128]{3,0,1,2:T(8,128)(2,1)S(1)} collective-permute-done((bf16[8,2,256,128]{3,0,1,2:T(8,128)(2,1)}, bf16[8,2,256,128]{3,0,1,2:T(8,128)(2,1)S(1)}, u32[]{:S(2)}, u32[]{:S(2)}) %collective-permute-start.3) | collective-permute-done | bytes 1048608 | tf_op jit(solution)/shard_map/ppermute | solution.py:14
  61.7 0.1 broadcast_select_fusion
  61.9 0.1 fusion.27
  62.0 6.8 %fusion.4 = bf16[128,256,128,1]{2,1,3,0:T(8,128)(2,1)} fusion(bf16[8,1,256,128]{3,0,1,2:T(8,128)(2,1)S(1)} %get-tuple-element.8, bf16[8,1,256,128]{3,0,1,2:T(8,128)(2,1)S(1)} %get-tuple-element.7, bf16[8,2,256,128]{3,0,1,2:T(8,128)(2,1)S(1)} %broadcast_select_fusion, bf16[8,2,128,128]{3,0,1,2:T(8,128)(2,1)S(1)} %fusion.41), kind=kOutput, calls=%fused_computation.11 | convolution fusion | flops 140509184 | bytes 11010048 | tf_op jit(solution)/shard_map/scfi,scfj->fij/dot_general | solution.py:36
  68.9 12.4 %copy.11 = bf16[128,128,2,128]{3,0,2,1:T(8,128)(2,1)} copy(bf16[128,128,2,128]{1,3,2,0:T(8,128)(2,1)} %bitcast.68) | data formatting | bytes 16777216 | tf_op jit(solution)/shard_map/reshape | solution.py:39
  81.2 0.0 copy-done.6
  81.2 6.8 %fusion.3 = bf16[128,256,128,1]{2,1,3,0:T(8,128)(2,1)} fusion(bf16[8,1,256,128]{3,0,1,2:T(8,128)(2,1)S(1)} %get-tuple-element.8, bf16[8,1,256,128]{3,0,1,2:T(8,128)(2,1)S(1)} %get-tuple-element.7, bf16[8,2,256,128]{3,0,1,2:T(8,128)(2,1)S(1)} %broadcast_select_fusion, bf16[8,2,128,128]{3,0,1,2:T(8,128)(2,1)S(1)} %copy-done.6), kind=kOutput, calls=%fused_computation.10 | convolution fusion | flops 140509184 | bytes 11010048 | tf_op jit(solution)/shard_map/scfi,scfj->fij/dot_general | solution.py:36
  88.1 12.4 %copy.12 = bf16[128,128,2,128]{3,0,2,1:T(8,128)(2,1)} copy(bf16[128,128,2,128]{1,3,2,0:T(8,128)(2,1)} %bitcast.67) | data formatting | bytes 16777216 | tf_op jit(solution)/shard_map/reshape | solution.py:39
  100.5 0.0 copy-done.2
  100.5 5.1 %fusion.19 = f32[64,128,128,1]{2,0,3,1:T(8,128)S(1)} fusion(bf16[128,128,2,128]{3,0,2,1:T(8,128)(2,1)} %copy.11, bf16[64,256,2]{1,0,2:T(8,128)(2,1)S(1)} %copy-done.2), kind=kOutput, calls=%fused_computation.35 | convolution fusion | flops 536870912 | bytes 12615680 | tf_op jit(solution)/shard_map/tfk,fikj->tij/dot_general | solution.py:41
  105.6 0.7 copy-done.1
  106.3 2.9 %fusion = bf16[64,128,128]{2,0,1:T(8,128)(2,1)} fusion(f32[64,128,128,1]{2,0,3,1:T(8,128)S(1)} %fusion.19, bf16[128,128,2,128]{3,0,2,1:T(8,128)(2,1)S(1)} %copy-done.1, bf16[64,256,2]{1,0,2:T(8,128)(2,1)S(1)} %copy-done.2), kind=kOutput, calls=%fused_computation.1 | convolution fusion | flops 538968064 | bytes 14712832 | tf_op jit(solution)/shard_map/tfk,fikj->tij/dot_general | solution.py:41
  109.2 0.0 reduce-scatter.5.cloned.1.call-update
  109.2 0.2 reduce-scatter.3.cloned.1.call-start
  109.5 0.0 collective-permute-done
  109.5 0.0 collective-permute-done.1
  109.5 1.4 broadcast_select_fusion.1
  110.8 0.1 fusion.26
  111.0 0.0 copy-done.5
  111.0 0.0 copy-start.4
  111.0 6.8 %fusion.6 = bf16[128,256,128,1]{2,1,3,0:T(8,128)(2,1)} fusion(bf16[8,1,256,128]{3,0,1,2:T(8,128)(2,1)S(1)} %get-tuple-element.6, bf16[8,1,256,128]{3,0,1,2:T(8,128)(2,1)S(1)} %get-tuple-element.5, bf16[8,2,256,128]{3,0,1,2:T(8,128)(2,1)S(1)} %broadcast_select_fusion.1, bf16[8,2,128,128]{3,0,1,2:T(8,128)(2,1)S(1)} %copy-done.5), kind=kOutput, calls=%fused_computation.13 | convolution fusion | flops 140509184 | bytes 11010048 | tf_op jit(solution)/shard_map/scfi,scfj->fij/dot_general | solution.py:36
  117.8 0.0 copy-done.4
  117.8 6.8 %fusion.5 = bf16[128,256,128,1]{2,1,3,0:T(8,128)(2,1)} fusion(bf16[8,1,256,128]{3,0,1,2:T(8,128)(2,1)S(1)} %get-tuple-element.6, bf16[8,1,256,128]{3,0,1,2:T(8,128)(2,1)S(1)} %get-tuple-element.5, bf16[8,2,256,128]{3,0,1,2:T(8,128)(2,1)S(1)} %broadcast_select_fusion.1, bf16[8,2,128,128]{3,0,1,2:T(8,128)(2,1)S(1)} %copy-done.4), kind=kOutput, calls=%fused_computation.12 | convolution fusion | flops 140509184 | bytes 11010048 | tf_op jit(solution)/shard_map/scfi,scfj->fij/dot_general | solution.py:36
  124.7 12.3 %copy.6 = bf16[128,128,2,128]{3,0,2,1:T(8,128)(2,1)} copy(bf16[128,128,2,128]{1,3,2,0:T(8,128)(2,1)} %bitcast.65) | data formatting | bytes 16777216 | tf_op jit(solution)/shard_map/reshape | solution.py:39
  137.0 12.4 %copy.8 = bf16[128,128,2,128]{3,0,2,1:T(8,128)(2,1)} copy(bf16[128,128,2,128]{1,3,2,0:T(8,128)(2,1)} %bitcast.66) | data formatting | bytes 16777216 | tf_op jit(solution)/shard_map/reshape | solution.py:39
  149.4 0.0 copy-done.3
  149.4 5.1 %fusion.20 = f32[64,128,128,1]{2,0,3,1:T(8,128)S(1)} fusion(bf16[128,128,2,128]{3,0,2,1:T(8,128)(2,1)} %copy.6, bf16[64,256,2]{1,0,2:T(8,128)(2,1)S(1)} %copy-done.3), kind=kOutput, calls=%fused_computation.36 | convolution fusion | flops 536870912 | bytes 12615680 | tf_op jit(solution)/shard_map/tfk,fikj->tij/dot_general | solution.py:41
  154.5 0.7 copy-done
  155.2 2.9 %fusion.1 = bf16[64,128,128]{2,0,1:T(8,128)(2,1)} fusion(f32[64,128,128,1]{2,0,3,1:T(8,128)S(1)} %fusion.20, bf16[128,128,2,128]{3,0,2,1:T(8,128)(2,1)S(1)} %copy-done, bf16[64,256,2]{1,0,2:T(8,128)(2,1)S(1)} %copy-done.3), kind=kOutput, calls=%fused_computation.3 | convolution fusion | flops 538968064 | bytes 14712832 | tf_op jit(solution)/shard_map/tfk,fikj->tij/dot_general | solution.py:41
  158.1 0.0 reduce-scatter.3.cloned.1.call-update
  158.2 0.0 reduce-scatter.5.cloned.1.call-done
  158.2 9.4 %reduce-scatter.3.cloned.1.call-done = bf16[32,128,128]{2,0,1:T(8,128)(2,1)} async-done(((bf16[64,128,128]{2,0,1:T(8,128)(2,1)}), bf16[32,128,128]{2,0,1:T(8,128)(2,1)}) %reduce-scatter.3.cloned.1.call-update) | async-done | bytes 1048592 | tf_op jit(solution)/shard_map/reduce_scatter | solution.py:59
  167.6 1.8 %fusion.2 = f32[2,1,32,128,128]{4,2,3,0,1:T(8,128)S(1)} fusion(bf16[1,32,128,128]{3,1,2,0:T(8,128)(2,1)} %bitcast.69, bf16[1,32,128,128]{3,1,2,0:T(8,128)(2,1)} %bitcast.70), kind=kLoop, calls=%fused_computation.7 | loop fusion | flops 2097152 | bytes 6291456 | tf_op jit(solution)/shard_map/broadcast_in_dim | solution.py:64
  169.4 4.4 %copy.13 = f32[2,1,32,128,128]{4,3,2,1,0:T(8,128)} copy(f32[2,1,32,128,128]{4,2,3,0,1:T(8,128)S(1)} %fusion.2) | data formatting | bytes 8388608 | tf_op jit(solution)/shard_map/broadcast_in_dim | solution.py:64
  (7 shorter events, 0.0 us)
Async XLA Ops:
  6.5 151.7 %reduce-scatter.5.cloned.1.call-start = ((), (), s32[]{:S(2)}) async-start(), calls=%async_computation.3 | async-start | bytes 3145728 | tf_op jit(solution)/shard_map/reduce_scatter | solution.py:59
  9.5 28.9 %collective-permute-start.2 = (bf16[8,2,256,128]{3,0,1,2:T(8,128)(2,1)}, bf16[8,2,256,128]{3,0,1,2:T(8,128)(2,1)S(1)}, u32[]{:S(2)}, u32[]{:S(2)}) collective-permute-start(bf16[8,2,256,128]{3,0,1,2:T(8,128)(2,1)} %copy.3), channel_id=1, source_target_pairs={{0,12},{2,14},{4,0},{6,2},{8,4},{10,6},{12,8},{14,10},{1,13},{3,15... | collective-permute-start | bytes 3145736 | tf_op jit(solution)/shard_map/ppermute | solution.py:14
  14.6 47.2 %collective-permute-start.3 = (bf16[8,2,256,128]{3,0,1,2:T(8,128)(2,1)}, bf16[8,2,256,128]{3,0,1,2:T(8,128)(2,1)S(1)}, u32[]{:S(2)}, u32[]{:S(2)}) collective-permute-start(bf16[8,2,256,128]{3,0,1,2:T(8,128)(2,1)} %copy.3), channel_id=1, source_target_pairs={{0,4},{2,6},{4,8},{6,10},{8,12},{10,14},{12,0},{14,2},{1,5},{3,7},... | collective-permute-start | bytes 3145736 | tf_op jit(solution)/shard_map/ppermute | solution.py:14
  14.6 94.9 %collective-permute-start = (bf16[8,2,256,128]{3,0,1,2:T(8,128)(2,1)}, bf16[8,2,256,128]{3,0,1,2:T(8,128)(2,1)}, u32[]{:S(2)}, u32[]{:S(2)}) collective-permute-start(bf16[8,2,256,128]{3,0,1,2:T(8,128)(2,1)} %copy.3), channel_id=1, source_target_pairs={{0,14},{2,0},{4,2},{6,4},{8,6},{10,8},{12,10},{14,12},{1,15},{3,1}... | collective-permute-start | bytes 3145736 | tf_op jit(solution)/shard_map/ppermute | solution.py:14
  19.3 90.1 %collective-permute-start.1 = (bf16[8,2,256,128]{3,0,1,2:T(8,128)(2,1)}, bf16[8,2,256,128]{3,0,1,2:T(8,128)(2,1)}, u32[]{:S(2)}, u32[]{:S(2)}) collective-permute-start(bf16[8,2,256,128]{3,0,1,2:T(8,128)(2,1)} %copy.3), channel_id=1, source_target_pairs={{0,2},{2,4},{4,6},{6,8},{8,10},{10,12},{12,14},{14,0},{1,3},{3,5},... | collective-permute-start | bytes 3145736 | tf_op jit(solution)/shard_map/ppermute | solution.py:14
  68.9 12.4 %copy-start.6 = (bf16[8,2,128,128]{3,0,1,2:T(8,128)(2,1)S(1)}, bf16[8,2,128,128]{3,0,1,2:T(8,128)(2,1)}, u32[]{:S(2)}) copy-start(bf16[8,2,128,128]{3,0,1,2:T(8,128)(2,1)} %fusion.39) | copy-start | bytes 1572868
  88.1 12.4 %copy-start.2 = (bf16[64,256,2]{1,0,2:T(8,128)(2,1)S(1)}, bf16[64,256,2]{1,0,2:T(8,128)(2,1)}, u32[]{:S(2)}) copy-start(bf16[64,256,2]{1,0,2:T(8,128)(2,1)} %fusion.11) | copy-start | bytes 196612
  100.5 5.8 %copy-start.1 = (bf16[128,128,2,128]{3,0,2,1:T(8,128)(2,1)S(1)}, bf16[128,128,2,128]{3,0,2,1:T(8,128)(2,1)}, u32[]{:S(2)}) copy-start(bf16[128,128,2,128]{3,0,2,1:T(8,128)(2,1)} %copy.12) | copy-start | bytes 25165828
  109.2 1.8 copy-start.5
  109.2 58.4 %reduce-scatter.3.cloned.1.call-start = ((), (), s32[]{:S(2)}) async-start(), calls=%async_computation.2 | async-start | bytes 3145728 | tf_op jit(solution)/shard_map/reduce_scatter | solution.py:59
  111.0 6.9 %copy-start.4 = (bf16[8,2,128,128]{3,0,1,2:T(8,128)(2,1)S(1)}, bf16[8,2,128,128]{3,0,1,2:T(8,128)(2,1)}, u32[]{:S(2)}) copy-start(bf16[8,2,128,128]{3,0,1,2:T(8,128)(2,1)} %fusion.43) | copy-start | bytes 1572868
  137.0 12.4 %copy-start.3 = (bf16[64,256,2]{1,0,2:T(8,128)(2,1)S(1)}, bf16[64,256,2]{1,0,2:T(8,128)(2,1)}, u32[]{:S(2)}) copy-start(bf16[64,256,2]{1,0,2:T(8,128)(2,1)} %fusion.11) | copy-start | bytes 196612
  149.4 5.8 %copy-start = (bf16[128,128,2,128]{3,0,2,1:T(8,128)(2,1)S(1)}, bf16[128,128,2,128]{3,0,2,1:T(8,128)(2,1)}, u32[]{:S(2)}) copy-start(bf16[128,128,2,128]{3,0,2,1:T(8,128)(2,1)} %copy.8) | copy-start | bytes 25165828
Sparse Core Ops, SparseCore 0:
  109.3 9.2 reduce-scatter.4
  158.3 9.2 reduce-scatter.2
where the time goes:
time: 182 us; the launch traced here: 181 us
  local copies, waits for them, and re-layouts  66.4 us (36%)
  matrix products  43.4 us (24%)
  waiting for transfers between devices  41.5 us (23%)
  between operations  14.8 us (8%)
  starting transfers between devices  10.1 us (6%)
  other arithmetic  4.52 us (2%)
    reshape x4, local copies, waits for them, and re-layouts, correlate(): cross_tile = cross_tile.reshape(bin_block, channels, 2, channels)  49.5 us
    ppermute x4, waiting for transfers between devices, from_behind(): return lax.ppermute(x, axis, [(i, (i + by) % size) for i in range(size)])  32.1 us
    dot_general x4, matrix products, correlate(): jnp.einsum('scfi,scfj->fij', left_part, right_part, preferred_element_typ...  27.4 us
    dot_general x4, matrix products, correlate(): jnp.einsum('tfk,fikj->tij', table_part, cross_tile, preferred_element_typ...  16.1 us
    ppermute x4, starting transfers between devices, from_behind(): return lax.ppermute(x, axis, [(i, (i + by) % size) for i in range(size)])  9.83 us
    reduce_scatter x2, waiting for transfers between devices, per_device(): lax.psum_scatter(partial_lags.astype(jnp.bfloat16), 'sub', scatter_dimens...  9.42 us
    dot_general x4, local copies, waits for them, and re-layouts, correlate(): jnp.einsum('scfi,scfj->fij', left_part, right_part, preferred_element_typ...  6.73 us
    broadcast_in_dim x1, local copies, waits for them, and re-layouts, per_device(): return reduced[:, None]  4.44 us
  transfers between devices with their start and end apart: 6, of which 3 were waited for; matrix products, arithmetic and copies ran while one was open for 57% of the time, Pallas kernels for 0%

commit v1 on v0

v1 whole, which is shorter than its diff:
```python
import functools
import math

import jax
import jax.numpy as jnp
from jax import lax
from jax.experimental import pallas as pl
from jax.experimental.pallas import tpu as pltpu
from jax.sharding import PartitionSpec as P

LAGS = 64
ROUNDS = 2
GROUP = 8
CHANNEL_BLOCK = 32
CHUNKS = (64, 64, 64, 64)
VMEM = 56 * 2**20


def ring_shift(x, axis, by):
    size = lax.axis_size(axis)
    return lax.ppermute(x, axis, [(i, (i + by) % size) for i in range(size)])


def pair_swap(x, axis):
    size = lax.axis_size(axis)
    return lax.ppermute(x, axis, [(i, i ^ 1) for i in range(size)])


def make_table(bin_count, windows, first_lag, lag_count):
    lags = jnp.arange(lag_count, dtype=jnp.int32) + first_lag
    bins = jnp.arange(bin_count, dtype=jnp.int32)
    period = 2 * bin_count
    phase = bins[None, :] * ((lags[:, None] + period) % period) % period
    angle = phase.astype(jnp.float32) * (math.pi / bin_count)
    weight = (bin_count * windows) ** (-0.5)
    both = jnp.stack([jnp.cos(angle), -jnp.sin(angle)], axis=1) * weight
    both = both.astype(jnp.bfloat16).reshape(lag_count, 2, bin_count // GROUP, GROUP)
    return both.transpose(0, 2, 1, 3).reshape(lag_count, 2 * bin_count)


def lag_kernel(table, re_own, re_other, im_own, im_other, p0_own, p0_other, p1_own, p1_other, *rest, has_total):
    if has_total:
        total, out, cross = rest
    else:
        out, cross = rest
    rows, depth = re_own.shape
    tile = GROUP * 16
    lag_count = table.shape[0]
    bin_of_row = lax.broadcasted_iota(jnp.int32, (GROUP, tile), 0)
    bin_of_lane = lax.broadcasted_iota(jnp.int32, (GROUP, tile), 1) // (tile // GROUP)
    same_bin = bin_of_row == bin_of_lane

    def spread(ref, i, lanes):
        return jnp.where(same_bin, jnp.broadcast_to(ref[i : i + 1, lanes], (GROUP, tile)), 0.0)

    for g in range(depth // tile):
        lanes = slice(g * tile, (g + 1) * tile)
        pieces = []
        for i in range(rows):
            own = jnp.concatenate([spread(re_own, i, lanes), spread(im_own, i, lanes)], axis=0)
            other = jnp.concatenate([spread(re_other, i, lanes), spread(im_other, i, lanes)], axis=0)
            pieces.append(jnp.concatenate([own, other], axis=1).astype(jnp.bfloat16))
        left = jnp.concatenate(pieces, axis=0)
        right = jnp.concatenate(
            [
                jnp.concatenate([p0_own[lanes, :], p1_own[lanes, :]], axis=1),
                jnp.concatenate([p0_other[lanes, :], p1_other[lanes, :]], axis=1),
            ],
            axis=0,
        )
        part = jnp.dot(left, right, preferred_element_type=jnp.float32).astype(jnp.bfloat16)
        cross[:, g * 2 * GROUP : (g + 1) * 2 * GROUP, :] = part.reshape(rows, 2 * GROUP, part.shape[-1])

    for first in range(0, rows, 8):
        lagged = [
            jnp.dot(table[...], cross[i], preferred_element_type=jnp.float32) for i in range(first, first + 8)
        ]
        for r in range(ROUNDS):
            width = p0_own.shape[1]
            stacked = jnp.stack([x[:, r * width : (r + 1) * width] for x in lagged], axis=0)
            tile_out = jnp.swapaxes(stacked, 0, 1)
            if has_total:
                tile_out = tile_out + total[r, :, first : first + 8, :]
            out[r, :, first : first + 8, :] = tile_out


def add_lags(table, local, partners, total):
    lag_count, cross_depth = table.shape
    channels, depth = local[0].shape
    width = partners[0].shape[1]
    block = CHANNEL_BLOCK
    whole = lambda b: (0, 0)
    part = lambda b: (b, 0)
    out_spec = pl.BlockSpec((ROUNDS, lag_count, block, width), lambda b: (0, 0, b, 0))
    in_specs = [pl.BlockSpec((lag_count, cross_depth), whole)]
    in_specs += [pl.BlockSpec((block, depth), part) for _ in local]
    in_specs += [pl.BlockSpec((depth, width), whole) for _ in partners]
    operands = [table, *local, *partners]
    aliases = {}
    if total is not None:
        in_specs.append(out_spec)
        aliases = {len(operands): 0}
        operands.append(total)
    out_shape = jax.ShapeDtypeStruct((ROUNDS, lag_count, channels, width), jnp.float32)
    return pl.pallas_call(
        functools.partial(lag_kernel, has_total=total is not None),
        grid=(channels // block,),
        in_specs=in_specs,
        out_specs=out_spec,
        out_shape=out_shape,
        input_output_aliases=aliases,
        scratch_shapes=[pltpu.VMEM((block, cross_depth, ROUNDS * width), jnp.bfloat16)],
        compiler_params=pltpu.CompilerParams(vmem_limit_bytes=VMEM),
        cost_estimate=pl.CostEstimate(
            flops=2 * channels * cross_depth * 256 * 256, bytes_accessed=8 * 2**20, transcendentals=0
        ),
    )(*operands)


def bins_first_kernel(x, *outs, sizes, first):
    for out, size in zip(outs, sizes):
        for low in range(0, size, 16):
            at = slice(first + low, first + low + 16)
            slabs = [x[s, c, at, :].astype(jnp.float32) for c in range(2) for s in range(x.shape[0])]
            turned = jnp.swapaxes(jnp.stack(slabs, axis=0), 0, 1)
            rows = turned.reshape(16 * len(slabs), x.shape[3]).astype(out.dtype)
            out[low * len(slabs) : (low + 16) * len(slabs), :] = rows
        first += size


def bins_first(x, first, sizes):
    windows, parts, bins, channels = x.shape
    read = bins if first else sum(sizes)
    return pl.pallas_call(
        functools.partial(bins_first_kernel, sizes=sizes, first=first),
        grid=(1,),
        in_specs=[pl.BlockSpec((windows, parts, read, channels), lambda b: (0, 0, 0, 0))],
        out_specs=[pl.BlockSpec((size * parts * windows, channels), lambda b: (0, 0)) for size in sizes],
        out_shape=[jax.ShapeDtypeStruct((size * parts * windows, channels), x.dtype) for size in sizes],
        compiler_params=pltpu.CompilerParams(vmem_limit_bytes=VMEM),
    )(x)


def channels_first_kernel(*refs, count):
    ins, outs = refs[: 2 * count], refs[2 * count :]
    for n in range(2 * count):
        rows, channels = ins[n].shape
        for low in range(0, rows, 128):
            tile = ins[n][low : low + 128, :].astype(jnp.float32).T
            lane = lax.broadcasted_iota(jnp.int32, tile.shape, 1)
            real_lane = lane % 16 < 8
            outs[n][:, low : low + 128] = tile
            swapped = jnp.where(real_lane, -pltpu.roll(tile, 128 - 8, 1), pltpu.roll(tile, 8, 1))
            outs[2 * count + n][:, low : low + 128] = swapped


def channels_first(own, other):
    shapes = [jax.ShapeDtypeStruct(x.shape[::-1], jnp.float32) for x in (*own, *other)]
    outs = pl.pallas_call(
        functools.partial(channels_first_kernel, count=len(own)),
        out_shape=shapes + shapes,
        compiler_params=pltpu.CompilerParams(vmem_limit_bytes=VMEM),
    )(*own, *other)
    count = len(own)
    return [[outs[n], outs[count + n], outs[2 * count + n], outs[3 * count + n]] for n in range(count)]


def choose_kernel(picks, mine, behind, ahead, *rest):
    far, near = rest[-2:]
    far[...] = jnp.where(picks[0] == 1, ahead[...], behind[...])
    near[...] = jnp.where(picks[1] == 1, mine[...], jnp.where(picks[2] == 1, behind[...], ahead[...]))


def choose(picks, mine, behind, ahead, after):
    vmem = pl.BlockSpec(memory_space=pltpu.VMEM)
    return pl.pallas_call(
        choose_kernel,
        in_specs=[pl.BlockSpec(memory_space=pltpu.SMEM), vmem, vmem, vmem]
        + [pl.BlockSpec(memory_space=pl.ANY)] * len(after),
        out_specs=[vmem, vmem],
        out_shape=[jax.ShapeDtypeStruct(mine.shape, mine.dtype)] * 2,
        compiler_params=pltpu.CompilerParams(vmem_limit_bytes=VMEM),
    )(picks, mine, behind, ahead, *after)


def per_device(spectra, direction):
    windows, _, bin_count, channels = spectra.shape
    cores = lax.axis_size("sub")
    lag_count = LAGS // cores
    odd = lax.axis_index("blk") % 2
    near_of_pair = pair_swap(direction[0], "blk")[0]
    picks = jnp.stack([direction[1, 0], jnp.where(odd == 1, near_of_pair, 1 - near_of_pair), odd])

    table = make_table(bin_count, windows * cores, lax.axis_index("sub") * lag_count - LAGS // 2, lag_count)

    mine = bins_first(spectra, 0, CHUNKS[:1]) + bins_first(spectra, CHUNKS[0], CHUNKS[1:])
    behind = [ring_shift(x, "blk", 2) for x in mine]
    ahead = [ring_shift(x, "blk", -2) for x in mine]
    other = [ring_shift(x, "sub", 1) for x in mine]
    local = channels_first(mine, other)

    totals = [None]
    first = 0
    for n, size in enumerate(CHUNKS):
        after = [totals[n - 1]] if n >= 2 else []
        far_own, passed_on = choose(picks, mine[n], behind[n], ahead[n], after)
        near_own = pair_swap(passed_on, "blk")
        far_other = ring_shift(far_own, "sub", 1)
        near_other = ring_shift(near_own, "sub", 1)
        table_part = table[:, 2 * first : 2 * (first + size)]
        totals.append(add_lags(table_part, local[n], [near_own, near_other, far_own, far_other], totals[-1]))
        first += size
    return totals[-1][:, None]


def solution(mesh):
    return jax.shard_map(
        per_device,
        mesh=mesh,
        in_specs=(P("sub", None, None, ("grp", "blk")), P(None, "blk")),
        out_specs=P(None, ("grp", "blk"), "sub", None, None),
        check_vma=False,
    )
```

time: 182 us -> 108 us (0.59)
  local copies, waits for them, and re-layouts: 66.4 us -> 9.44 us
  Pallas kernels: 0 us -> 48.7 us
  matrix products: 43.4 us -> 0 us
  waiting for transfers between devices: 41.5 us -> 16.7 us
  starting transfers between devices: 10.1 us -> 28.6 us
  between operations: 14.8 us -> 1.68 us
  other arithmetic: 4.52 us -> 1.87 us
    reshape x4 -> x0, local copies, waits for them, and re-layouts: 49.5 us -> none  [correlate(): cross_tile = cross_tile.reshape(bin_block, channels, 2, channels)]
    pallas_call x0 -> x11, Pallas kernels: none -> 48.7 us  [the longest x4 31.2 us: add_lags(): pl.pallas_call(functools.partial(lag_kernel, has_total=total is not None)...]
    dot_general x8 -> x0, matrix products: 43.4 us -> none  [the longest x4 27.4 us: correlate(): jnp.einsum('scfi,scfj->fij', left_part, right_part, preferred_element_typ...]
    ppermute x4 -> x25, starting transfers between devices: 9.83 us -> 28.6 us  [the longest x20 21.6 us: ring_shift(): return lax.ppermute(x, axis, [(i, (i + by) % size) for i in range(size)])]
    ppermute x4 -> x25, waiting for transfers between devices: 32.1 us -> 16.7 us  [the longest x20 9.09 us: ring_shift(): return lax.ppermute(x, axis, [(i, (i + by) % size) for i in range(size)])]
    reduce_scatter x2 -> x0, waiting for transfers between devices: 9.42 us -> none  [per_device(): lax.psum_scatter(partial_lags.astype(jnp.bfloat16), 'sub', scatter_dimens...]
    dot_general x4 -> x0, local copies, waits for them, and re-layouts: 6.73 us -> none  [correlate(): jnp.einsum('scfi,scfj->fij', left_part, right_part, preferred_element_typ...]
    broadcast_in_dim x1 -> x0, local copies, waits for them, and re-layouts: 4.44 us -> none  [per_device(): return reduced[:, None]]
  transfers between devices with their start and end apart: 6 -> 25, of which waited for: 3 -> 5; matrix products, arithmetic and copies ran while one was open for 57% -> 6% of each run, Pallas kernels for 0% -> 36%
where the time goes in v1:
time: 108 us; the launch traced here: 107 us
  Pallas kernels  48.7 us (45%)
  starting transfers between devices  28.6 us (26%)
  waiting for transfers between devices  16.7 us (15%)
  local copies, waits for them, and re-layouts  9.44 us (9%)
  other arithmetic  1.87 us (2%)
  between operations  1.68 us (2%)
    pallas_call x4, Pallas kernels, add_lags(): pl.pallas_call(functools.partial(lag_kernel, has_total=total is not None)...  31.2 us
    ppermute x20, starting transfers between devices, ring_shift(): return lax.ppermute(x, axis, [(i, (i + by) % size) for i in range(size)])  21.6 us
    ppermute x20, waiting for transfers between devices, ring_shift(): return lax.ppermute(x, axis, [(i, (i + by) % size) for i in range(size)])  9.09 us
    pallas_call x4, Pallas kernels, choose(): pl.pallas_call(choose_kernel, in_specs=[pl.BlockSpec(memory_space=pltpu.S...  8.34 us
    unnamed x56, local copies, waits for them, and re-layouts  8.12 us
    ppermute x5, waiting for transfers between devices, pair_swap(): return lax.ppermute(x, axis, [(i, i ^ 1) for i in range(size)])  7.57 us
    ppermute x5, starting transfers between devices, pair_swap(): return lax.ppermute(x, axis, [(i, i ^ 1) for i in range(size)])  7.05 us
    pallas_call x1, Pallas kernels, channels_first(): pl.pallas_call(functools.partial(channels_first_kernel, count=len(own)),...  5.1 us
  transfers between devices with their start and end apart: 25, of which 5 were waited for; matrix products, arithmetic and copies ran while one was open for 6% of the time, Pallas kernels for 36%

profile of v1, /device:TPU:0, one launch (start us, length us, event | category | flops | bytes accessed | tf_op | source)
XLA Modules:
  0.0 107.0 jit_solution(10942168991774960725)
XLA Ops:
  0.0 1.8 %shard_map.28.refs_0_.mine = bf16[1024,128]{1,0:T(8,128)(2,1)} custom-call(bf16[8,2,256,128]{3,2,1,0:T(8,128)(2,1)} %x.3), custom_call_target="tpu_custom_call" | custom-call | tf_op jit(solution)/shard_map/pallas_call | solution.py:134
  1.8 3.0 %collective-permute-start.12 = (bf16[1024,128]{1,0:T(8,128)(2,1)}, bf16[1024,128]{1,0:T(8,128)(2,1)S(1)}, u32[]{:S(2)}, u32[]{:S(2)}) collective-permute-start(bf16[1024,128]{1,0:T(8,128)(2,1)} %shard_map.28.refs_0_.mine), channel_id=1, source_target_pairs={{0,4},{2,6},{4,8},{6,10},{8,12},{10,14},{12,0},{14,2},{1,5},{3,7},... | collective-permute-start | bytes 786440 | tf_op jit(solution)/shard_map/ppermute | solution.py:21
  4.8 2.0 %collective-permute-start.13 = (bf16[1024,128]{1,0:T(8,128)(2,1)}, bf16[1024,128]{1,0:T(8,128)(2,1)S(1)}, u32[]{:S(2)}, u32[]{:S(2)}) collective-permute-start(bf16[1024,128]{1,0:T(8,128)(2,1)} %shard_map.28.refs_0_.mine), channel_id=1, source_target_pairs={{0,12},{2,14},{4,0},{6,2},{8,4},{10,6},{12,8},{14,10},{1,13},{3,15... | collective-permute-start | bytes 786440 | tf_op jit(solution)/shard_map/ppermute | solution.py:21
  6.8 2.3 %shard_map.29 = (bf16[1024,128]{1,0:T(8,128)(2,1)}, bf16[1024,128]{1,0:T(8,128)(2,1)}, bf16[1024,128]{1,0:T(8,128)(2,1)}) custom-call(bf16[8,2,256,128]{3,2,1,0:T(8,128)(2,1)} %x.3), custom_call_target="tpu_custom_call" | custom-call | tf_op jit(solution)/shard_map/pallas_call | solution.py:134
  9.1 1.3 %fusion.7 = (s32[1,1]{0,1:T(1,128)}, s32[1,1]{0,1:T(1,128)}) fusion(s32[2,1]{0,1:T(1,128)} %param.3), kind=kLoop, calls=%fused_computation.19 | loop fusion | bytes 16 | tf_op jit(solution)/shard_map/slice | solution.py:192
  10.4 1.7 %collective-permute-start.4 = (s32[1]{0:T(128)}, s32[1]{0:T(128)}, u32[]{:S(2)}, u32[]{:S(2)}) collective-permute-start(s32[1]{0:T(128)} %bitcast.3), channel_id=1, source_target_pairs={{0,2},{2,0},{4,6},{6,4},{8,10},{10,8},{12,14},{14,12},{1,3},{3,1},... | collective-permute-start | bytes 20 | tf_op jit(solution)/shard_map/ppermute | solution.py:26
  12.2 2.0 %collective-permute-done.4 = s32[1]{0:T(128)} collective-permute-done((s32[1]{0:T(128)}, s32[1]{0:T(128)}, u32[]{:S(2)}, u32[]{:S(2)}) %collective-permute-start.4) | collective-permute-done | bytes 36 | tf_op jit(solution)/shard_map/ppermute | solution.py:26
  14.1 3.8 %collective-permute-start.8 = (bf16[1024,128]{1,0:T(8,128)(2,1)}, bf16[1024,128]{1,0:T(8,128)(2,1)S(1)}, u32[]{:S(2)}, u32[]{:S(2)}) collective-permute-start(bf16[1024,128]{1,0:T(8,128)(2,1)} %get-tuple-element.32.refs_1_.mine), channel_id=1, source_target_pairs={{0,12},{2,14},{4,0},{6,2},{8,4},{10,6},{12,8},{14,10},{1,13},{3,15... | collective-permute-start | bytes 786440 | tf_op jit(solution)/shard_map/ppermute | solution.py:21
  19.3 1.2 %pad_add_fusion.picks = s32[3]{0:T(128)} fusion(s32[1]{0:T(128)} %bitcast.6, s32[1]{0:T(128)} %bitcast.5, s32[1]{0:T(128)} %bitcast.2), kind=kLoop, calls=%fused_computation.17 | loop fusion | flops 6 | bytes 24 | tf_op jit(solution)/shard_map/stack | solution.py:192
  20.6 0.5 collective-permute-start.3
  21.1 0.2 copy-done.17
  21.3 2.1 %shard_map.32 = (bf16[1024,128]{1,0:T(8,128)(2,1)}, bf16[1024,128]{1,0:T(8,128)(2,1)}) custom-call(s32[3]{0:T(128)} %pad_add_fusion.picks, bf16[1024,128]{1,0:T(8,128)(2,1)} %shard_map.28.refs_0_.mine, bf16[1024,128]{1,0:T(8,128)(2,1)} %copy-done.16, bf16[1024,128]{1,0:T(8,128)(2,1)} %copy-done.17), custom_call_target="tpu_custom_call" | custom-call | tf_op jit(solution)/shard_map/pallas_call | solution.py:176
  23.4 2.1 %collective-permute-done.7.behind = bf16[1024,128]{1,0:T(8,128)(2,1)S(1)} collective-permute-done((bf16[1024,128]{1,0:T(8,128)(2,1)}, bf16[1024,128]{1,0:T(8,128)(2,1)S(1)}, u32[]{:S(2)}, u32[]{:S(2)}) %collective-permute-start.7) | collective-permute-done | bytes 262176 | tf_op jit(solution)/shard_map/ppermute | solution.py:21
  25.5 1.8 %collective-permute-start.14 = (bf16[1024,128]{1,0:T(8,128)(2,1)}, bf16[1024,128]{1,0:T(8,128)(2,1)S(1)}, u32[]{:S(2)}, u32[]{:S(2)}) collective-permute-start(bf16[1024,128]{1,0:T(8,128)(2,1)} %get-tuple-element.49), channel_id=1, source_target_pairs={{0,2},{2,0},{4,6},{6,4},{8,10},{10,8},{12,14},{14,12},{1,3},{3,1},... | collective-permute-start | bytes 786440 | tf_op jit(solution)/shard_map/ppermute | solution.py:26
  27.3 2.4 %collective-permute-done.8.ahead = bf16[1024,128]{1,0:T(8,128)(2,1)S(1)} collective-permute-done((bf16[1024,128]{1,0:T(8,128)(2,1)}, bf16[1024,128]{1,0:T(8,128)(2,1)S(1)}, u32[]{:S(2)}, u32[]{:S(2)}) %collective-permute-start.8) | collective-permute-done | bytes 262176 | tf_op jit(solution)/shard_map/ppermute | solution.py:21
  29.6 0.7 copy-done.18
  30.3 2.1 %shard_map.31 = (bf16[1024,128]{1,0:T(8,128)(2,1)}, bf16[1024,128]{1,0:T(8,128)(2,1)}) custom-call(s32[3]{0:T(128)} %pad_add_fusion.picks, bf16[1024,128]{1,0:T(8,128)(2,1)} %get-tuple-element.32.refs_1_.mine, bf16[1024,128]{1,0:T(8,128)(2,1)} %copy-done.15, bf16[1024,128]{1,0:T(8,128)(2,1)} %copy-done.18), custom_call_target="tpu_custom_call" | custom-call | tf_op jit(solution)/shard_map/pallas_call | solution.py:176
  32.4 1.1 %collective-permute-start.20 = (bf16[1024,128]{1,0:T(8,128)(2,1)}, bf16[1024,128]{1,0:T(8,128)(2,1)S(1)}, u32[]{:S(2)}, u32[]{:S(2)}) collective-permute-start(bf16[1024,128]{1,0:T(8,128)(2,1)} %get-tuple-element.33.refs_2_.mine), channel_id=1, source_target_pairs={{0,4},{2,6},{4,8},{6,10},{8,12},{10,14},{12,0},{14,2},{1,5},{3,7},... | collective-permute-start | bytes 786440 | tf_op jit(solution)/shard_map/ppermute | solution.py:21
  33.6 1.5 %collective-permute-start.9 = (bf16[1024,128]{1,0:T(8,128)(2,1)}, bf16[1024,128]{1,0:T(8,128)(2,1)S(1)}, u32[]{:S(2)}, u32[]{:S(2)}) collective-permute-start(bf16[1024,128]{1,0:T(8,128)(2,1)} %get-tuple-element.43), channel_id=1, source_target_pairs={{0,2},{2,0},{4,6},{6,4},{8,10},{10,8},{12,14},{14,12},{1,3},{3,1},... | collective-permute-start | bytes 786440 | tf_op jit(solution)/shard_map/ppermute | solution.py:26
  35.1 0.6 fusion.4
  35.8 0.5 collective-permute-start.15
  36.3 2.8 %collective-permute-start.21 = (bf16[1024,128]{1,0:T(8,128)(2,1)}, bf16[1024,128]{1,0:T(8,128)(2,1)S(1)}, u32[]{:S(2)}, u32[]{:S(2)}) collective-permute-start(bf16[1024,128]{1,0:T(8,128)(2,1)} %get-tuple-element.33.refs_2_.mine), channel_id=1, source_target_pairs={{0,12},{2,14},{4,0},{6,2},{8,4},{10,6},{12,8},{14,10},{1,13},{3,15... | collective-permute-start | bytes 786440 | tf_op jit(solution)/shard_map/ppermute | solution.py:21
  39.1 4.6 %collective-permute-done.20.behind = bf16[1024,128]{1,0:T(8,128)(2,1)S(1)} collective-permute-done((bf16[1024,128]{1,0:T(8,128)(2,1)}, bf16[1024,128]{1,0:T(8,128)(2,1)S(1)}, u32[]{:S(2)}, u32[]{:S(2)}) %collective-permute-start.20) | collective-permute-done | bytes 262176 | tf_op jit(solution)/shard_map/ppermute | solution.py:21
  43.7 0.5 collective-permute-start.10
  44.2 0.7 copy.14.table
  44.9 0.7 copy.13.table
  45.5 5.1 %shard_map.30 = (f32[128,1024]{1,0:T(8,128)}, f32[128,1024]{1,0:T(8,128)}, f32[128,1024]{1,0:T(8,128)}, f32[128,1024]{1,0:T(8,128)}, f32[128,1024]{1,0:T(8,128)}...) custom-call(bf16[1024,128]{1,0:T(8,128)(2,1)} %shard_map.28.refs_0_., ...), custom_call_target="tpu_custom_call" | custom-call | tf_op jit(solution)/shard_map/pallas_call | solution.py:159
  50.8 6.6 %collective-permute-start.6 = (bf16[1024,128]{1,0:T(8,128)(2,1)S(1)}, bf16[1024,128]{1,0:T(8,128)(2,1)S(1)}, u32[]{:S(2)}, u32[]{:S(2)}) collective-permute-start(bf16[1024,128]{1,0:T(8,128)(2,1)S(1)} %copy-done), channel_id=1, source_target_pairs={{0,12},{2,14},{4,0},{6,2},{8,4},{10,6},{12,8},{14,10},{1,13},{3,15... | collective-permute-start | bytes 786440 | tf_op jit(solution)/shard_map/ppermute | solution.py:21
  57.4 7.3 %shard_map.33.rest_0_ = f32[2,32,128,128]{3,2,1,0:T(8,128)} custom-call(bf16[32,128]{1,0:T(8,128)(2,1)} %copy.14.table, f32[128,1024]{1,0:T(8,128)} %get-tuple-element.45.re_own, f32[128,1024]{1,0:T(8,128)} %get-tuple-element.46.re_other, f32[128,1024]{1,0:T(8,128)} %get-tuple-element.47.im_own, f32[128,1024]{1,0:T(8,128)} %get-tuple-element.48.im_other, ...), custom_call_target="tpu_custom_call" | custom-call | flops 2147483648 | bytes 8388608 | tf_op jit(solution)/shard_map/pallas_call | solution.py:105
  64.7 0.7 copy-done.5
  65.4 2.1 %shard_map.36 = (bf16[1024,128]{1,0:T(8,128)(2,1)}, bf16[1024,128]{1,0:T(8,128)(2,1)}) custom-call(s32[3]{0:T(128)} %pad_add_fusion.picks, bf16[1024,128]{1,0:T(8,128)(2,1)} %get-tuple-element.33.refs_2_.mine, bf16[1024,128]{1,0:T(8,128)(2,1)} %copy-done.2, bf16[1024,128]{1,0:T(8,128)(2,1)} %copy-done.5, f32[2,32,128,128]{3,2,1,0:T(8,128)} %shard_map.33.rest_0_), custom_call_target="tpu_custom_call" | custom-call | tf_op jit(solution)/shard_map/pallas_call | solution.py:176
  67.5 0.7 copy-done.3
  68.2 0.1 copy-done.6
  68.3 8.0 %shard_map.34.rest_0_ = f32[2,32,128,128]{3,2,1,0:T(8,128)} custom-call(bf16[32,128]{1,0:T(8,128)(2,1)} %copy.13.table, f32[128,1024]{1,0:T(8,128)} %get-tuple-element.39.re_own, f32[128,1024]{1,0:T(8,128)} %get-tuple-element.40.re_other, f32[128,1024]{1,0:T(8,128)} %get-tuple-element.41.im_own, ...), custom_call_target="tpu_custom_call", output_to_operand_aliasing={{}: (9, {})} | custom-call | flops 2147483648 | bytes 8388608 | tf_op jit(solution)/shard_map/pallas_call | solution.py:105
  76.3 0.7 copy-done.9
  77.0 0.7 copy-done.10
  77.7 2.1 %shard_map.35 = (bf16[1024,128]{1,0:T(8,128)(2,1)}, bf16[1024,128]{1,0:T(8,128)(2,1)}) custom-call(s32[3]{0:T(128)} %pad_add_fusion.picks, bf16[1024,128]{1,0:T(8,128)(2,1)} %get-tuple-element.34.refs_3_.mine, bf16[1024,128]{1,0:T(8,128)(2,1)} %copy-done.9, bf16[1024,128]{1,0:T(8,128)(2,1)} %copy-done.10, f32[2,32,128,128]{3,2,1,0:T(8,128)} %shard_map.34.rest_0_), custom_call_target="tpu_custom_call" | custom-call | tf_op jit(solution)/shard_map/pallas_call | solution.py:176
  79.8 2.0 %collective-permute-start.17 = (bf16[1024,128]{1,0:T(8,128)(2,1)}, bf16[1024,128]{1,0:T(8,128)(2,1)S(1)}, u32[]{:S(2)}, u32[]{:S(2)}) collective-permute-start(bf16[1024,128]{1,0:T(8,128)(2,1)} %get-tuple-element.51), channel_id=1, source_target_pairs={{0,2},{2,0},{4,6},{6,4},{8,10},{10,8},{12,14},{14,12},{1,3},{3,1},... | collective-permute-start | bytes 786440 | tf_op jit(solution)/shard_map/ppermute | solution.py:26
  81.8 0.5 collective-permute-start.23
  82.4 5.6 %collective-permute-done.17.p0_own = bf16[1024,128]{1,0:T(8,128)(2,1)S(1)} collective-permute-done((bf16[1024,128]{1,0:T(8,128)(2,1)}, bf16[1024,128]{1,0:T(8,128)(2,1)S(1)}, u32[]{:S(2)}, u32[]{:S(2)}) %collective-permute-start.17) | collective-permute-done | bytes 262176 | tf_op jit(solution)/shard_map/ppermute | solution.py:26
  88.0 0.7 copy.15.table
  88.7 0.7 copy.12.table
  89.4 0.7 copy-done.12
  90.1 0.1 copy-done.14
  90.2 8.0 %shard_map.37.rest_0_ = f32[2,32,128,128]{3,2,1,0:T(8,128)} custom-call(bf16[32,128]{1,0:T(8,128)(2,1)} %copy.15.table, f32[128,1024]{1,0:T(8,128)} %get-tuple-element.53.re_own, f32[128,1024]{1,0:T(8,128)} %get-tuple-element.54.re_other, f32[128,1024]{1,0:T(8,128)} %get-tuple-element.55.im_own, ...), custom_call_target="tpu_custom_call", output_to_operand_aliasing={{}: (9, {})} | custom-call | flops 2147483648 | bytes 8388608 | tf_op jit(solution)/shard_map/pallas_call | solution.py:105
  98.2 0.7 copy-done.11
  98.9 0.1 copy-done.13
  99.0 8.0 %shard_map.38 = f32[2,32,128,128]{3,2,1,0:T(8,128)} custom-call(bf16[32,128]{1,0:T(8,128)(2,1)} %copy.12.table, f32[128,1024]{1,0:T(8,128)} %get-tuple-element.35.re_own, f32[128,1024]{1,0:T(8,128)} %get-tuple-element.36.re_other, f32[128,1024]{1,0:T(8,128)} %get-tuple-element.37.im_own, ...), custom_call_target="tpu_custom_call", output_to_operand_aliasing={{}: (9, {})} | custom-call | flops 2147483648 | bytes 8388608 | tf_op jit(solution)/shard_map/pallas_call | solution.py:105
  (76 shorter events, 0.4 us)
Async XLA Ops:
  1.8 16.2 %collective-permute-start.12 = (bf16[1024,128]{1,0:T(8,128)(2,1)}, bf16[1024,128]{1,0:T(8,128)(2,1)S(1)}, u32[]{:S(2)}, u32[]{:S(2)}) collective-permute-start(bf16[1024,128]{1,0:T(8,128)(2,1)} %shard_map.28.refs_0_.mine), channel_id=1, source_target_pairs={{0,4},{2,6},{4,8},{6,10},{8,12},{10,14},{12,0},{14,2},{1,5},{3,7},... | collective-permute-start | bytes 786440 | tf_op jit(solution)/shard_map/ppermute | solution.py:21
  4.8 15.8 %collective-permute-start.13 = (bf16[1024,128]{1,0:T(8,128)(2,1)}, bf16[1024,128]{1,0:T(8,128)(2,1)S(1)}, u32[]{:S(2)}, u32[]{:S(2)}) collective-permute-start(bf16[1024,128]{1,0:T(8,128)(2,1)} %shard_map.28.refs_0_.mine), channel_id=1, source_target_pairs={{0,12},{2,14},{4,0},{6,2},{8,4},{10,6},{12,8},{14,10},{1,13},{3,15... | collective-permute-start | bytes 786440 | tf_op jit(solution)/shard_map/ppermute | solution.py:21
  9.1 41.6 %copy-start = (bf16[1024,128]{1,0:T(8,128)(2,1)S(1)}, bf16[1024,128]{1,0:T(8,128)(2,1)}, u32[]{:S(2)}) copy-start(bf16[1024,128]{1,0:T(8,128)(2,1)} %get-tuple-element.34.refs_3_.mine) | copy-start | bytes 786436
  9.1 23.3 %collective-permute-start.1 = (bf16[1024,128]{1,0:T(8,128)(2,1)}, bf16[1024,128]{1,0:T(8,128)(2,1)S(1)}, u32[]{:S(2)}, u32[]{:S(2)}) collective-permute-start(bf16[1024,128]{1,0:T(8,128)(2,1)} %get-tuple-element.32.refs_1_.mine), channel_id=1, source_target_pairs={{0,1},{1,0},{2,3},{3,2},{4,5},{5,4},{6,7},{7,6},{8,9},{9,8},{10,11... | collective-permute-start | bytes 786440 | tf_op jit(solution)/shard_map/ppermute | solution.py:21
  9.1 16.4 %collective-permute-start.7 = (bf16[1024,128]{1,0:T(8,128)(2,1)}, bf16[1024,128]{1,0:T(8,128)(2,1)S(1)}, u32[]{:S(2)}, u32[]{:S(2)}) collective-permute-start(bf16[1024,128]{1,0:T(8,128)(2,1)} %get-tuple-element.32.refs_1_.mine), channel_id=1, source_target_pairs={{0,4},{2,6},{4,8},{6,10},{8,12},{10,14},{12,0},{14,2},{1,5},{3,7},... | collective-permute-start | bytes 786440 | tf_op jit(solution)/shard_map/ppermute | solution.py:21
  10.4 3.7 %collective-permute-start.4 = (s32[1]{0:T(128)}, s32[1]{0:T(128)}, u32[]{:S(2)}, u32[]{:S(2)}) collective-permute-start(s32[1]{0:T(128)} %bitcast.3), channel_id=1, source_target_pairs={{0,2},{2,0},{4,6},{6,4},{8,10},{10,8},{12,14},{14,12},{1,3},{3,1},... | collective-permute-start | bytes 20 | tf_op jit(solution)/shard_map/ppermute | solution.py:26
  14.1 15.5 %collective-permute-start.8 = (bf16[1024,128]{1,0:T(8,128)(2,1)}, bf16[1024,128]{1,0:T(8,128)(2,1)S(1)}, u32[]{:S(2)}, u32[]{:S(2)}) collective-permute-start(bf16[1024,128]{1,0:T(8,128)(2,1)} %get-tuple-element.32.refs_1_.mine), channel_id=1, source_target_pairs={{0,12},{2,14},{4,0},{6,2},{8,4},{10,6},{12,8},{14,10},{1,13},{3,15... | collective-permute-start | bytes 786440 | tf_op jit(solution)/shard_map/ppermute | solution.py:21
  17.9 3.1 %copy-start.16 = (bf16[1024,128]{1,0:T(8,128)(2,1)}, bf16[1024,128]{1,0:T(8,128)(2,1)S(1)}, u32[]{:S(2)}) copy-start(bf16[1024,128]{1,0:T(8,128)(2,1)S(1)} %collective-permute-done.12.behind) | copy-start | bytes 786436
  17.9 15.6 %collective-permute-start.2 = (bf16[1024,128]{1,0:T(8,128)(2,1)}, bf16[1024,128]{1,0:T(8,128)(2,1)S(1)}, u32[]{:S(2)}, u32[]{:S(2)}) collective-permute-start(bf16[1024,128]{1,0:T(8,128)(2,1)} %get-tuple-element.33.refs_2_.mine), channel_id=1, source_target_pairs={{0,1},{1,0},{2,3},{3,2},{4,5},{5,4},{6,7},{7,6},{8,9},{9,8},{10,11... | collective-permute-start | bytes 786440 | tf_op jit(solution)/shard_map/ppermute | solution.py:21
  20.6 15.1 %collective-permute-start.3 = (bf16[1024,128]{1,0:T(8,128)(2,1)}, bf16[1024,128]{1,0:T(8,128)(2,1)S(1)}, u32[]{:S(2)}, u32[]{:S(2)}) collective-permute-start(bf16[1024,128]{1,0:T(8,128)(2,1)} %get-tuple-element.34.refs_3_.mine), channel_id=1, source_target_pairs={{0,1},{1,0},{2,3},{3,2},{4,5},{5,4},{6,7},{7,6},{8,9},{9,8},{10,11... | collective-permute-start | bytes 786440 | tf_op jit(solution)/shard_map/ppermute | solution.py:21
  25.5 4.1 %copy-start.15 = (bf16[1024,128]{1,0:T(8,128)(2,1)}, bf16[1024,128]{1,0:T(8,128)(2,1)S(1)}, u32[]{:S(2)}) copy-start(bf16[1024,128]{1,0:T(8,128)(2,1)S(1)} %collective-permute-done.7.behind) | copy-start | bytes 786436
  25.5 10.3 %collective-permute-start.14 = (bf16[1024,128]{1,0:T(8,128)(2,1)}, bf16[1024,128]{1,0:T(8,128)(2,1)S(1)}, u32[]{:S(2)}, u32[]{:S(2)}) collective-permute-start(bf16[1024,128]{1,0:T(8,128)(2,1)} %get-tuple-element.49), channel_id=1, source_target_pairs={{0,2},{2,0},{4,6},{6,4},{8,10},{10,8},{12,14},{14,12},{1,3},{3,1},... | collective-permute-start | bytes 786440 | tf_op jit(solution)/shard_map/ppermute | solution.py:26
  29.6 6.7 %collective-permute-start = (bf16[1024,128]{1,0:T(8,128)(2,1)}, bf16[1024,128]{1,0:T(8,128)(2,1)S(1)}, u32[]{:S(2)}, u32[]{:S(2)}) collective-permute-start(bf16[1024,128]{1,0:T(8,128)(2,1)} %shard_map.28.refs_0_.mine), channel_id=1, source_target_pairs={{0,1},{1,0},{2,3},{3,2},{4,5},{5,4},{6,7},{7,6},{8,9},{9,8},{10,11... | collective-permute-start | bytes 786440 | tf_op jit(solution)/shard_map/ppermute | solution.py:21
  32.4 13.1 %copy-start.19 = (bf16[1024,128]{1,0:T(8,128)(2,1)}, bf16[1024,128]{1,0:T(8,128)(2,1)S(1)}, u32[]{:S(2)}) copy-start(bf16[1024,128]{1,0:T(8,128)(2,1)S(1)} %collective-permute-done.1.refs_5_) | copy-start | bytes 786436
  32.4 11.2 %collective-permute-start.20 = (bf16[1024,128]{1,0:T(8,128)(2,1)}, bf16[1024,128]{1,0:T(8,128)(2,1)S(1)}, u32[]{:S(2)}, u32[]{:S(2)}) collective-permute-start(bf16[1024,128]{1,0:T(8,128)(2,1)} %get-tuple-element.33.refs_2_.mine), channel_id=1, source_target_pairs={{0,4},{2,6},{4,8},{6,10},{8,12},{10,14},{12,0},{14,2},{1,5},{3,7},... | collective-permute-start | bytes 786440 | tf_op jit(solution)/shard_map/ppermute | solution.py:21
  33.6 12.0 %copy-start.20 = (bf16[1024,128]{1,0:T(8,128)(2,1)}, bf16[1024,128]{1,0:T(8,128)(2,1)S(1)}, u32[]{:S(2)}) copy-start(bf16[1024,128]{1,0:T(8,128)(2,1)S(1)} %collective-permute-done.2.refs_6_) | copy-start | bytes 786436
  33.6 10.1 %collective-permute-start.9 = (bf16[1024,128]{1,0:T(8,128)(2,1)}, bf16[1024,128]{1,0:T(8,128)(2,1)S(1)}, u32[]{:S(2)}, u32[]{:S(2)}) collective-permute-start(bf16[1024,128]{1,0:T(8,128)(2,1)} %get-tuple-element.43), channel_id=1, source_target_pairs={{0,2},{2,0},{4,6},{6,4},{8,10},{10,8},{12,14},{14,12},{1,3},{3,1},... | collective-permute-start | bytes 786440 | tf_op jit(solution)/shard_map/ppermute | solution.py:26
  35.7 9.9 %copy-start.21 = (bf16[1024,128]{1,0:T(8,128)(2,1)}, bf16[1024,128]{1,0:T(8,128)(2,1)S(1)}, u32[]{:S(2)}) copy-start(bf16[1024,128]{1,0:T(8,128)(2,1)S(1)} %collective-permute-done.3.refs_7_) | copy-start | bytes 786436
  35.7 15.0 %collective-permute-start.16 = (bf16[1024,128]{1,0:T(8,128)(2,1)}, bf16[1024,128]{1,0:T(8,128)(2,1)S(1)}, u32[]{:S(2)}, u32[]{:S(2)}) collective-permute-start(bf16[1024,128]{1,0:T(8,128)(2,1)} %get-tuple-element.50.p1_own), channel_id=1, source_target_pairs={{0,1},{1,0},{2,3},{3,2},{4,5},{5,4},{6,7},{7,6},{8,9},{9,8},{10,11... | collective-permute-start | bytes 786440 | tf_op jit(solution)/shard_map/ppermute | solution.py:21
  35.8 21.6 %copy-start.23 = (bf16[1024,128]{1,0:T(8,128)(2,1)}, bf16[1024,128]{1,0:T(8,128)(2,1)S(1)}, u32[]{:S(2)}) copy-start(bf16[1024,128]{1,0:T(8,128)(2,1)S(1)} %collective-permute-done.14.p0_own) | copy-start | bytes 786436
  35.8 15.0 %collective-permute-start.15 = (bf16[1024,128]{1,0:T(8,128)(2,1)S(1)}, bf16[1024,128]{1,0:T(8,128)(2,1)S(1)}, u32[]{:S(2)}, u32[]{:S(2)}) collective-permute-start(bf16[1024,128]{1,0:T(8,128)(2,1)S(1)} %collective-permute-done.14.p0_own), channel_id=1, source_target_pairs={{0,1},{1,0},{2,3},{3,2},{4,5},{5,4},{6,7},{7,6},{8,9},{9,8},{10,11... | collective-permute-start | bytes 786440 | tf_op jit(solution)/shard_map/ppermute | solution.py:21
  36.3 9.2 %copy-start.22 = (bf16[1024,128]{1,0:T(8,128)(2,1)}, bf16[1024,128]{1,0:T(8,128)(2,1)S(1)}, u32[]{:S(2)}) copy-start(bf16[1024,128]{1,0:T(8,128)(2,1)S(1)} %collective-permute-done.refs_4_) | copy-start | bytes 786436
  36.3 28.3 %collective-permute-start.21 = (bf16[1024,128]{1,0:T(8,128)(2,1)}, bf16[1024,128]{1,0:T(8,128)(2,1)S(1)}, u32[]{:S(2)}, u32[]{:S(2)}) collective-permute-start(bf16[1024,128]{1,0:T(8,128)(2,1)} %get-tuple-element.33.refs_2_.mine), channel_id=1, source_target_pairs={{0,12},{2,14},{4,0},{6,2},{8,4},{10,6},{12,8},{14,10},{1,13},{3,15... | collective-permute-start | bytes 786440 | tf_op jit(solution)/shard_map/ppermute | solution.py:21
  43.6 21.0 %copy-start.2 = (bf16[1024,128]{1,0:T(8,128)(2,1)}, bf16[1024,128]{1,0:T(8,128)(2,1)S(1)}, u32[]{:S(2)}) copy-start(bf16[1024,128]{1,0:T(8,128)(2,1)S(1)} %collective-permute-done.20.behind) | copy-start | bytes 786436
  43.6 23.8 %collective-permute-start.11 = (bf16[1024,128]{1,0:T(8,128)(2,1)}, bf16[1024,128]{1,0:T(8,128)(2,1)S(1)}, u32[]{:S(2)}, u32[]{:S(2)}) collective-permute-start(bf16[1024,128]{1,0:T(8,128)(2,1)} %get-tuple-element.44.p1_own), channel_id=1, source_target_pairs={{0,1},{1,0},{2,3},{3,2},{4,5},{5,4},{6,7},{7,6},{8,9},{9,8},{10,11... | collective-permute-start | bytes 786440 | tf_op jit(solution)/shard_map/ppermute | solution.py:21
  43.7 21.0 %copy-start.1 = (bf16[1024,128]{1,0:T(8,128)(2,1)}, bf16[1024,128]{1,0:T(8,128)(2,1)S(1)}, u32[]{:S(2)}) copy-start(bf16[1024,128]{1,0:T(8,128)(2,1)S(1)} %collective-permute-done.9.p0_own) | copy-start | bytes 786436
  43.7 23.8 %collective-permute-start.10 = (bf16[1024,128]{1,0:T(8,128)(2,1)S(1)}, bf16[1024,128]{1,0:T(8,128)(2,1)S(1)}, u32[]{:S(2)}, u32[]{:S(2)}) collective-permute-start(bf16[1024,128]{1,0:T(8,128)(2,1)S(1)} %collective-permute-done.9.p0_own), channel_id=1, source_target_pairs={{0,1},{1,0},{2,3},{3,2},{4,5},{5,4},{6,7},{7,6},{8,9},{9,8},{10,11... | collective-permute-start | bytes 786440 | tf_op jit(solution)/shard_map/ppermute | solution.py:21
  50.7 6.7 %copy-start.24 = (bf16[1024,128]{1,0:T(8,128)(2,1)}, bf16[1024,128]{1,0:T(8,128)(2,1)S(1)}, u32[]{:S(2)}) copy-start(bf16[1024,128]{1,0:T(8,128)(2,1)S(1)} %collective-permute-done.16.p1_other) | copy-start | bytes 786436
  50.7 25.6 %collective-permute-start.5 = (bf16[1024,128]{1,0:T(8,128)(2,1)S(1)}, bf16[1024,128]{1,0:T(8,128)(2,1)S(1)}, u32[]{:S(2)}, u32[]{:S(2)}) collective-permute-start(bf16[1024,128]{1,0:T(8,128)(2,1)S(1)} %copy-done), channel_id=1, source_target_pairs={{0,4},{2,6},{4,8},{6,10},{8,12},{10,14},{12,0},{14,2},{1,5},{3,7},... | collective-permute-start | bytes 786440 | tf_op jit(solution)/shard_map/ppermute | solution.py:21
  50.8 6.6 %copy-start.25 = (bf16[1024,128]{1,0:T(8,128)(2,1)}, bf16[1024,128]{1,0:T(8,128)(2,1)S(1)}, u32[]{:S(2)}) copy-start(bf16[1024,128]{1,0:T(8,128)(2,1)S(1)} %collective-permute-done.15.p0_other) | copy-start | bytes 786436
  50.8 25.5 %collective-permute-start.6 = (bf16[1024,128]{1,0:T(8,128)(2,1)S(1)}, bf16[1024,128]{1,0:T(8,128)(2,1)S(1)}, u32[]{:S(2)}, u32[]{:S(2)}) collective-permute-start(bf16[1024,128]{1,0:T(8,128)(2,1)S(1)} %copy-done), channel_id=1, source_target_pairs={{0,12},{2,14},{4,0},{6,2},{8,4},{10,6},{12,8},{14,10},{1,13},{3,15... | collective-permute-start | bytes 786440 | tf_op jit(solution)/shard_map/ppermute | solution.py:21
  64.7 0.7 copy-start.5
  67.5 14.3 %collective-permute-start.22 = (bf16[1024,128]{1,0:T(8,128)(2,1)}, bf16[1024,128]{1,0:T(8,128)(2,1)S(1)}, u32[]{:S(2)}, u32[]{:S(2)}) collective-permute-start(bf16[1024,128]{1,0:T(8,128)(2,1)} %get-tuple-element.57), channel_id=1, source_target_pairs={{0,2},{2,0},{4,6},{6,4},{8,10},{10,8},{12,14},{14,12},{1,3},{3,1},... | collective-permute-start | bytes 786440 | tf_op jit(solution)/shard_map/ppermute | solution.py:26
  67.5 0.7 copy-start.3
  67.5 0.8 copy-start.6
  76.3 5.5 %copy-start.4 = (bf16[1024,128]{1,0:T(8,128)(2,1)S(1)}, bf16[1024,128]{1,0:T(8,128)(2,1)}, u32[]{:S(2)}) copy-start(bf16[1024,128]{1,0:T(8,128)(2,1)} %get-tuple-element.58.p1_own) | copy-start | bytes 786436
  76.3 0.7 copy-start.9
  79.8 8.2 %collective-permute-start.17 = (bf16[1024,128]{1,0:T(8,128)(2,1)}, bf16[1024,128]{1,0:T(8,128)(2,1)S(1)}, u32[]{:S(2)}, u32[]{:S(2)}) collective-permute-start(bf16[1024,128]{1,0:T(8,128)(2,1)} %get-tuple-element.51), channel_id=1, source_target_pairs={{0,2},{2,0},{4,6},{6,4},{8,10},{10,8},{12,14},{14,12},{1,3},{3,1},... | collective-permute-start | bytes 786440 | tf_op jit(solution)/shard_map/ppermute | solution.py:26
  81.8 7.6 %collective-permute-start.24 = (bf16[1024,128]{1,0:T(8,128)(2,1)S(1)}, bf16[1024,128]{1,0:T(8,128)(2,1)S(1)}, u32[]{:S(2)}, u32[]{:S(2)}) collective-permute-start(bf16[1024,128]{1,0:T(8,128)(2,1)S(1)} %copy-done.4), channel_id=1, source_target_pairs={{0,1},{1,0},{2,3},{3,2},{4,5},{5,4},{6,7},{7,6},{8,9},{9,8},{10,11... | collective-permute-start | bytes 786440 | tf_op jit(solution)/shard_map/ppermute | solution.py:21
  81.8 7.6 %copy-start.7 = (bf16[1024,128]{1,0:T(8,128)(2,1)}, bf16[1024,128]{1,0:T(8,128)(2,1)S(1)}, u32[]{:S(2)}) copy-start(bf16[1024,128]{1,0:T(8,128)(2,1)S(1)} %collective-permute-done.22.p0_own) | copy-start | bytes 786436
  81.8 7.5 %collective-permute-start.23 = (bf16[1024,128]{1,0:T(8,128)(2,1)S(1)}, bf16[1024,128]{1,0:T(8,128)(2,1)S(1)}, u32[]{:S(2)}, u32[]{:S(2)}) collective-permute-start(bf16[1024,128]{1,0:T(8,128)(2,1)S(1)} %collective-permute-done.22.p0_own), channel_id=1, source_target_pairs={{0,1},{1,0},{2,3},{3,2},{4,5},{5,4},{6,7},{7,6},{8,9},{9,8},{10,11... | collective-permute-start | bytes 786440 | tf_op jit(solution)/shard_map/ppermute | solution.py:21
  82.3 15.9 %collective-permute-start.19 = (bf16[1024,128]{1,0:T(8,128)(2,1)}, bf16[1024,128]{1,0:T(8,128)(2,1)S(1)}, u32[]{:S(2)}, u32[]{:S(2)}) collective-permute-start(bf16[1024,128]{1,0:T(8,128)(2,1)} %get-tuple-element.52.p1_own), channel_id=1, source_target_pairs={{0,1},{1,0},{2,3},{3,2},{4,5},{5,4},{6,7},{7,6},{8,9},{9,8},{10,11... | collective-permute-start | bytes 786440 | tf_op jit(solution)/shard_map/ppermute | solution.py:21
  88.0 10.2 %copy-start.8 = (bf16[1024,128]{1,0:T(8,128)(2,1)}, bf16[1024,128]{1,0:T(8,128)(2,1)S(1)}, u32[]{:S(2)}) copy-start(bf16[1024,128]{1,0:T(8,128)(2,1)S(1)} %collective-permute-done.17.p0_own) | copy-start | bytes 786436
  88.0 10.2 %collective-permute-start.18 = (bf16[1024,128]{1,0:T(8,128)(2,1)S(1)}, bf16[1024,128]{1,0:T(8,128)(2,1)S(1)}, u32[]{:S(2)}, u32[]{:S(2)}) collective-permute-start(bf16[1024,128]{1,0:T(8,128)(2,1)S(1)} %collective-permute-done.17.p0_own), channel_id=1, source_target_pairs={{0,1},{1,0},{2,3},{3,2},{4,5},{5,4},{6,7},{7,6},{8,9},{9,8},{10,11... | collective-permute-start | bytes 786440 | tf_op jit(solution)/shard_map/ppermute | solution.py:21
  89.4 0.7 copy-start.12
  89.4 0.8 copy-start.14
  98.2 0.7 copy-start.11
  98.2 0.8 copy-start.13
  (3 other events, 2.1 us)

commit v2 on v0

v2 whole, which is shorter than its diff:
```python
import functools
import math

import jax
import jax.numpy as jnp
from jax import lax
from jax.experimental import pallas as pl
from jax.experimental.pallas import tpu as pltpu
from jax.sharding import PartitionSpec as P

LAGS = 64
ROUNDS = 2
GROUP = 8
CHANNEL_BLOCK = 32
CHUNKS = (64, 64, 64, 64)
VMEM = 32 * 2**20
AFTER = {2: 0, 3: 1}
GATE = {}
COST = pl.CostEstimate(flops=0, bytes_accessed=0, transcendentals=0)


def ring_shift(x, axis, by):
    size = lax.axis_size(axis)
    return lax.ppermute(x, axis, [(i, (i + by) % size) for i in range(size)])


def pair_swap(x, axis):
    size = lax.axis_size(axis)
    return lax.ppermute(x, axis, [(i, i ^ 1) for i in range(size)])


def make_table(bin_count, windows, lag_count):
    lags = jnp.arange(lag_count, dtype=jnp.int32) - lag_count // 2
    bins = jnp.arange(bin_count, dtype=jnp.int32)
    period = 2 * bin_count
    phase = bins[None, :] * ((lags[:, None] + period) % period) % period
    angle = phase.astype(jnp.float32) * (math.pi / bin_count)
    weight = (bin_count * windows) ** (-0.5)
    both = jnp.stack([jnp.cos(angle), -jnp.sin(angle)], axis=1) * weight
    both = both.astype(jnp.bfloat16).reshape(lag_count, 2, bin_count // GROUP, GROUP)
    return both.transpose(0, 2, 1, 3).reshape(lag_count, 2 * bin_count)


def lag_kernel(*refs, first, has_total, last):
    table, re_own, re_other, im_own, im_other, p0_own, p0_other, p1_own, p1_other = refs[:9]
    total = refs[9] if has_total else None
    out, cross = refs[9 + has_total : 11 + has_total]
    rows = CHANNEL_BLOCK
    channels, depth = re_own.shape
    width = p0_own.shape[1]
    tile = GROUP * 16
    lag_count = out.shape[1]
    mine = pl.ds(pl.multiple_of(lax.axis_index("sub") * lag_count, lag_count), lag_count)
    weights = table[mine, 2 * first : 2 * (first + depth // 16)]
    bin_of_row = lax.broadcasted_iota(jnp.int32, (GROUP, tile), 0)
    bin_of_lane = lax.broadcasted_iota(jnp.int32, (GROUP, tile), 1) // (tile // GROUP)
    same_bin = bin_of_row == bin_of_lane

    def spread(ref, i, lanes):
        return jnp.where(same_bin, jnp.broadcast_to(ref[i : i + 1, lanes], (GROUP, tile)), 0.0)

    def block(b):
        start = pl.multiple_of(b * rows, rows)
        here = [ref.at[pl.ds(start, rows), :] for ref in (re_own, im_own, re_other, im_other)]
        for g in range(depth // tile):
            lanes = slice(g * tile, (g + 1) * tile)
            pieces = []
            for i in range(rows):
                own = jnp.concatenate([spread(here[0], i, lanes), spread(here[1], i, lanes)], axis=0)
                other = jnp.concatenate([spread(here[2], i, lanes), spread(here[3], i, lanes)], axis=0)
                pieces.append(jnp.concatenate([own, other], axis=1).astype(jnp.bfloat16))
            left = jnp.concatenate(pieces, axis=0)
            right = jnp.concatenate(
                [
                    jnp.concatenate([p0_own[lanes, :], p1_own[lanes, :]], axis=1),
                    jnp.concatenate([p0_other[lanes, :], p1_other[lanes, :]], axis=1),
                ],
                axis=0,
            )
            part = jnp.dot(left, right, preferred_element_type=jnp.float32).astype(jnp.bfloat16)
            cross[:, g * 2 * GROUP : (g + 1) * 2 * GROUP, :] = part.reshape(rows, 2 * GROUP, part.shape[-1])

        for low in range(0, rows, 8):
            lagged = [jnp.dot(weights, cross[i], preferred_element_type=jnp.float32) for i in range(low, low + 8)]
            at = pl.ds(pl.multiple_of(start + low, 8), 8)
            for r in range(ROUNDS):
                stacked = jnp.stack([x[:, r * width : (r + 1) * width] for x in lagged], axis=0)
                tile_out = jnp.swapaxes(stacked, 0, 1)
                if has_total:
                    tile_out = tile_out + total[r, :, at, :]
                if last:
                    stage[b, r, :, low : low + 8, :] = tile_out
                else:
                    out[r, :, at, :] = tile_out

    if last:
        stage, sems = refs[11 + has_total :]

        def store(b):
            at = pl.ds(pl.multiple_of(b * rows, rows), rows)
            return pltpu.make_async_copy(stage.at[b], out.at[:, :, at, :], sems.at[b])

        @pl.loop(0, channels // rows)
        def _(b):
            block(b)
            store(b).start()

        for b in range(channels // rows):
            store(b).wait()
    else:

        @pl.loop(0, channels // rows)
        def _(b):
            block(b)


def add_lags(table, first, local, partners, total, last):
    channels, depth = local[0].shape
    lag_count = table.shape[0] // lax.axis_size("sub")
    cross_depth = depth // 8
    width = partners[0].shape[1]
    block = CHANNEL_BLOCK
    vmem = pl.BlockSpec(memory_space=pltpu.VMEM)
    operands = [table, *local, *partners]
    aliases = {}
    if total is not None:
        if not last:
            aliases = {len(operands): 0}
        operands.append(total)
    shape = (ROUNDS, lag_count, channels, width)
    scratch = [pltpu.VMEM((block, cross_depth, ROUNDS * width), jnp.bfloat16)]
    if last:
        blocks = channels // block
        scratch += [pltpu.VMEM((blocks, ROUNDS, lag_count, block, width), jnp.float32), pltpu.SemaphoreType.DMA((blocks,))]
    return pl.pallas_call(
        functools.partial(lag_kernel, first=first, has_total=total is not None, last=last),
        in_specs=[vmem] * len(operands),
        out_specs=pl.BlockSpec(memory_space=pl.ANY) if last else vmem,
        out_shape=jax.ShapeDtypeStruct(shape, jnp.float32) if last else pltpu.VMEM(shape, jnp.float32),
        input_output_aliases=aliases,
        scratch_shapes=scratch,
        compiler_params=pltpu.CompilerParams(vmem_limit_bytes=VMEM),
        cost_estimate=COST,
    )(*operands)


def bins_first_kernel(x, *outs, sizes, first):
    for out, size in zip(outs, sizes):
        if size == x.shape[2] and first:
            first = 0
        for low in range(0, size, 16):
            at = slice(first + low, first + low + 16)
            slabs = [x[s, c, at, :].astype(jnp.float32) for c in range(2) for s in range(x.shape[0])]
            turned = jnp.swapaxes(jnp.stack(slabs, axis=0), 0, 1)
            rows = turned.reshape(16 * len(slabs), x.shape[3]).astype(out.dtype)
            out[low * len(slabs) : (low + 16) * len(slabs), :] = rows
        first += size


def bins_first(x, first, sizes):
    windows, parts, bins, channels = x.shape
    read = bins if first else sum(sizes)
    return pl.pallas_call(
        functools.partial(bins_first_kernel, sizes=sizes, first=first),
        grid=(1,),
        in_specs=[pl.BlockSpec((windows, parts, read, channels), lambda b: (0, 0, 0, 0))],
        out_specs=[pl.BlockSpec((size * parts * windows, channels), lambda b: (0, 0)) for size in sizes],
        out_shape=[jax.ShapeDtypeStruct((size * parts * windows, channels), x.dtype) for size in sizes],
        compiler_params=pltpu.CompilerParams(vmem_limit_bytes=VMEM),
        cost_estimate=COST,
    )(x)


def channels_first_kernel(own, other, *outs):
    quarter = len(outs) // 4
    for k, ref in enumerate((own, other)):
        first = 0
        for n in range(quarter):
            plain, turned = outs[4 * n + k], outs[4 * n + 2 + k]
            depth = plain.shape[1]
            for low in range(0, depth, 128):
                tile = ref[first + low : first + low + 128, :].astype(jnp.float32).T
                real_lane = lax.broadcasted_iota(jnp.int32, tile.shape, 1) % 16 < 8
                plain[:, low : low + 128] = tile
                swapped = jnp.where(real_lane, -pltpu.roll(tile, 128 - 8, 1), pltpu.roll(tile, 8, 1))
                turned[:, low : low + 128] = swapped
            first += depth


def channels_first(own, other, depths):
    outs = pl.pallas_call(
        channels_first_kernel,
        out_shape=[pltpu.VMEM((own.shape[1], depth), jnp.float32) for depth in depths for _ in range(4)],
        in_specs=[pl.BlockSpec(memory_space=pltpu.VMEM)] * 2,
        out_specs=[pl.BlockSpec(memory_space=pltpu.VMEM)] * (4 * len(depths)),
        compiler_params=pltpu.CompilerParams(vmem_limit_bytes=VMEM),
        cost_estimate=COST,
    )(own, other)
    return [outs[4 * n : 4 * n + 4] for n in range(len(depths))]


def choose_kernel(direction, of_pair, mine, behind, ahead, *rest):
    far, near, held, sems = rest[-4:]
    odd = lax.axis_index("blk") % 2

    def fetch(source, n):
        return pltpu.make_async_copy(source, held.at[n], sems.at[n])

    pl.when(direction[1, 0] == 1)(lambda: fetch(ahead, 0).start())
    pl.when(direction[1, 0] != 1)(lambda: fetch(behind, 0).start())
    pl.when(of_pair[0] == odd)(lambda: fetch(mine, 1).start())
    pl.when((of_pair[0] != odd) & (odd == 1))(lambda: fetch(behind, 1).start())
    pl.when((of_pair[0] != odd) & (odd == 0))(lambda: fetch(ahead, 1).start())
    for n, out in enumerate((far, near)):
        fetch(mine, n).wait()
        pltpu.make_async_copy(held.at[n], out, sems.at[n]).start()
    for n, out in enumerate((far, near)):
        pltpu.make_async_copy(held.at[n], out, sems.at[n]).wait()


def choose(direction, of_pair, mine, behind, ahead, after):
    smem = pl.BlockSpec(memory_space=pltpu.SMEM)
    hbm = pl.BlockSpec(memory_space=pl.ANY)
    return pl.pallas_call(
        choose_kernel,
        in_specs=[smem, smem] + [hbm] * (3 + len(after)),
        out_specs=[hbm, hbm],
        out_shape=[jax.ShapeDtypeStruct(mine.shape, mine.dtype)] * 2,
        scratch_shapes=[pltpu.VMEM((2, *mine.shape), mine.dtype), pltpu.SemaphoreType.DMA((2,))],
        compiler_params=pltpu.CompilerParams(vmem_limit_bytes=VMEM),
        cost_estimate=COST,
    )(direction, of_pair, mine, behind, ahead, *after)


def per_device(spectra, direction):
    windows, _, bin_count, channels = spectra.shape
    with jax.named_scope("direction_of_pair"):
        of_pair = pair_swap(direction[0], "blk")
    table = make_table(bin_count, windows * lax.axis_size("sub"), LAGS)

    mine = bins_first(spectra, 0, CHUNKS[:1])
    *later, whole = bins_first(spectra, CHUNKS[0], (*CHUNKS[1:], bin_count))
    mine = [*mine, *later]
    behind, ahead = [], []
    for n, x in enumerate(mine):
        with jax.named_scope(f"two_behind_{n}"):
            behind.append(ring_shift(x, "blk", 2))
        with jax.named_scope(f"two_ahead_{n}"):
            ahead.append(ring_shift(x, "blk", -2))
    with jax.named_scope("my_other_half"):
        other = ring_shift(whole, "sub", 1)
    local = channels_first(whole, other, [size * whole.shape[0] // bin_count for size in CHUNKS])

    totals = [None]
    first = 0
    for n, size in enumerate(CHUNKS):
        after = [totals[AFTER[n] + 1]] if n in AFTER else []
        if n == 0:
            after = [local[0][0], table]
        far_own, passed_on = choose(direction, of_pair, mine[n], behind[n], ahead[n], after)
        with jax.named_scope(f"near_{n}"):
            near_own = pair_swap(passed_on, "blk")
        with jax.named_scope(f"far_other_half_{n}"):
            far_other = ring_shift(far_own, "sub", 1)
        if n in GATE:
            near_own, _ = lax.optimization_barrier((near_own, totals[GATE[n] + 1]))
        with jax.named_scope(f"near_other_half_{n}"):
            near_other = ring_shift(near_own, "sub", 1)
        totals.append(add_lags(table, first, local[n], [near_own, near_other, far_own, far_other], totals[-1], n == len(CHUNKS) - 1))
        first += size
    return totals[-1][:, None]


def solution(mesh):
    return jax.shard_map(
        per_device,
        mesh=mesh,
        in_specs=(P("sub", None, None, ("grp", "blk")), P(None, "blk")),
        out_specs=P(None, ("grp", "blk"), "sub", None, None),
        check_vma=False,
    )
```

time: 182 us -> 76.6 us (0.42)
  local copies, waits for them, and re-layouts: 66.4 us -> 2.96 us
  matrix products: 43.4 us -> 0 us
  Pallas kernels: 0 us -> 28.8 us
  waiting for transfers between devices: 41.5 us -> 16.5 us
  starting transfers between devices: 10.1 us -> 26.1 us
  between operations: 14.8 us -> 0.15 us
  other arithmetic: 4.52 us -> 1.29 us
    reshape x4 -> x1, local copies, waits for them, and re-layouts: 49.5 us -> 0.99 us  [make_table(): return both.transpose(0, 2, 1, 3).reshape(lag_count, 2 * bin_count)]
    dot_general x8 -> x0, matrix products: 43.4 us -> none  [the longest x4 27.4 us: correlate(): jnp.einsum('scfi,scfj->fij', left_part, right_part, preferred_element_typ...]
    pallas_call x0 -> x11, Pallas kernels: none -> 28.8 us  [the longest x4 19.3 us: add_lags(): pl.pallas_call(functools.partial(lag_kernel, first=first, has_total=total...]
    ppermute x4 -> x22, starting transfers between devices: 9.83 us -> 26.1 us  [the longest x17 19.4 us: ring_shift(): return lax.ppermute(x, axis, [(i, (i + by) % size) for i in range(size)])]
    ppermute x4 -> x22, waiting for transfers between devices: 32.1 us -> 16.5 us  [the longest x5 8.82 us: pair_swap(): return lax.ppermute(x, axis, [(i, i ^ 1) for i in range(size)])]
    reduce_scatter x2 -> x0, waiting for transfers between devices: 9.42 us -> none  [per_device(): lax.psum_scatter(partial_lags.astype(jnp.bfloat16), 'sub', scatter_dimens...]
    dot_general x4 -> x0, local copies, waits for them, and re-layouts: 6.73 us -> none  [correlate(): jnp.einsum('scfi,scfj->fij', left_part, right_part, preferred_element_typ...]
    broadcast_in_dim x1 -> x0, local copies, waits for them, and re-layouts: 4.44 us -> none  [per_device(): return reduced[:, None]]
  transfers between devices with their start and end apart: 6 -> 22, of which waited for: 3 -> 7; matrix products, arithmetic and copies ran while one was open for 57% -> 4% of each run, Pallas kernels for 0% -> 30%
where the time goes in v2:
time: 76.6 us; the launch traced here: 75.9 us
  Pallas kernels  28.8 us (38%)
  starting transfers between devices  26.1 us (34%)
  waiting for transfers between devices  16.5 us (22%)
  local copies, waits for them, and re-layouts  2.96 us (4%)
  other arithmetic  1.29 us (2%)
    ppermute x17, starting transfers between devices, ring_shift(): return lax.ppermute(x, axis, [(i, (i + by) % size) for i in range(size)])  19.4 us
    pallas_call x4, Pallas kernels, add_lags(): pl.pallas_call(functools.partial(lag_kernel, first=first, has_total=total...  19.3 us
    ppermute x5, waiting for transfers between devices, pair_swap(): return lax.ppermute(x, axis, [(i, i ^ 1) for i in range(size)])  8.82 us
    ppermute x17, waiting for transfers between devices, ring_shift(): return lax.ppermute(x, axis, [(i, (i + by) % size) for i in range(size)])  7.73 us
    pallas_call x4, Pallas kernels, choose(): pl.pallas_call(choose_kernel, in_specs=[smem, smem] + [hbm] * (3 + len(af...  6.9 us
    ppermute x5, starting transfers between devices, pair_swap(): return lax.ppermute(x, axis, [(i, i ^ 1) for i in range(size)])  6.76 us
    unnamed x3, local copies, waits for them, and re-layouts  1.97 us
    pallas_call x1, Pallas kernels, channels_first(): pl.pallas_call(channels_first_kernel, out_shape=[pltpu.VMEM((own.shape[1]...  1.72 us
  transfers between devices with their start and end apart: 22, of which 7 were waited for; matrix products, arithmetic and copies ran while one was open for 4% of the time, Pallas kernels for 30%

profile of v2, /device:TPU:0, one launch (start us, length us, event | category | flops | bytes accessed | tf_op | source)
XLA Modules:
  0.0 75.9 jit_solution(17987381076438862579)
XLA Ops:
  0.0 1.2 %copy-done = bf16[8,2,256,128]{3,2,1,0:T(8,128)(2,1)S(1)} copy-done((bf16[8,2,256,128]{3,2,1,0:T(8,128)(2,1)S(1)}, bf16[8,2,256,128]{3,2,1,0:T(8,128)(2,1)}, u32[]{:S(2)}) %copy-start) | copy-done | bytes 1048600
  1.2 0.8 %shard_map.28 = (bf16[1024,128]{1,0:T(8,128)(2,1)S(1)}, bf16[1024,128]{1,0:T(8,128)(2,1)S(1)}, bf16[1024,128]{1,0:T(8,128)(2,1)S(1)}, bf16[4096,128]{1,0:T(8,128)(2,1)S(1)}) custom-call(bf16[8,2,256,128]{3,2,1,0:T(8,128)(2,1)S(1)} %copy-done), custom_call_target="tpu_custom_call" | custom-call | tf_op jit(solution)/shard_map/pallas_call | solution.py:163
  2.0 0.5 collective-permute-start
  2.5 0.1 shard_map.31.mine
  2.7 4.7 %collective-permute-start.10 = (bf16[1024,128]{1,0:T(8,128)(2,1)S(1)}, bf16[1024,128]{1,0:T(8,128)(2,1)}, u32[]{:S(2)}, u32[]{:S(2)}) collective-permute-start(bf16[1024,128]{1,0:T(8,128)(2,1)S(1)} %shard_map.31.mine), channel_id=1, source_target_pairs={{0,12},{2,14},{4,0},{6,2},{8,4},{10,6},{12,8},{14,10},{1,13},{3,15... | collective-permute-start | bytes 786440 | tf_op jit(solution)/shard_map/two_ahead_0/ppermute | solution.py:24
  7.3 0.0 collective-permute-start.9
  7.3 3.9 %collective-permute-start.5 = (bf16[1024,128]{1,0:T(8,128)(2,1)S(1)}, bf16[1024,128]{1,0:T(8,128)(2,1)}, u32[]{:S(2)}, u32[]{:S(2)}) collective-permute-start(bf16[1024,128]{1,0:T(8,128)(2,1)S(1)} %get-tuple-element.43.mine), channel_id=1, source_target_pairs={{0,12},{2,14},{4,0},{6,2},{8,4},{10,6},{12,8},{14,10},{1,13},{3,15... | collective-permute-start | bytes 786440 | tf_op jit(solution)/shard_map/two_ahead_1/ppermute | solution.py:24
  11.2 0.6 fusion.4
  11.8 0.7 fusion
  12.5 1.0 %copy.18.rest_1_.refs_0_ = bf16[64,512]{1,0:T(8,128)(2,1)S(1)} copy(bf16[64,512]{0,1:T(8,128)(2,1)} %bitcast.8) | data formatting | bytes 131072 | tf_op jit(solution)/shard_map/reshape | solution.py:41
  13.5 0.7 copy.15.direction
  14.2 0.0 collective-permute-done.other
  14.2 1.5 %collective-permute-start.1 = (s32[1]{0:T(128)}, s32[1]{0:T(128)}, u32[]{:S(2)}, u32[]{:S(2)}) collective-permute-start(s32[1]{0:T(128)} %bitcast.9), channel_id=1, source_target_pairs={{0,2},{2,0},{4,6},{6,4},{8,10},{10,8},{12,14},{14,12},{1,3},{3,1},... | collective-permute-start | bytes 20 | tf_op jit(solution)/shard_map/direction_of_pair/ppermute | solution.py:29
  15.8 1.7 %shard_map.29 = (f32[128,1024]{1,0:T(8,128)S(1)}, f32[128,1024]{1,0:T(8,128)S(1)}, f32[128,1024]{1,0:T(8,128)S(1)}, f32[128,1024]{1,0:T(8,128)S(1)}, f32[128,102...) custom-call(bf16[4096,128]{1,0:T(8,128)(2,1)S(1)} %get-tuple-element, ...), custom_call_target="tpu_custom_call" | custom-call | tf_op jit(solution)/shard_map/pallas_call | solution.py:191
  17.5 0.5 collective-permute-done.1.of_pair
  18.0 2.7 %collective-permute-done.9.behind = bf16[1024,128]{1,0:T(8,128)(2,1)} collective-permute-done((bf16[1024,128]{1,0:T(8,128)(2,1)S(1)}, bf16[1024,128]{1,0:T(8,128)(2,1)}, u32[]{:S(2)}, u32[]{:S(2)}) %collective-permute-start.9) | collective-permute-done | bytes 262176 | tf_op jit(solution)/shard_map/two_behind_0/ppermute | solution.py:24
  20.7 2.2 %shard_map.32 = (bf16[1024,128]{1,0:T(8,128)(2,1)S(1)}, bf16[1024,128]{1,0:T(8,128)(2,1)S(1)}) custom-call(s32[2,1]{1,0:T(2,128)S(1)} %copy.15.direction, s32[1]{0:T(128)} %collective-permute-done.1.of_pair, bf16[1024,128]{1,0:T(8,128)(2,1)S(1)} %shard_map.31.mine, bf16[1024,128]{1,0:T(8,128)(2,1)} %collective-permute-done.9.behind, ...), custom_call_target="tpu_custom_call" | custom-call | tf_op jit(solution)/shard_map/pallas_call | solution.py:224
  22.9 1.6 %collective-permute-start.11 = (bf16[1024,128]{1,0:T(8,128)(2,1)S(1)}, bf16[1024,128]{1,0:T(8,128)(2,1)S(1)}, u32[]{:S(2)}, u32[]{:S(2)}) collective-permute-start(bf16[1024,128]{1,0:T(8,128)(2,1)S(1)} %get-tuple-element.50), channel_id=1, source_target_pairs={{0,2},{2,0},{4,6},{6,4},{8,10},{10,8},{12,14},{14,12},{1,3},{3,1},... | collective-permute-start | bytes 786440 | tf_op jit(solution)/shard_map/near_0/ppermute | solution.py:29
  24.5 1.4 %collective-permute-start.17 = (bf16[1024,128]{1,0:T(8,128)(2,1)S(1)}, bf16[1024,128]{1,0:T(8,128)(2,1)S(1)}, u32[]{:S(2)}, u32[]{:S(2)}) collective-permute-start(bf16[1024,128]{1,0:T(8,128)(2,1)S(1)} %get-tuple-element.58.mine), channel_id=1, source_target_pairs={{0,4},{2,6},{4,8},{6,10},{8,12},{10,14},{12,0},{14,2},{1,5},{3,7},... | collective-permute-start | bytes 786440 | tf_op jit(solution)/shard_map/two_behind_2/ppermute | solution.py:24
  25.9 0.2 collective-permute-done.4.behind
  26.2 4.8 %collective-permute-done.5.ahead = bf16[1024,128]{1,0:T(8,128)(2,1)} collective-permute-done((bf16[1024,128]{1,0:T(8,128)(2,1)S(1)}, bf16[1024,128]{1,0:T(8,128)(2,1)}, u32[]{:S(2)}, u32[]{:S(2)}) %collective-permute-start.5) | collective-permute-done | bytes 262176 | tf_op jit(solution)/shard_map/two_ahead_1/ppermute | solution.py:24
  30.9 2.2 %shard_map.30 = (bf16[1024,128]{1,0:T(8,128)(2,1)S(1)}, bf16[1024,128]{1,0:T(8,128)(2,1)S(1)}) custom-call(s32[2,1]{1,0:T(2,128)S(1)} %copy.15.direction, s32[1]{0:T(128)} %collective-permute-done.1.of_pair, bf16[1024,128]{1,0:T(8,128)(2,1)S(1)} %get-tuple-element.43.mine, bf16[1024,128]{1,0:T(8,128)(2,1)S(1)} %collective-permute-done.4.behind, ...), custom_call_target="tpu_custom_call" | custom-call | tf_op jit(solution)/shard_map/pallas_call | solution.py:224
  33.1 1.5 %collective-permute-start.6 = (bf16[1024,128]{1,0:T(8,128)(2,1)S(1)}, bf16[1024,128]{1,0:T(8,128)(2,1)S(1)}, u32[]{:S(2)}, u32[]{:S(2)}) collective-permute-start(bf16[1024,128]{1,0:T(8,128)(2,1)S(1)} %get-tuple-element.44), channel_id=1, source_target_pairs={{0,2},{2,0},{4,6},{6,4},{8,10},{10,8},{12,14},{14,12},{1,3},{3,1},... | collective-permute-start | bytes 786440 | tf_op jit(solution)/shard_map/near_1/ppermute | solution.py:29
  34.6 0.0 collective-permute-done.11.refs_5_
  34.6 0.5 collective-permute-start.12
  35.1 3.5 %collective-permute-start.18 = (bf16[1024,128]{1,0:T(8,128)(2,1)S(1)}, bf16[1024,128]{1,0:T(8,128)(2,1)S(1)}, u32[]{:S(2)}, u32[]{:S(2)}) collective-permute-start(bf16[1024,128]{1,0:T(8,128)(2,1)S(1)} %get-tuple-element.58.mine), channel_id=1, source_target_pairs={{0,12},{2,14},{4,0},{6,2},{8,4},{10,6},{12,8},{14,10},{1,13},{3,15... | collective-permute-start | bytes 786440 | tf_op jit(solution)/shard_map/two_ahead_2/ppermute | solution.py:24
  38.6 0.0 collective-permute-done.17.behind
  38.7 0.0 collective-permute-start.8
  38.7 2.0 %collective-permute-done.6.refs_5_ = bf16[1024,128]{1,0:T(8,128)(2,1)S(1)} collective-permute-done((bf16[1024,128]{1,0:T(8,128)(2,1)S(1)}, bf16[1024,128]{1,0:T(8,128)(2,1)S(1)}, u32[]{:S(2)}, u32[]{:S(2)}) %collective-permute-start.6) | collective-permute-done | bytes 262176 | tf_op jit(solution)/shard_map/near_1/ppermute | solution.py:29
  40.7 0.4 collective-permute-start.2
  41.1 4.0 %collective-permute-start.3 = (bf16[1024,128]{1,0:T(8,128)(2,1)S(1)}, bf16[1024,128]{1,0:T(8,128)(2,1)S(1)}, u32[]{:S(2)}, u32[]{:S(2)}) collective-permute-start(bf16[1024,128]{1,0:T(8,128)(2,1)S(1)} %get-tuple-element.38.mine), channel_id=1, source_target_pairs={{0,12},{2,14},{4,0},{6,2},{8,4},{10,6},{12,8},{14,10},{1,13},{3,15... | collective-permute-start | bytes 786440 | tf_op jit(solution)/shard_map/two_ahead_3/ppermute | solution.py:24
  45.1 4.4 %shard_map.33.refs_9_.rest_0_ = f32[2,32,128,128]{3,2,1,0:T(8,128)S(1)} custom-call(bf16[64,512]{1,0:T(8,128)(2,1)S(1)} %copy.18.rest_1_.refs_0_, f32[128,1024]{1,0:T(8,128)S(1)} %get-tuple-element.46.rest_0_.refs_1_, f32[128,1024]{1,0:T(8,128)S(1)} %get-tuple-element.47.refs_2_, f32[128,1024]{1,0:T(8,128)S(1)} %get-tuple-element.48.refs_3_, ...), custom_call_target="tpu_custom_call" | custom-call | tf_op jit(solution)/shard_map/pallas_call | solution.py:135
  49.5 0.0 collective-permute-done.18.ahead
  49.5 1.3 %shard_map.36 = (bf16[1024,128]{1,0:T(8,128)(2,1)S(1)}, bf16[1024,128]{1,0:T(8,128)(2,1)S(1)}) custom-call(s32[2,1]{1,0:T(2,128)S(1)} %copy.15.direction, s32[1]{0:T(128)} %collective-permute-done.1.of_pair, bf16[1024,128]{1,0:T(8,128)(2,1)S(1)} %get-tuple-element.58.mine, bf16[1024,128]{1,0:T(8,128)(2,1)S(1)} %collective-permute-done.17.behind, ...), custom_call_target="tpu_custom_call" | custom-call | tf_op jit(solution)/shard_map/pallas_call | solution.py:224
  50.8 0.9 %collective-permute-start.19 = (bf16[1024,128]{1,0:T(8,128)(2,1)S(1)}, bf16[1024,128]{1,0:T(8,128)(2,1)S(1)}, u32[]{:S(2)}, u32[]{:S(2)}) collective-permute-start(bf16[1024,128]{1,0:T(8,128)(2,1)S(1)} %get-tuple-element.59), channel_id=1, source_target_pairs={{0,2},{2,0},{4,6},{6,4},{8,10},{10,8},{12,14},{14,12},{1,3},{3,1},... | collective-permute-start | bytes 786440 | tf_op jit(solution)/shard_map/near_2/ppermute | solution.py:29
  51.7 4.7 %shard_map.34.rest_0_.refs_9_ = f32[2,32,128,128]{3,2,1,0:T(8,128)S(1)} custom-call(bf16[64,512]{1,0:T(8,128)(2,1)S(1)} %copy.18.rest_1_.refs_0_, f32[128,1024]{1,0:T(8,128)S(1)} %get-tuple-element.39.refs_1_, f32[128,1024]{1,0:T(8,128)S(1)} %get-tuple-element.40.refs_2_, f32[128,1024]{1,0:T(8,128)S(1)} %get-tuple-element.41.refs_3_, ...), custom_call_target="tpu_custom_call", output_to_operand_aliasing={{}: (9, {})} | custom-call | tf_op jit(solution)/shard_map/pallas_call | solution.py:135
  56.4 0.0 collective-permute-done.3.ahead
  56.4 1.3 %shard_map.35 = (bf16[1024,128]{1,0:T(8,128)(2,1)S(1)}, bf16[1024,128]{1,0:T(8,128)(2,1)S(1)}) custom-call(s32[2,1]{1,0:T(2,128)S(1)} %copy.15.direction, s32[1]{0:T(128)} %collective-permute-done.1.of_pair, bf16[1024,128]{1,0:T(8,128)(2,1)S(1)} %get-tuple-element.38.mine, bf16[1024,128]{1,0:T(8,128)(2,1)S(1)} %collective-permute-done.2.behind, ...), custom_call_target="tpu_custom_call" | custom-call | tf_op jit(solution)/shard_map/pallas_call | solution.py:224
  57.7 1.2 %collective-permute-start.14 = (bf16[1024,128]{1,0:T(8,128)(2,1)S(1)}, bf16[1024,128]{1,0:T(8,128)(2,1)S(1)}, u32[]{:S(2)}, u32[]{:S(2)}) collective-permute-start(bf16[1024,128]{1,0:T(8,128)(2,1)S(1)} %get-tuple-element.52), channel_id=1, source_target_pairs={{0,2},{2,0},{4,6},{6,4},{8,10},{10,8},{12,14},{14,12},{1,3},{3,1},... | collective-permute-start | bytes 786440 | tf_op jit(solution)/shard_map/near_3/ppermute | solution.py:29
  58.9 0.3 collective-permute-done.19.refs_5_
  59.2 0.2 collective-permute-start.20
  59.4 0.3 collective-permute-start.16
  59.7 5.9 %collective-permute-done.14.refs_5_ = bf16[1024,128]{1,0:T(8,128)(2,1)S(1)} collective-permute-done((bf16[1024,128]{1,0:T(8,128)(2,1)S(1)}, bf16[1024,128]{1,0:T(8,128)(2,1)S(1)}, u32[]{:S(2)}, u32[]{:S(2)}) %collective-permute-start.14) | collective-permute-done | bytes 262176 | tf_op jit(solution)/shard_map/near_3/ppermute | solution.py:29
  65.7 0.0 collective-permute-start.15
  65.7 0.0 collective-permute-done.21.refs_8_
  65.7 4.7 %shard_map.37.refs_9_ = f32[2,32,128,128]{3,2,1,0:T(8,128)S(1)} custom-call(bf16[64,512]{1,0:T(8,128)(2,1)S(1)} %copy.18.rest_1_.refs_0_, f32[128,1024]{1,0:T(8,128)S(1)} %get-tuple-element.54.refs_1_, f32[128,1024]{1,0:T(8,128)S(1)} %get-tuple-element.55.refs_2_, f32[128,1024]{1,0:T(8,128)S(1)} %get-tuple-element.56.refs_3_, ...), custom_call_target="tpu_custom_call", output_to_operand_aliasing={{}: (9, {})} | custom-call | tf_op jit(solution)/shard_map/pallas_call | solution.py:135
  70.4 0.0 collective-permute-done.16.refs_8_
  70.4 5.5 %shard_map.38 = f32[2,32,128,128]{3,2,1,0:T(8,128)} custom-call(bf16[64,512]{1,0:T(8,128)(2,1)S(1)} %copy.18.rest_1_.refs_0_, f32[128,1024]{1,0:T(8,128)S(1)} %get-tuple-element.34.refs_1_, f32[128,1024]{1,0:T(8,128)S(1)} %get-tuple-element.35.refs_2_, f32[128,1024]{1,0:T(8,128)S(1)} %get-tuple-element.36.refs_3_, ...), custom_call_target="tpu_custom_call" | custom-call | tf_op jit(solution)/shard_map/pallas_call | solution.py:135
  (15 shorter events, 0.0 us)
Async XLA Ops:
  0.0 1.2 %copy-start = (bf16[8,2,256,128]{3,2,1,0:T(8,128)(2,1)S(1)}, bf16[8,2,256,128]{3,2,1,0:T(8,128)(2,1)}, u32[]{:S(2)}) copy-start(bf16[8,2,256,128]{3,2,1,0:T(8,128)(2,1)} %x.3) | copy-start | bytes 3145732
  2.0 12.2 %collective-permute-start = (bf16[4096,128]{1,0:T(8,128)(2,1)S(1)}, bf16[4096,128]{1,0:T(8,128)(2,1)S(1)}, u32[]{:S(2)}, u32[]{:S(2)}) collective-permute-start(bf16[4096,128]{1,0:T(8,128)(2,1)S(1)} %get-tuple-element.33.own), channel_id=1, source_target_pairs={{0,1},{1,0},{2,3},{3,2},{4,5},{5,4},{6,7},{7,6},{8,9},{9,8},{10,11... | collective-permute-start | bytes 3145736 | tf_op jit(solution)/shard_map/my_other_half/ppermute | solution.py:24
  2.7 15.4 %collective-permute-start.10 = (bf16[1024,128]{1,0:T(8,128)(2,1)S(1)}, bf16[1024,128]{1,0:T(8,128)(2,1)}, u32[]{:S(2)}, u32[]{:S(2)}) collective-permute-start(bf16[1024,128]{1,0:T(8,128)(2,1)S(1)} %shard_map.31.mine), channel_id=1, source_target_pairs={{0,12},{2,14},{4,0},{6,2},{8,4},{10,6},{12,8},{14,10},{1,13},{3,15... | collective-permute-start | bytes 786440 | tf_op jit(solution)/shard_map/two_ahead_0/ppermute | solution.py:24
  7.3 13.4 %collective-permute-start.9 = (bf16[1024,128]{1,0:T(8,128)(2,1)S(1)}, bf16[1024,128]{1,0:T(8,128)(2,1)}, u32[]{:S(2)}, u32[]{:S(2)}) collective-permute-start(bf16[1024,128]{1,0:T(8,128)(2,1)S(1)} %shard_map.31.mine), channel_id=1, source_target_pairs={{0,4},{2,6},{4,8},{6,10},{8,12},{10,14},{12,0},{14,2},{1,5},{3,7},... | collective-permute-start | bytes 786440 | tf_op jit(solution)/shard_map/two_behind_0/ppermute | solution.py:24
  7.3 18.8 %collective-permute-start.4 = (bf16[1024,128]{1,0:T(8,128)(2,1)S(1)}, bf16[1024,128]{1,0:T(8,128)(2,1)S(1)}, u32[]{:S(2)}, u32[]{:S(2)}) collective-permute-start(bf16[1024,128]{1,0:T(8,128)(2,1)S(1)} %get-tuple-element.43.mine), channel_id=1, source_target_pairs={{0,4},{2,6},{4,8},{6,10},{8,12},{10,14},{12,0},{14,2},{1,5},{3,7},... | collective-permute-start | bytes 786440 | tf_op jit(solution)/shard_map/two_behind_1/ppermute | solution.py:24
  7.3 23.6 %collective-permute-start.5 = (bf16[1024,128]{1,0:T(8,128)(2,1)S(1)}, bf16[1024,128]{1,0:T(8,128)(2,1)}, u32[]{:S(2)}, u32[]{:S(2)}) collective-permute-start(bf16[1024,128]{1,0:T(8,128)(2,1)S(1)} %get-tuple-element.43.mine), channel_id=1, source_target_pairs={{0,12},{2,14},{4,0},{6,2},{8,4},{10,6},{12,8},{14,10},{1,13},{3,15... | collective-permute-start | bytes 786440 | tf_op jit(solution)/shard_map/two_ahead_1/ppermute | solution.py:24
  14.2 3.8 %collective-permute-start.1 = (s32[1]{0:T(128)}, s32[1]{0:T(128)}, u32[]{:S(2)}, u32[]{:S(2)}) collective-permute-start(s32[1]{0:T(128)} %bitcast.9), channel_id=1, source_target_pairs={{0,2},{2,0},{4,6},{6,4},{8,10},{10,8},{12,14},{14,12},{1,3},{3,1},... | collective-permute-start | bytes 20 | tf_op jit(solution)/shard_map/direction_of_pair/ppermute | solution.py:29
  22.9 11.7 %collective-permute-start.11 = (bf16[1024,128]{1,0:T(8,128)(2,1)S(1)}, bf16[1024,128]{1,0:T(8,128)(2,1)S(1)}, u32[]{:S(2)}, u32[]{:S(2)}) collective-permute-start(bf16[1024,128]{1,0:T(8,128)(2,1)S(1)} %get-tuple-element.50), channel_id=1, source_target_pairs={{0,2},{2,0},{4,6},{6,4},{8,10},{10,8},{12,14},{14,12},{1,3},{3,1},... | collective-permute-start | bytes 786440 | tf_op jit(solution)/shard_map/near_0/ppermute | solution.py:29
  24.5 14.1 %collective-permute-start.17 = (bf16[1024,128]{1,0:T(8,128)(2,1)S(1)}, bf16[1024,128]{1,0:T(8,128)(2,1)S(1)}, u32[]{:S(2)}, u32[]{:S(2)}) collective-permute-start(bf16[1024,128]{1,0:T(8,128)(2,1)S(1)} %get-tuple-element.58.mine), channel_id=1, source_target_pairs={{0,4},{2,6},{4,8},{6,10},{8,12},{10,14},{12,0},{14,2},{1,5},{3,7},... | collective-permute-start | bytes 786440 | tf_op jit(solution)/shard_map/two_behind_2/ppermute | solution.py:24
  33.1 7.6 %collective-permute-start.6 = (bf16[1024,128]{1,0:T(8,128)(2,1)S(1)}, bf16[1024,128]{1,0:T(8,128)(2,1)S(1)}, u32[]{:S(2)}, u32[]{:S(2)}) collective-permute-start(bf16[1024,128]{1,0:T(8,128)(2,1)S(1)} %get-tuple-element.44), channel_id=1, source_target_pairs={{0,2},{2,0},{4,6},{6,4},{8,10},{10,8},{12,14},{14,12},{1,3},{3,1},... | collective-permute-start | bytes 786440 | tf_op jit(solution)/shard_map/near_1/ppermute | solution.py:29
  34.6 6.1 %collective-permute-start.13 = (bf16[1024,128]{1,0:T(8,128)(2,1)S(1)}, bf16[1024,128]{1,0:T(8,128)(2,1)S(1)}, u32[]{:S(2)}, u32[]{:S(2)}) collective-permute-start(bf16[1024,128]{1,0:T(8,128)(2,1)S(1)} %get-tuple-element.51.refs_7_), channel_id=1, source_target_pairs={{0,1},{1,0},{2,3},{3,2},{4,5},{5,4},{6,7},{7,6},{8,9},{9,8},{10,11... | collective-permute-start | bytes 786440 | tf_op jit(solution)/shard_map/far_other_half_0/ppermute | solution.py:24
  34.6 6.5 %collective-permute-start.12 = (bf16[1024,128]{1,0:T(8,128)(2,1)S(1)}, bf16[1024,128]{1,0:T(8,128)(2,1)S(1)}, u32[]{:S(2)}, u32[]{:S(2)}) collective-permute-start(bf16[1024,128]{1,0:T(8,128)(2,1)S(1)} %collective-permute-done.11.refs_5_), channel_id=1, source_target_pairs={{0,1},{1,0},{2,3},{3,2},{4,5},{5,4},{6,7},{7,6},{8,9},{9,8},{10,11... | collective-permute-start | bytes 786440 | tf_op jit(solution)/shard_map/near_other_half_0/ppermute | solution.py:24
  35.1 14.3 %collective-permute-start.18 = (bf16[1024,128]{1,0:T(8,128)(2,1)S(1)}, bf16[1024,128]{1,0:T(8,128)(2,1)S(1)}, u32[]{:S(2)}, u32[]{:S(2)}) collective-permute-start(bf16[1024,128]{1,0:T(8,128)(2,1)S(1)} %get-tuple-element.58.mine), channel_id=1, source_target_pairs={{0,12},{2,14},{4,0},{6,2},{8,4},{10,6},{12,8},{14,10},{1,13},{3,15... | collective-permute-start | bytes 786440 | tf_op jit(solution)/shard_map/two_ahead_2/ppermute | solution.py:24
  38.7 13.0 %collective-permute-start.8 = (bf16[1024,128]{1,0:T(8,128)(2,1)S(1)}, bf16[1024,128]{1,0:T(8,128)(2,1)S(1)}, u32[]{:S(2)}, u32[]{:S(2)}) collective-permute-start(bf16[1024,128]{1,0:T(8,128)(2,1)S(1)} %get-tuple-element.45.refs_7_), channel_id=1, source_target_pairs={{0,1},{1,0},{2,3},{3,2},{4,5},{5,4},{6,7},{7,6},{8,9},{9,8},{10,11... | collective-permute-start | bytes 786440 | tf_op jit(solution)/shard_map/far_other_half_1/ppermute | solution.py:24
  40.7 11.0 %collective-permute-start.7 = (bf16[1024,128]{1,0:T(8,128)(2,1)S(1)}, bf16[1024,128]{1,0:T(8,128)(2,1)S(1)}, u32[]{:S(2)}, u32[]{:S(2)}) collective-permute-start(bf16[1024,128]{1,0:T(8,128)(2,1)S(1)} %collective-permute-done.6.refs_5_), channel_id=1, source_target_pairs={{0,1},{1,0},{2,3},{3,2},{4,5},{5,4},{6,7},{7,6},{8,9},{9,8},{10,11... | collective-permute-start | bytes 786440 | tf_op jit(solution)/shard_map/near_other_half_1/ppermute | solution.py:24
  40.7 15.7 %collective-permute-start.2 = (bf16[1024,128]{1,0:T(8,128)(2,1)S(1)}, bf16[1024,128]{1,0:T(8,128)(2,1)S(1)}, u32[]{:S(2)}, u32[]{:S(2)}) collective-permute-start(bf16[1024,128]{1,0:T(8,128)(2,1)S(1)} %get-tuple-element.38.mine), channel_id=1, source_target_pairs={{0,4},{2,6},{4,8},{6,10},{8,12},{10,14},{12,0},{14,2},{1,5},{3,7},... | collective-permute-start | bytes 786440 | tf_op jit(solution)/shard_map/two_behind_3/ppermute | solution.py:24
  41.1 15.3 %collective-permute-start.3 = (bf16[1024,128]{1,0:T(8,128)(2,1)S(1)}, bf16[1024,128]{1,0:T(8,128)(2,1)S(1)}, u32[]{:S(2)}, u32[]{:S(2)}) collective-permute-start(bf16[1024,128]{1,0:T(8,128)(2,1)S(1)} %get-tuple-element.38.mine), channel_id=1, source_target_pairs={{0,12},{2,14},{4,0},{6,2},{8,4},{10,6},{12,8},{14,10},{1,13},{3,15... | collective-permute-start | bytes 786440 | tf_op jit(solution)/shard_map/two_ahead_3/ppermute | solution.py:24
  50.8 8.5 %collective-permute-start.19 = (bf16[1024,128]{1,0:T(8,128)(2,1)S(1)}, bf16[1024,128]{1,0:T(8,128)(2,1)S(1)}, u32[]{:S(2)}, u32[]{:S(2)}) collective-permute-start(bf16[1024,128]{1,0:T(8,128)(2,1)S(1)} %get-tuple-element.59), channel_id=1, source_target_pairs={{0,2},{2,0},{4,6},{6,4},{8,10},{10,8},{12,14},{14,12},{1,3},{3,1},... | collective-permute-start | bytes 786440 | tf_op jit(solution)/shard_map/near_2/ppermute | solution.py:29
  57.7 8.0 %collective-permute-start.14 = (bf16[1024,128]{1,0:T(8,128)(2,1)S(1)}, bf16[1024,128]{1,0:T(8,128)(2,1)S(1)}, u32[]{:S(2)}, u32[]{:S(2)}) collective-permute-start(bf16[1024,128]{1,0:T(8,128)(2,1)S(1)} %get-tuple-element.52), channel_id=1, source_target_pairs={{0,2},{2,0},{4,6},{6,4},{8,10},{10,8},{12,14},{14,12},{1,3},{3,1},... | collective-permute-start | bytes 786440 | tf_op jit(solution)/shard_map/near_3/ppermute | solution.py:29
  58.9 6.8 %collective-permute-start.21 = (bf16[1024,128]{1,0:T(8,128)(2,1)S(1)}, bf16[1024,128]{1,0:T(8,128)(2,1)S(1)}, u32[]{:S(2)}, u32[]{:S(2)}) collective-permute-start(bf16[1024,128]{1,0:T(8,128)(2,1)S(1)} %get-tuple-element.60.refs_7_), channel_id=1, source_target_pairs={{0,1},{1,0},{2,3},{3,2},{4,5},{5,4},{6,7},{7,6},{8,9},{9,8},{10,11... | collective-permute-start | bytes 786440 | tf_op jit(solution)/shard_map/far_other_half_2/ppermute | solution.py:24
  59.2 6.4 %collective-permute-start.20 = (bf16[1024,128]{1,0:T(8,128)(2,1)S(1)}, bf16[1024,128]{1,0:T(8,128)(2,1)S(1)}, u32[]{:S(2)}, u32[]{:S(2)}) collective-permute-start(bf16[1024,128]{1,0:T(8,128)(2,1)S(1)} %collective-permute-done.19.refs_5_), channel_id=1, source_target_pairs={{0,1},{1,0},{2,3},{3,2},{4,5},{5,4},{6,7},{7,6},{8,9},{9,8},{10,11... | collective-permute-start | bytes 786440 | tf_op jit(solution)/shard_map/near_other_half_2/ppermute | solution.py:24
  59.4 11.0 %collective-permute-start.16 = (bf16[1024,128]{1,0:T(8,128)(2,1)S(1)}, bf16[1024,128]{1,0:T(8,128)(2,1)S(1)}, u32[]{:S(2)}, u32[]{:S(2)}) collective-permute-start(bf16[1024,128]{1,0:T(8,128)(2,1)S(1)} %get-tuple-element.53.refs_7_), channel_id=1, source_target_pairs={{0,1},{1,0},{2,3},{3,2},{4,5},{5,4},{6,7},{7,6},{8,9},{9,8},{10,11... | collective-permute-start | bytes 786440 | tf_op jit(solution)/shard_map/far_other_half_3/ppermute | solution.py:24
  65.7 4.8 %collective-permute-start.15 = (bf16[1024,128]{1,0:T(8,128)(2,1)S(1)}, bf16[1024,128]{1,0:T(8,128)(2,1)S(1)}, u32[]{:S(2)}, u32[]{:S(2)}) collective-permute-start(bf16[1024,128]{1,0:T(8,128)(2,1)S(1)} %collective-permute-done.14.refs_5_), channel_id=1, source_target_pairs={{0,1},{1,0},{2,3},{3,2},{4,5},{5,4},{6,7},{7,6},{8,9},{9,8},{10,11... | collective-permute-start | bytes 786440 | tf_op jit(solution)/shard_map/near_other_half_3/ppermute | solution.py:24

commit v3 on v2

--- a/solution.py
+++ b/solution.py
@@ -12,10 +12,16 @@
 ROUNDS = 2
 GROUP = 8
 CHANNEL_BLOCK = 32
+UNROLL = 2
 CHUNKS = (64, 64, 64, 64)
-VMEM = 32 * 2**20
-AFTER = {2: 0, 3: 1}
-GATE = {}
+VMEM = 20 * 2**20
+AFTER = {3: 0}
+GATE = {3: 2}
+NEAR_GATE = {}
+SPLIT = False
+EXPAND = {}
+GATE_FAR = False
+LAG_FLOPS = 3e9
 COST = pl.CostEstimate(flops=0, bytes_accessed=0, transcendentals=0)
 
 
@@ -41,110 +47,156 @@
     return both.transpose(0, 2, 1, 3).reshape(lag_count, 2 * bin_count)
 
 
-def lag_kernel(*refs, first, has_total, last):
-    table, re_own, re_other, im_own, im_other, p0_own, p0_other, p1_own, p1_other = refs[:9]
-    total = refs[9] if has_total else None
-    out, cross = refs[9 + has_total : 11 + has_total]
-    rows = CHANNEL_BLOCK
-    channels, depth = re_own.shape
-    width = p0_own.shape[1]
-    tile = GROUP * 16
-    lag_count = out.shape[1]
-    mine = pl.ds(pl.multiple_of(lax.axis_index("sub") * lag_count, lag_count), lag_count)
-    weights = table[mine, 2 * first : 2 * (first + depth // 16)]
+def left_side(local, start, rows, lanes):
+    tile = lanes.stop - lanes.start
     bin_of_row = lax.broadcasted_iota(jnp.int32, (GROUP, tile), 0)
     bin_of_lane = lax.broadcasted_iota(jnp.int32, (GROUP, tile), 1) // (tile // GROUP)
     same_bin = bin_of_row == bin_of_lane
-
-    def spread(ref, i, lanes):
+    re_own, re_other, im_own, im_other = (ref.at[pl.ds(start, rows), :] for ref in local)
+
+    def spread(ref, i):
         return jnp.where(same_bin, jnp.broadcast_to(ref[i : i + 1, lanes], (GROUP, tile)), 0.0)
 
-    def block(b):
+    pieces = []
+    for i in range(rows):
+        own = jnp.concatenate([spread(re_own, i), spread(im_own, i)], axis=0)
+        other = jnp.concatenate([spread(re_other, i), spread(im_other, i)], axis=0)
+        pieces.append(jnp.concatenate([own, other], axis=1).astype(jnp.bfloat16))
+    return jnp.concatenate(pieces, axis=0)
+
+
+def left_sides_kernel(*refs):
+    local, out = refs[:4], refs[4]
+    channels, depth = local[0].shape
+    rows = CHANNEL_BLOCK
+    tile = GROUP * 16
+
+    @pl.loop(0, channels // rows)
+    def _(b):
         start = pl.multiple_of(b * rows, rows)
-        here = [ref.at[pl.ds(start, rows), :] for ref in (re_own, im_own, re_other, im_other)]
+        for g in range(depth // tile):
+            at = pl.ds(pl.multiple_of(b * rows * 16, rows * 16), rows * 16)
+            out[g, at, :] = left_side(local, start, rows, slice(g * tile, (g + 1) * tile))
+
+
+def left_sides(local):
+    channels, depth = local[0].shape
+    vmem = pl.BlockSpec(memory_space=pltpu.VMEM)
+    return pl.pallas_call(
+        left_sides_kernel,
+        in_specs=[vmem] * len(local),
+        out_specs=vmem,
+        out_shape=pltpu.VMEM((depth // (GROUP * 16), channels * 2 * GROUP, 2 * GROUP * 16), jnp.bfloat16),
+        compiler_params=pltpu.CompilerParams(vmem_limit_bytes=VMEM),
+        cost_estimate=COST,
+    )(*local)
+
+
+def lag_kernel(*refs, first, rounds, local_count, has_total, last):
+    table, local, refs = refs[0], refs[1 : 1 + local_count], refs[1 + local_count :]
+    partners, refs = refs[: 2 * len(rounds)], refs[2 * len(rounds) :]
+    depth = partners[0].shape[0]
+    total, refs = (refs[0], refs[1:]) if has_total else (None, refs)
+    out, cross = refs[:2] if not last else refs[-4:-2]
+    rows = CHANNEL_BLOCK
+    width = partners[0].shape[1]
+    tile = GROUP * 16
+    _, lag_count, channels, _ = out.shape
+    mine = pl.ds(pl.multiple_of(lax.axis_index("sub") * lag_count, lag_count), lag_count)
+    weights = table[mine, 2 * first : 2 * (first + depth // 16)]
+    def block(b, slot):
+        start = pl.multiple_of(b * rows, rows)
         for g in range(depth // tile):
             lanes = slice(g * tile, (g + 1) * tile)
-            pieces = []
-            for i in range(rows):
-                own = jnp.concatenate([spread(here[0], i, lanes), spread(here[1], i, lanes)], axis=0)
-                other = jnp.concatenate([spread(here[2], i, lanes), spread(here[3], i, lanes)], axis=0)
-                pieces.append(jnp.concatenate([own, other], axis=1).astype(jnp.bfloat16))
-            left = jnp.concatenate(pieces, axis=0)
-            right = jnp.concatenate(
-                [
-                    jnp.concatenate([p0_own[lanes, :], p1_own[lanes, :]], axis=1),
-                    jnp.concatenate([p0_other[lanes, :], p1_other[lanes, :]], axis=1),
-                ],
-                axis=0,
-            )
+            if len(local) == 1:
+                left = local[0][g, pl.ds(pl.multiple_of(b * rows * 16, rows * 16), rows * 16), :]
+            else:
+                left = left_side(local, start, rows, lanes)
+            halves = [jnp.concatenate([x[lanes, :] for x in partners[k::2]], axis=1) for k in range(2)]
+            right = jnp.concatenate(halves, axis=0)
             part = jnp.dot(left, right, preferred_element_type=jnp.float32).astype(jnp.bfloat16)
-            cross[:, g * 2 * GROUP : (g + 1) * 2 * GROUP, :] = part.reshape(rows, 2 * GROUP, part.shape[-1])
+            cross[slot, :, g * 2 * GROUP : (g + 1) * 2 * GROUP, :] = part.reshape(rows, 2 * GROUP, part.shape[-1])
 
         for low in range(0, rows, 8):
-            lagged = [jnp.dot(weights, cross[i], preferred_element_type=jnp.float32) for i in range(low, low + 8)]
+            lagged = [jnp.dot(weights, cross[slot, i], preferred_element_type=jnp.float32) for i in range(low, low + 8)]
             at = pl.ds(pl.multiple_of(start + low, 8), 8)
-            for r in range(ROUNDS):
-                stacked = jnp.stack([x[:, r * width : (r + 1) * width] for x in lagged], axis=0)
+            for n, r in enumerate(rounds):
+                stacked = jnp.stack([x[:, n * width : (n + 1) * width] for x in lagged], axis=0)
                 tile_out = jnp.swapaxes(stacked, 0, 1)
                 if has_total:
                     tile_out = tile_out + total[r, :, at, :]
                 if last:
-                    stage[b, r, :, low : low + 8, :] = tile_out
+                    stage[b, n, :, low : low + 8, :] = tile_out
                 else:
                     out[r, :, at, :] = tile_out
 
     if last:
-        stage, sems = refs[11 + has_total :]
+        stage, sems = refs[-2:]
 
         def store(b):
             at = pl.ds(pl.multiple_of(b * rows, rows), rows)
-            return pltpu.make_async_copy(stage.at[b], out.at[:, :, at, :], sems.at[b])
-
-        @pl.loop(0, channels // rows)
+            there = out.at[rounds[0] : rounds[-1] + 1, :, at, :]
+            return pltpu.make_async_copy(stage.at[b], there, sems.at[b])
+
+        @pl.loop(0, channels // rows, step=UNROLL)
         def _(b):
-            block(b)
-            store(b).start()
+            for n in range(UNROLL):
+                block(b + n, n)
+                store(b + n).start()
 
         for b in range(channels // rows):
             store(b).wait()
     else:
 
-        @pl.loop(0, channels // rows)
+        @pl.loop(0, channels // rows, step=UNROLL)
         def _(b):
-            block(b)
-
-
-def add_lags(table, first, local, partners, total, last):
-    channels, depth = local[0].shape
+            for n in range(UNROLL):
+                block(b + n, n)
+
+
+def add_lags(table, first, local, partners, total, rounds=(0, 1), last=False, result=None):
+    depth, width = partners[0].shape
+    channels = local[0].shape[0] if len(local) > 1 else local[0].shape[1] // (2 * GROUP)
     lag_count = table.shape[0] // lax.axis_size("sub")
-    cross_depth = depth // 8
-    width = partners[0].shape[1]
     block = CHANNEL_BLOCK
     vmem = pl.BlockSpec(memory_space=pltpu.VMEM)
+    hbm = pl.BlockSpec(memory_space=pl.ANY)
     operands = [table, *local, *partners]
+    in_specs = [vmem] * len(operands)
     aliases = {}
     if total is not None:
         if not last:
             aliases = {len(operands): 0}
         operands.append(total)
+        in_specs.append(vmem)
+    if result is not None:
+        aliases = {len(operands): 0}
+        operands.append(result)
+        in_specs.append(hbm)
     shape = (ROUNDS, lag_count, channels, width)
-    scratch = [pltpu.VMEM((block, cross_depth, ROUNDS * width), jnp.bfloat16)]
+    scratch = [pltpu.VMEM((UNROLL, block, depth // 8, len(rounds) * width), jnp.bfloat16)]
     if last:
         blocks = channels // block
-        scratch += [pltpu.VMEM((blocks, ROUNDS, lag_count, block, width), jnp.float32), pltpu.SemaphoreType.DMA((blocks,))]
+        scratch += [
+            pltpu.VMEM((blocks, len(rounds), lag_count, block, width), jnp.float32),
+            pltpu.SemaphoreType.DMA((blocks,)),
+        ]
     return pl.pallas_call(
-        functools.partial(lag_kernel, first=first, has_total=total is not None, last=last),
-        in_specs=[vmem] * len(operands),
-        out_specs=pl.BlockSpec(memory_space=pl.ANY) if last else vmem,
+        functools.partial(lag_kernel, first=first, rounds=rounds, local_count=len(local), has_total=total is not None, last=last),
+        in_specs=in_specs,
+        out_specs=hbm if last else vmem,
         out_shape=jax.ShapeDtypeStruct(shape, jnp.float32) if last else pltpu.VMEM(shape, jnp.float32),
         input_output_aliases=aliases,
         scratch_shapes=scratch,
         compiler_params=pltpu.CompilerParams(vmem_limit_bytes=VMEM),
-        cost_estimate=COST,
+        cost_estimate=pl.CostEstimate(
+            flops=int(LAG_FLOPS) * len(rounds) // ROUNDS, bytes_accessed=0, transcendentals=0
+        ),
     )(*operands)
 
 
 def bins_first_kernel(x, *outs, sizes, first):
+    outs = outs[-len(sizes) :]
     for out, size in zip(outs, sizes):
         if size == x.shape[2] and first:
             first = 0
@@ -157,18 +209,19 @@
         first += size
 
 
-def bins_first(x, first, sizes):
+def bins_first(x, first, sizes, after):
     windows, parts, bins, channels = x.shape
     read = bins if first else sum(sizes)
     return pl.pallas_call(
         functools.partial(bins_first_kernel, sizes=sizes, first=first),
         grid=(1,),
-        in_specs=[pl.BlockSpec((windows, parts, read, channels), lambda b: (0, 0, 0, 0))],
+        in_specs=[pl.BlockSpec((windows, parts, read, channels), lambda b: (0, 0, 0, 0))]
+        + [pl.BlockSpec(memory_space=pl.ANY)] * len(after),
         out_specs=[pl.BlockSpec((size * parts * windows, channels), lambda b: (0, 0)) for size in sizes],
         out_shape=[jax.ShapeDtypeStruct((size * parts * windows, channels), x.dtype) for size in sizes],
         compiler_params=pltpu.CompilerParams(vmem_limit_bytes=VMEM),
         cost_estimate=COST,
-    )(x)
+    )(x, *after)
 
 
 def channels_first_kernel(own, other, *outs):
@@ -238,8 +291,8 @@
         of_pair = pair_swap(direction[0], "blk")
     table = make_table(bin_count, windows * lax.axis_size("sub"), LAGS)
 
-    mine = bins_first(spectra, 0, CHUNKS[:1])
-    *later, whole = bins_first(spectra, CHUNKS[0], (*CHUNKS[1:], bin_count))
+    mine = bins_first(spectra, 0, CHUNKS[:1], [])
+    *later, whole = bins_first(spectra, CHUNKS[0], (*CHUNKS[1:], bin_count), mine)
     mine = [*mine, *later]
     behind, ahead = [], []
     for n, x in enumerate(mine):
@@ -257,16 +310,32 @@
         after = [totals[AFTER[n] + 1]] if n in AFTER else []
         if n == 0:
             after = [local[0][0], table]
+        if n in EXPAND:
+            m = EXPAND[n]
+            local[m] = [left_sides(local[m])]
+            after = after + local[m]
         far_own, passed_on = choose(direction, of_pair, mine[n], behind[n], ahead[n], after)
+        if n in NEAR_GATE:
+            passed_on, _ = lax.optimization_barrier((passed_on, totals[NEAR_GATE[n] + 1]))
         with jax.named_scope(f"near_{n}"):
             near_own = pair_swap(passed_on, "blk")
         with jax.named_scope(f"far_other_half_{n}"):
             far_other = ring_shift(far_own, "sub", 1)
+        ends = n == len(CHUNKS) - 1
+        far_total = None
+        if ends and SPLIT:
+            far_total = add_lags(table, first, local[n], [far_own, far_other], totals[-1], (1,), True)
         if n in GATE:
-            near_own, _ = lax.optimization_barrier((near_own, totals[GATE[n] + 1]))
+            done = far_total if ends and SPLIT and GATE_FAR else totals[GATE[n] + 1]
+            near_own, _ = lax.optimization_barrier((near_own, done))
         with jax.named_scope(f"near_other_half_{n}"):
             near_other = ring_shift(near_own, "sub", 1)
-        totals.append(add_lags(table, first, local[n], [near_own, near_other, far_own, far_other], totals[-1], n == len(CHUNKS) - 1))
+        if ends and SPLIT:
+            total = add_lags(table, first, local[n], [near_own, near_other], totals[-1], (0,), True, far_total)
+        else:
+            partners = [near_own, near_other, far_own, far_other]
+            total = add_lags(table, first, local[n], partners, totals[-1], last=ends)
+        totals.append(total)
         first += size
     return totals[-1][:, None]
 

time: 76.6 us -> 74.3 us (0.970)
  Pallas kernels: 28.8 us -> 27.3 us
    ppermute x5, waiting for transfers between devices: 8.82 us -> 2.73 us  [pair_swap(): return lax.ppermute(x, axis, [(i, i ^ 1) for i in range(size)])]
    ppermute x17, waiting for transfers between devices: 7.73 us -> 13.8 us  [ring_shift(): return lax.ppermute(x, axis, [(i, (i + by) % size) for i in range(size)])]
    ppermute x17, starting transfers between devices: 19.4 us -> 17.3 us  [ring_shift(): return lax.ppermute(x, axis, [(i, (i + by) % size) for i in range(size)])]
    ppermute x5, starting transfers between devices: 6.76 us -> 8.27 us  [pair_swap(): return lax.ppermute(x, axis, [(i, i ^ 1) for i in range(size)])]
    pallas_call x4, Pallas kernels: 6.9 us -> 6.07 us  [choose(): pl.pallas_call(choose_kernel, in_specs=[smem, smem] + [hbm] * (3 + len(af...]
  transfers between devices with their start and end apart: 22 -> 22, of which waited for: 7 -> 7; matrix products, arithmetic and copies ran while one was open for 4% -> 4% of each run, Pallas kernels for 30% -> 29%
where the time goes in v3:
time: 74.3 us; the launch traced here: 74 us
  Pallas kernels  27.3 us (37%)
  starting transfers between devices  25.6 us (34%)
  waiting for transfers between devices  16.5 us (22%)
  local copies, waits for them, and re-layouts  2.96 us (4%)
  other arithmetic  1.29 us (2%)
    pallas_call x4, Pallas kernels, add_lags(): pl.pallas_call(functools.partial(lag_kernel, first=first, rounds=rounds,...  18.6 us
    ppermute x17, starting transfers between devices, ring_shift(): return lax.ppermute(x, axis, [(i, (i + by) % size) for i in range(size)])  17.3 us
    ppermute x17, waiting for transfers between devices, ring_shift(): return lax.ppermute(x, axis, [(i, (i + by) % size) for i in range(size)])  13.8 us
    ppermute x5, starting transfers between devices, pair_swap(): return lax.ppermute(x, axis, [(i, i ^ 1) for i in range(size)])  8.27 us
    pallas_call x4, Pallas kernels, choose(): pl.pallas_call(choose_kernel, in_specs=[smem, smem] + [hbm] * (3 + len(af...  6.07 us
    ppermute x5, waiting for transfers between devices, pair_swap(): return lax.ppermute(x, axis, [(i, i ^ 1) for i in range(size)])  2.73 us
    unnamed x3, local copies, waits for them, and re-layouts  1.97 us
    pallas_call x1, Pallas kernels, channels_first(): pl.pallas_call(channels_first_kernel, out_shape=[pltpu.VMEM((own.shape[1]...  1.72 us
  transfers between devices with their start and end apart: 22, of which 7 were waited for; matrix products, arithmetic and copies ran while one was open for 4% of the time, Pallas kernels for 29%

profile of v3, /device:TPU:0, one launch (start us, length us, event | category | flops | bytes accessed | tf_op | source)
XLA Modules:
  0.0 74.0 jit_solution(1203511829284964761)
XLA Ops:
  0.0 1.2 %copy-done = bf16[8,2,256,128]{3,2,1,0:T(8,128)(2,1)S(1)} copy-done((bf16[8,2,256,128]{3,2,1,0:T(8,128)(2,1)S(1)}, bf16[8,2,256,128]{3,2,1,0:T(8,128)(2,1)}, u32[]{:S(2)}) %copy-start) | copy-done | bytes 1048600
  1.2 0.1 shard_map.28.outs_0_.mine
  1.4 0.8 %shard_map.29 = (bf16[1024,128]{1,0:T(8,128)(2,1)S(1)}, bf16[1024,128]{1,0:T(8,128)(2,1)S(1)}, bf16[1024,128]{1,0:T(8,128)(2,1)S(1)}, bf16[4096,128]{1,0:T(8,128)(2,1)S(1)}) custom-call(bf16[8,2,256,128]{3,2,1,0:T(8,128)(2,1)S(1)} %copy-done, bf16[1024,128]{1,0:T(8,128)(2,1)S(1)} %shard_map.28.outs_0_.mine), custom_call_target="tpu_custom_call" | custom-call | tf_op jit(solution)/shard_map/pallas_call | solution.py:215
  2.2 0.5 collective-permute-start
  2.7 2.6 %collective-permute-start.4 = (bf16[1024,128]{1,0:T(8,128)(2,1)S(1)}, bf16[1024,128]{1,0:T(8,128)(2,1)}, u32[]{:S(2)}, u32[]{:S(2)}) collective-permute-start(bf16[1024,128]{1,0:T(8,128)(2,1)S(1)} %shard_map.28.outs_0_.mine), channel_id=1, source_target_pairs={{0,4},{2,6},{4,8},{6,10},{8,12},{10,14},{12,0},{14,2},{1,5},{3,7},... | collective-permute-start | bytes 786440 | tf_op jit(solution)/shard_map/two_behind_0/ppermute | solution.py:30
  5.3 2.1 %collective-permute-start.5 = (bf16[1024,128]{1,0:T(8,128)(2,1)S(1)}, bf16[1024,128]{1,0:T(8,128)(2,1)}, u32[]{:S(2)}, u32[]{:S(2)}) collective-permute-start(bf16[1024,128]{1,0:T(8,128)(2,1)S(1)} %shard_map.28.outs_0_.mine), channel_id=1, source_target_pairs={{0,12},{2,14},{4,0},{6,2},{8,4},{10,6},{12,8},{14,10},{1,13},{3,15... | collective-permute-start | bytes 786440 | tf_op jit(solution)/shard_map/two_ahead_0/ppermute | solution.py:30
  7.4 0.0 collective-permute-start.15
  7.4 3.8 %collective-permute-start.16 = (bf16[1024,128]{1,0:T(8,128)(2,1)S(1)}, bf16[1024,128]{1,0:T(8,128)(2,1)}, u32[]{:S(2)}, u32[]{:S(2)}) collective-permute-start(bf16[1024,128]{1,0:T(8,128)(2,1)S(1)} %get-tuple-element.58.mine), channel_id=1, source_target_pairs={{0,12},{2,14},{4,0},{6,2},{8,4},{10,6},{12,8},{14,10},{1,13},{3,15... | collective-permute-start | bytes 786440 | tf_op jit(solution)/shard_map/two_ahead_1/ppermute | solution.py:30
  11.3 0.6 fusion.4
  11.9 0.7 fusion
  12.6 1.0 %copy.18.rest_1_.refs_0_ = bf16[64,512]{1,0:T(8,128)(2,1)S(1)} copy(bf16[64,512]{0,1:T(8,128)(2,1)} %bitcast.8) | data formatting | bytes 131072 | tf_op jit(solution)/shard_map/reshape | solution.py:47
  13.5 0.7 %copy.13.direction = s32[2,1]{1,0:T(2,128)S(1)} copy(s32[2,1]{0,1:T(1,128)} %param.3) | data formatting | bytes 16 | tf_op args[1]
  14.3 1.7 %collective-permute-start.1 = (s32[1]{0:T(128)}, s32[1]{0:T(128)}, u32[]{:S(2)}, u32[]{:S(2)}) collective-permute-start(s32[1]{0:T(128)} %bitcast.9), channel_id=1, source_target_pairs={{0,2},{2,0},{4,6},{6,4},{8,10},{10,8},{12,14},{14,12},{1,3},{3,1},... | collective-permute-start | bytes 20 | tf_op jit(solution)/shard_map/direction_of_pair/ppermute | solution.py:35
  16.0 1.7 %shard_map.30 = (f32[128,1024]{1,0:T(8,128)S(1)}, f32[128,1024]{1,0:T(8,128)S(1)}, f32[128,1024]{1,0:T(8,128)S(1)}, f32[128,1024]{1,0:T(8,128)S(1)}, f32[128,102...) custom-call(bf16[4096,128]{1,0:T(8,128)(2,1)S(1)} %get-tuple-element, ...), custom_call_target="tpu_custom_call" | custom-call | tf_op jit(solution)/shard_map/pallas_call | solution.py:244
  17.7 0.4 collective-permute-done.1.of_pair
  18.1 0.0 collective-permute-done.4.behind
  18.1 2.2 %collective-permute-done.5.ahead = bf16[1024,128]{1,0:T(8,128)(2,1)} collective-permute-done((bf16[1024,128]{1,0:T(8,128)(2,1)S(1)}, bf16[1024,128]{1,0:T(8,128)(2,1)}, u32[]{:S(2)}, u32[]{:S(2)}) %collective-permute-start.5) | collective-permute-done | bytes 262176 | tf_op jit(solution)/shard_map/two_ahead_0/ppermute | solution.py:30
  20.3 2.1 %shard_map.31 = (bf16[1024,128]{1,0:T(8,128)(2,1)S(1)}, bf16[1024,128]{1,0:T(8,128)(2,1)S(1)}) custom-call(s32[2,1]{1,0:T(2,128)S(1)} %copy.13.direction, s32[1]{0:T(128)} %collective-permute-done.1.of_pair, bf16[1024,128]{1,0:T(8,128)(2,1)S(1)} %shard_map.28.outs_0_.mine, bf16[1024,128]{1,0:T(8,128)(2,1)} %collective-permute-done.4.behind, ...), custom_call_target="tpu_custom_call" | custom-call | tf_op jit(solution)/shard_map/pallas_call | solution.py:277
  22.4 1.7 %collective-permute-start.6 = (bf16[1024,128]{1,0:T(8,128)(2,1)S(1)}, bf16[1024,128]{1,0:T(8,128)(2,1)S(1)}, u32[]{:S(2)}, u32[]{:S(2)}) collective-permute-start(bf16[1024,128]{1,0:T(8,128)(2,1)S(1)} %get-tuple-element.44), channel_id=1, source_target_pairs={{0,2},{2,0},{4,6},{6,4},{8,10},{10,8},{12,14},{14,12},{1,3},{3,1},... | collective-permute-start | bytes 786440 | tf_op jit(solution)/shard_map/near_0/ppermute | solution.py:35
  24.2 0.6 collective-permute-start.10
  24.8 3.2 %collective-permute-start.11 = (bf16[1024,128]{1,0:T(8,128)(2,1)S(1)}, bf16[1024,128]{1,0:T(8,128)(2,1)S(1)}, u32[]{:S(2)}, u32[]{:S(2)}) collective-permute-start(bf16[1024,128]{1,0:T(8,128)(2,1)S(1)} %get-tuple-element.51.mine), channel_id=1, source_target_pairs={{0,12},{2,14},{4,0},{6,2},{8,4},{10,6},{12,8},{14,10},{1,13},{3,15... | collective-permute-start | bytes 786440 | tf_op jit(solution)/shard_map/two_ahead_2/ppermute | solution.py:30
  28.0 3.5 %collective-permute-done.16.ahead = bf16[1024,128]{1,0:T(8,128)(2,1)} collective-permute-done((bf16[1024,128]{1,0:T(8,128)(2,1)S(1)}, bf16[1024,128]{1,0:T(8,128)(2,1)}, u32[]{:S(2)}, u32[]{:S(2)}) %collective-permute-start.16) | collective-permute-done | bytes 262176 | tf_op jit(solution)/shard_map/two_ahead_1/ppermute | solution.py:30
  31.5 1.2 %shard_map.35 = (bf16[1024,128]{1,0:T(8,128)(2,1)S(1)}, bf16[1024,128]{1,0:T(8,128)(2,1)S(1)}) custom-call(s32[2,1]{1,0:T(2,128)S(1)} %copy.13.direction, s32[1]{0:T(128)} %collective-permute-done.1.of_pair, bf16[1024,128]{1,0:T(8,128)(2,1)S(1)} %get-tuple-element.58.mine, bf16[1024,128]{1,0:T(8,128)(2,1)S(1)} %collective-permute-done.15.behind, ...), custom_call_target="tpu_custom_call" | custom-call | tf_op jit(solution)/shard_map/pallas_call | solution.py:277
  32.8 1.7 %collective-permute-start.17 = (bf16[1024,128]{1,0:T(8,128)(2,1)S(1)}, bf16[1024,128]{1,0:T(8,128)(2,1)S(1)}, u32[]{:S(2)}, u32[]{:S(2)}) collective-permute-start(bf16[1024,128]{1,0:T(8,128)(2,1)S(1)} %get-tuple-element.59), channel_id=1, source_target_pairs={{0,2},{2,0},{4,6},{6,4},{8,10},{10,8},{12,14},{14,12},{1,3},{3,1},... | collective-permute-start | bytes 786440 | tf_op jit(solution)/shard_map/near_1/ppermute | solution.py:35
  34.5 0.0 collective-permute-done.6.refs_5_
  34.5 0.5 collective-permute-start.7
  35.0 2.1 %collective-permute-done.10.behind = bf16[1024,128]{1,0:T(8,128)(2,1)S(1)} collective-permute-done((bf16[1024,128]{1,0:T(8,128)(2,1)S(1)}, bf16[1024,128]{1,0:T(8,128)(2,1)S(1)}, u32[]{:S(2)}, u32[]{:S(2)}) %collective-permute-start.10) | collective-permute-done | bytes 262176 | tf_op jit(solution)/shard_map/two_behind_2/ppermute | solution.py:30
  37.1 4.7 %collective-permute-done.11.ahead = bf16[1024,128]{1,0:T(8,128)(2,1)S(1)} collective-permute-done((bf16[1024,128]{1,0:T(8,128)(2,1)S(1)}, bf16[1024,128]{1,0:T(8,128)(2,1)S(1)}, u32[]{:S(2)}, u32[]{:S(2)}) %collective-permute-start.11) | collective-permute-done | bytes 262176 | tf_op jit(solution)/shard_map/two_ahead_2/ppermute | solution.py:30
  41.8 2.7 %collective-permute-start.3 = (bf16[1024,128]{1,0:T(8,128)(2,1)S(1)}, bf16[1024,128]{1,0:T(8,128)(2,1)S(1)}, u32[]{:S(2)}, u32[]{:S(2)}) collective-permute-start(bf16[1024,128]{1,0:T(8,128)(2,1)S(1)} %get-tuple-element.39.mine), channel_id=1, source_target_pairs={{0,12},{2,14},{4,0},{6,2},{8,4},{10,6},{12,8},{14,10},{1,13},{3,15... | collective-permute-start | bytes 786440 | tf_op jit(solution)/shard_map/two_ahead_3/ppermute | solution.py:30
  44.5 1.3 %shard_map.34 = (bf16[1024,128]{1,0:T(8,128)(2,1)S(1)}, bf16[1024,128]{1,0:T(8,128)(2,1)S(1)}) custom-call(s32[2,1]{1,0:T(2,128)S(1)} %copy.13.direction, s32[1]{0:T(128)} %collective-permute-done.1.of_pair, bf16[1024,128]{1,0:T(8,128)(2,1)S(1)} %get-tuple-element.51.mine, bf16[1024,128]{1,0:T(8,128)(2,1)S(1)} %collective-permute-done.10.behind, ...), custom_call_target="tpu_custom_call" | custom-call | tf_op jit(solution)/shard_map/pallas_call | solution.py:277
  45.7 0.0 collective-permute-done.17.refs_5_
  45.7 0.1 collective-permute-start.19
  45.8 1.6 %collective-permute-start.12 = (bf16[1024,128]{1,0:T(8,128)(2,1)S(1)}, bf16[1024,128]{1,0:T(8,128)(2,1)S(1)}, u32[]{:S(2)}, u32[]{:S(2)}) collective-permute-start(bf16[1024,128]{1,0:T(8,128)(2,1)S(1)} %get-tuple-element.52), channel_id=1, source_target_pairs={{0,2},{2,0},{4,6},{6,4},{8,10},{10,8},{12,14},{14,12},{1,3},{3,1},... | collective-permute-start | bytes 786440 | tf_op jit(solution)/shard_map/near_2/ppermute | solution.py:35
  47.4 0.0 collective-permute-done.7.refs_6_
  47.4 0.2 collective-permute-start.18
  47.6 4.2 %shard_map.32.rest_0_.refs_9_ = f32[2,32,128,128]{3,2,1,0:T(8,128)S(1)} custom-call(bf16[64,512]{1,0:T(8,128)(2,1)S(1)} %copy.18.rest_1_.refs_0_, f32[128,1024]{1,0:T(8,128)S(1)} %get-tuple-element.40.rest_0_.refs_1_, f32[128,1024]{1,0:T(8,128)S(1)} %get-tuple-element.41.refs_2_, f32[128,1024]{1,0:T(8,128)S(1)} %get-tuple-element.42.refs_3_, ...), custom_call_target="tpu_custom_call" | custom-call | flops 3000000000 | tf_op jit(solution)/shard_map/pallas_call | solution.py:184
  51.8 0.4 collective-permute-start.14
  52.2 2.3 %collective-permute-done.12.refs_5_ = bf16[1024,128]{1,0:T(8,128)(2,1)S(1)} collective-permute-done((bf16[1024,128]{1,0:T(8,128)(2,1)S(1)}, bf16[1024,128]{1,0:T(8,128)(2,1)S(1)}, u32[]{:S(2)}, u32[]{:S(2)}) %collective-permute-start.12) | collective-permute-done | bytes 262176 | tf_op jit(solution)/shard_map/near_2/ppermute | solution.py:35
  54.6 1.4 %shard_map.33 = (bf16[1024,128]{1,0:T(8,128)(2,1)S(1)}, bf16[1024,128]{1,0:T(8,128)(2,1)S(1)}) custom-call(s32[2,1]{1,0:T(2,128)S(1)} %copy.13.direction, s32[1]{0:T(128)} %collective-permute-done.1.of_pair, bf16[1024,128]{1,0:T(8,128)(2,1)S(1)} %get-tuple-element.39.mine, bf16[1024,128]{1,0:T(8,128)(2,1)S(1)} %collective-permute-done.2.behind, ...), custom_call_target="tpu_custom_call" | custom-call | tf_op jit(solution)/shard_map/pallas_call | solution.py:277
  56.0 1.6 %collective-permute-start.9 = (bf16[1024,128]{1,0:T(8,128)(2,1)S(1)}, bf16[1024,128]{1,0:T(8,128)(2,1)S(1)}, u32[]{:S(2)}, u32[]{:S(2)}) collective-permute-start(bf16[1024,128]{1,0:T(8,128)(2,1)S(1)} %get-tuple-element.46), channel_id=1, source_target_pairs={{0,2},{2,0},{4,6},{6,4},{8,10},{10,8},{12,14},{14,12},{1,3},{3,1},... | collective-permute-start | bytes 786440 | tf_op jit(solution)/shard_map/near_3/ppermute | solution.py:35
  57.6 0.0 collective-permute-done.19.refs_8_
  57.6 0.2 collective-permute-start.21
  57.8 4.6 %shard_map.36.refs_9_ = f32[2,32,128,128]{3,2,1,0:T(8,128)S(1)} custom-call(bf16[64,512]{1,0:T(8,128)(2,1)S(1)} %copy.18.rest_1_.refs_0_, f32[128,1024]{1,0:T(8,128)S(1)} %get-tuple-element.54.refs_1_, f32[128,1024]{1,0:T(8,128)S(1)} %get-tuple-element.55.refs_2_, f32[128,1024]{1,0:T(8,128)S(1)} %get-tuple-element.56.refs_3_, ...), custom_call_target="tpu_custom_call", output_to_operand_aliasing={{}: (9, {})} | custom-call | flops 3000000000 | tf_op jit(solution)/shard_map/pallas_call | solution.py:184
  62.4 0.0 collective-permute-done.13.refs_6_
  62.4 4.5 %shard_map.37.refs_9_ = f32[2,32,128,128]{3,2,1,0:T(8,128)S(1)} custom-call(bf16[64,512]{1,0:T(8,128)(2,1)S(1)} %copy.18.rest_1_.refs_0_, f32[128,1024]{1,0:T(8,128)S(1)} %get-tuple-element.47.refs_1_, f32[128,1024]{1,0:T(8,128)S(1)} %get-tuple-element.48.refs_2_, f32[128,1024]{1,0:T(8,128)S(1)} %get-tuple-element.49.refs_3_, ...), custom_call_target="tpu_custom_call", output_to_operand_aliasing={{}: (9, {})} | custom-call | flops 3000000000 | tf_op jit(solution)/shard_map/pallas_call | solution.py:184
  67.0 0.3 collective-permute-start.20
  67.3 1.3 %collective-permute-done.20.refs_6_ = bf16[1024,128]{1,0:T(8,128)(2,1)S(1)} collective-permute-done((bf16[1024,128]{1,0:T(8,128)(2,1)S(1)}, bf16[1024,128]{1,0:T(8,128)(2,1)S(1)}, u32[]{:S(2)}, u32[]{:S(2)}) %collective-permute-start.20) | collective-permute-done | bytes 262176 | tf_op jit(solution)/shard_map/near_other_half_3/ppermute | solution.py:30
  68.6 5.3 %shard_map.38 = f32[2,32,128,128]{3,2,1,0:T(8,128)} custom-call(bf16[64,512]{1,0:T(8,128)(2,1)S(1)} %copy.18.rest_1_.refs_0_, f32[128,1024]{1,0:T(8,128)S(1)} %get-tuple-element.35.refs_1_, f32[128,1024]{1,0:T(8,128)S(1)} %get-tuple-element.36.refs_2_, f32[128,1024]{1,0:T(8,128)S(1)} %get-tuple-element.37.refs_3_, ...), custom_call_target="tpu_custom_call" | custom-call | flops 3000000000 | tf_op jit(solution)/shard_map/pallas_call | solution.py:184
  (15 shorter events, 0.0 us)
Async XLA Ops:
  0.0 1.2 %copy-start = (bf16[8,2,256,128]{3,2,1,0:T(8,128)(2,1)S(1)}, bf16[8,2,256,128]{3,2,1,0:T(8,128)(2,1)}, u32[]{:S(2)}) copy-start(bf16[8,2,256,128]{3,2,1,0:T(8,128)(2,1)} %x.3) | copy-start | bytes 3145732
  2.2 12.1 %collective-permute-start = (bf16[4096,128]{1,0:T(8,128)(2,1)S(1)}, bf16[4096,128]{1,0:T(8,128)(2,1)S(1)}, u32[]{:S(2)}, u32[]{:S(2)}) collective-permute-start(bf16[4096,128]{1,0:T(8,128)(2,1)S(1)} %get-tuple-element.34.own), channel_id=1, source_target_pairs={{0,1},{1,0},{2,3},{3,2},{4,5},{5,4},{6,7},{7,6},{8,9},{9,8},{10,11... | collective-permute-start | bytes 3145736 | tf_op jit(solution)/shard_map/my_other_half/ppermute | solution.py:30
  2.7 15.4 %collective-permute-start.4 = (bf16[1024,128]{1,0:T(8,128)(2,1)S(1)}, bf16[1024,128]{1,0:T(8,128)(2,1)}, u32[]{:S(2)}, u32[]{:S(2)}) collective-permute-start(bf16[1024,128]{1,0:T(8,128)(2,1)S(1)} %shard_map.28.outs_0_.mine), channel_id=1, source_target_pairs={{0,4},{2,6},{4,8},{6,10},{8,12},{10,14},{12,0},{14,2},{1,5},{3,7},... | collective-permute-start | bytes 786440 | tf_op jit(solution)/shard_map/two_behind_0/ppermute | solution.py:30
  5.3 15.0 %collective-permute-start.5 = (bf16[1024,128]{1,0:T(8,128)(2,1)S(1)}, bf16[1024,128]{1,0:T(8,128)(2,1)}, u32[]{:S(2)}, u32[]{:S(2)}) collective-permute-start(bf16[1024,128]{1,0:T(8,128)(2,1)S(1)} %shard_map.28.outs_0_.mine), channel_id=1, source_target_pairs={{0,12},{2,14},{4,0},{6,2},{8,4},{10,6},{12,8},{14,10},{1,13},{3,15... | collective-permute-start | bytes 786440 | tf_op jit(solution)/shard_map/two_ahead_0/ppermute | solution.py:30
  7.4 20.6 %collective-permute-start.15 = (bf16[1024,128]{1,0:T(8,128)(2,1)S(1)}, bf16[1024,128]{1,0:T(8,128)(2,1)S(1)}, u32[]{:S(2)}, u32[]{:S(2)}) collective-permute-start(bf16[1024,128]{1,0:T(8,128)(2,1)S(1)} %get-tuple-element.58.mine), channel_id=1, source_target_pairs={{0,4},{2,6},{4,8},{6,10},{8,12},{10,14},{12,0},{14,2},{1,5},{3,7},... | collective-permute-start | bytes 786440 | tf_op jit(solution)/shard_map/two_behind_1/ppermute | solution.py:30
  7.4 24.1 %collective-permute-start.16 = (bf16[1024,128]{1,0:T(8,128)(2,1)S(1)}, bf16[1024,128]{1,0:T(8,128)(2,1)}, u32[]{:S(2)}, u32[]{:S(2)}) collective-permute-start(bf16[1024,128]{1,0:T(8,128)(2,1)S(1)} %get-tuple-element.58.mine), channel_id=1, source_target_pairs={{0,12},{2,14},{4,0},{6,2},{8,4},{10,6},{12,8},{14,10},{1,13},{3,15... | collective-permute-start | bytes 786440 | tf_op jit(solution)/shard_map/two_ahead_1/ppermute | solution.py:30
  14.3 3.8 %collective-permute-start.1 = (s32[1]{0:T(128)}, s32[1]{0:T(128)}, u32[]{:S(2)}, u32[]{:S(2)}) collective-permute-start(s32[1]{0:T(128)} %bitcast.9), channel_id=1, source_target_pairs={{0,2},{2,0},{4,6},{6,4},{8,10},{10,8},{12,14},{14,12},{1,3},{3,1},... | collective-permute-start | bytes 20 | tf_op jit(solution)/shard_map/direction_of_pair/ppermute | solution.py:35
  22.4 12.0 %collective-permute-start.6 = (bf16[1024,128]{1,0:T(8,128)(2,1)S(1)}, bf16[1024,128]{1,0:T(8,128)(2,1)S(1)}, u32[]{:S(2)}, u32[]{:S(2)}) collective-permute-start(bf16[1024,128]{1,0:T(8,128)(2,1)S(1)} %get-tuple-element.44), channel_id=1, source_target_pairs={{0,2},{2,0},{4,6},{6,4},{8,10},{10,8},{12,14},{14,12},{1,3},{3,1},... | collective-permute-start | bytes 786440 | tf_op jit(solution)/shard_map/near_0/ppermute | solution.py:35
  24.2 12.9 %collective-permute-start.10 = (bf16[1024,128]{1,0:T(8,128)(2,1)S(1)}, bf16[1024,128]{1,0:T(8,128)(2,1)S(1)}, u32[]{:S(2)}, u32[]{:S(2)}) collective-permute-start(bf16[1024,128]{1,0:T(8,128)(2,1)S(1)} %get-tuple-element.51.mine), channel_id=1, source_target_pairs={{0,4},{2,6},{4,8},{6,10},{8,12},{10,14},{12,0},{14,2},{1,5},{3,7},... | collective-permute-start | bytes 786440 | tf_op jit(solution)/shard_map/two_behind_2/ppermute | solution.py:30
  24.8 17.0 %collective-permute-start.11 = (bf16[1024,128]{1,0:T(8,128)(2,1)S(1)}, bf16[1024,128]{1,0:T(8,128)(2,1)S(1)}, u32[]{:S(2)}, u32[]{:S(2)}) collective-permute-start(bf16[1024,128]{1,0:T(8,128)(2,1)S(1)} %get-tuple-element.51.mine), channel_id=1, source_target_pairs={{0,12},{2,14},{4,0},{6,2},{8,4},{10,6},{12,8},{14,10},{1,13},{3,15... | collective-permute-start | bytes 786440 | tf_op jit(solution)/shard_map/two_ahead_2/ppermute | solution.py:30
  32.8 13.0 %collective-permute-start.17 = (bf16[1024,128]{1,0:T(8,128)(2,1)S(1)}, bf16[1024,128]{1,0:T(8,128)(2,1)S(1)}, u32[]{:S(2)}, u32[]{:S(2)}) collective-permute-start(bf16[1024,128]{1,0:T(8,128)(2,1)S(1)} %get-tuple-element.59), channel_id=1, source_target_pairs={{0,2},{2,0},{4,6},{6,4},{8,10},{10,8},{12,14},{14,12},{1,3},{3,1},... | collective-permute-start | bytes 786440 | tf_op jit(solution)/shard_map/near_1/ppermute | solution.py:35
  34.5 11.3 %collective-permute-start.8 = (bf16[1024,128]{1,0:T(8,128)(2,1)S(1)}, bf16[1024,128]{1,0:T(8,128)(2,1)S(1)}, u32[]{:S(2)}, u32[]{:S(2)}) collective-permute-start(bf16[1024,128]{1,0:T(8,128)(2,1)S(1)} %get-tuple-element.45.refs_7_), channel_id=1, source_target_pairs={{0,1},{1,0},{2,3},{3,2},{4,5},{5,4},{6,7},{7,6},{8,9},{9,8},{10,11... | collective-permute-start | bytes 786440 | tf_op jit(solution)/shard_map/far_other_half_0/ppermute | solution.py:30
  34.5 12.9 %collective-permute-start.7 = (bf16[1024,128]{1,0:T(8,128)(2,1)S(1)}, bf16[1024,128]{1,0:T(8,128)(2,1)S(1)}, u32[]{:S(2)}, u32[]{:S(2)}) collective-permute-start(bf16[1024,128]{1,0:T(8,128)(2,1)S(1)} %collective-permute-done.6.refs_5_), channel_id=1, source_target_pairs={{0,1},{1,0},{2,3},{3,2},{4,5},{5,4},{6,7},{7,6},{8,9},{9,8},{10,11... | collective-permute-start | bytes 786440 | tf_op jit(solution)/shard_map/near_other_half_0/ppermute | solution.py:30
  37.1 14.7 %collective-permute-start.2 = (bf16[1024,128]{1,0:T(8,128)(2,1)S(1)}, bf16[1024,128]{1,0:T(8,128)(2,1)S(1)}, u32[]{:S(2)}, u32[]{:S(2)}) collective-permute-start(bf16[1024,128]{1,0:T(8,128)(2,1)S(1)} %get-tuple-element.39.mine), channel_id=1, source_target_pairs={{0,4},{2,6},{4,8},{6,10},{8,12},{10,14},{12,0},{14,2},{1,5},{3,7},... | collective-permute-start | bytes 786440 | tf_op jit(solution)/shard_map/two_behind_3/ppermute | solution.py:30
  41.8 12.8 %collective-permute-start.3 = (bf16[1024,128]{1,0:T(8,128)(2,1)S(1)}, bf16[1024,128]{1,0:T(8,128)(2,1)S(1)}, u32[]{:S(2)}, u32[]{:S(2)}) collective-permute-start(bf16[1024,128]{1,0:T(8,128)(2,1)S(1)} %get-tuple-element.39.mine), channel_id=1, source_target_pairs={{0,12},{2,14},{4,0},{6,2},{8,4},{10,6},{12,8},{14,10},{1,13},{3,15... | collective-permute-start | bytes 786440 | tf_op jit(solution)/shard_map/two_ahead_3/ppermute | solution.py:30
  45.7 11.8 %collective-permute-start.19 = (bf16[1024,128]{1,0:T(8,128)(2,1)S(1)}, bf16[1024,128]{1,0:T(8,128)(2,1)S(1)}, u32[]{:S(2)}, u32[]{:S(2)}) collective-permute-start(bf16[1024,128]{1,0:T(8,128)(2,1)S(1)} %get-tuple-element.60.refs_7_), channel_id=1, source_target_pairs={{0,1},{1,0},{2,3},{3,2},{4,5},{5,4},{6,7},{7,6},{8,9},{9,8},{10,11... | collective-permute-start | bytes 786440 | tf_op jit(solution)/shard_map/far_other_half_1/ppermute | solution.py:30
  45.8 8.7 %collective-permute-start.12 = (bf16[1024,128]{1,0:T(8,128)(2,1)S(1)}, bf16[1024,128]{1,0:T(8,128)(2,1)S(1)}, u32[]{:S(2)}, u32[]{:S(2)}) collective-permute-start(bf16[1024,128]{1,0:T(8,128)(2,1)S(1)} %get-tuple-element.52), channel_id=1, source_target_pairs={{0,2},{2,0},{4,6},{6,4},{8,10},{10,8},{12,14},{14,12},{1,3},{3,1},... | collective-permute-start | bytes 786440 | tf_op jit(solution)/shard_map/near_2/ppermute | solution.py:35
  47.4 10.4 %collective-permute-start.18 = (bf16[1024,128]{1,0:T(8,128)(2,1)S(1)}, bf16[1024,128]{1,0:T(8,128)(2,1)S(1)}, u32[]{:S(2)}, u32[]{:S(2)}) collective-permute-start(bf16[1024,128]{1,0:T(8,128)(2,1)S(1)} %collective-permute-done.17.refs_5_), channel_id=1, source_target_pairs={{0,1},{1,0},{2,3},{3,2},{4,5},{5,4},{6,7},{7,6},{8,9},{9,8},{10,11... | collective-permute-start | bytes 786440 | tf_op jit(solution)/shard_map/near_other_half_1/ppermute | solution.py:30
  51.8 10.6 %collective-permute-start.14 = (bf16[1024,128]{1,0:T(8,128)(2,1)S(1)}, bf16[1024,128]{1,0:T(8,128)(2,1)S(1)}, u32[]{:S(2)}, u32[]{:S(2)}) collective-permute-start(bf16[1024,128]{1,0:T(8,128)(2,1)S(1)} %get-tuple-element.53.refs_7_), channel_id=1, source_target_pairs={{0,1},{1,0},{2,3},{3,2},{4,5},{5,4},{6,7},{7,6},{8,9},{9,8},{10,11... | collective-permute-start | bytes 786440 | tf_op jit(solution)/shard_map/far_other_half_2/ppermute | solution.py:30
  54.5 7.9 %collective-permute-start.13 = (bf16[1024,128]{1,0:T(8,128)(2,1)S(1)}, bf16[1024,128]{1,0:T(8,128)(2,1)S(1)}, u32[]{:S(2)}, u32[]{:S(2)}) collective-permute-start(bf16[1024,128]{1,0:T(8,128)(2,1)S(1)} %collective-permute-done.12.refs_5_), channel_id=1, source_target_pairs={{0,1},{1,0},{2,3},{3,2},{4,5},{5,4},{6,7},{7,6},{8,9},{9,8},{10,11... | collective-permute-start | bytes 786440 | tf_op jit(solution)/shard_map/near_other_half_2/ppermute | solution.py:30
  56.0 11.0 %collective-permute-start.9 = (bf16[1024,128]{1,0:T(8,128)(2,1)S(1)}, bf16[1024,128]{1,0:T(8,128)(2,1)S(1)}, u32[]{:S(2)}, u32[]{:S(2)}) collective-permute-start(bf16[1024,128]{1,0:T(8,128)(2,1)S(1)} %get-tuple-element.46), channel_id=1, source_target_pairs={{0,2},{2,0},{4,6},{6,4},{8,10},{10,8},{12,14},{14,12},{1,3},{3,1},... | collective-permute-start | bytes 786440 | tf_op jit(solution)/shard_map/near_3/ppermute | solution.py:35
  57.6 9.7 %collective-permute-start.21 = (bf16[1024,128]{1,0:T(8,128)(2,1)S(1)}, bf16[1024,128]{1,0:T(8,128)(2,1)S(1)}, u32[]{:S(2)}, u32[]{:S(2)}) collective-permute-start(bf16[1024,128]{1,0:T(8,128)(2,1)S(1)} %get-tuple-element.62.refs_7_), channel_id=1, source_target_pairs={{0,1},{1,0},{2,3},{3,2},{4,5},{5,4},{6,7},{7,6},{8,9},{9,8},{10,11... | collective-permute-start | bytes 786440 | tf_op jit(solution)/shard_map/far_other_half_3/ppermute | solution.py:30
  67.0 1.6 %collective-permute-start.20 = (bf16[1024,128]{1,0:T(8,128)(2,1)S(1)}, bf16[1024,128]{1,0:T(8,128)(2,1)S(1)}, u32[]{:S(2)}, u32[]{:S(2)}) collective-permute-start(bf16[1024,128]{1,0:T(8,128)(2,1)S(1)} %collective-permute-done.9.refs_5_), channel_id=1, source_target_pairs={{0,1},{1,0},{2,3},{3,2},{4,5},{5,4},{6,7},{7,6},{8,9},{9,8},{10,11... | collective-permute-start | bytes 786440 | tf_op jit(solution)/shard_map/near_other_half_3/ppermute | solution.py:30

commit v4 on v3

--- a/solution.py
+++ b/solution.py
@@ -17,11 +17,9 @@
 VMEM = 20 * 2**20
 AFTER = {3: 0}
 GATE = {3: 2}
-NEAR_GATE = {}
-SPLIT = False
-EXPAND = {}
-GATE_FAR = False
-LAG_FLOPS = 3e9
+LATE = {1: 2, 2: 3}
+LAG_FLOPS = 6e9
+RUNS = ((0,), (1, 2), (3,))
 COST = pl.CostEstimate(flops=0, bytes_accessed=0, transcendentals=0)
 
 
@@ -65,87 +63,64 @@
     return jnp.concatenate(pieces, axis=0)
 
 
-def left_sides_kernel(*refs):
-    local, out = refs[:4], refs[4]
-    channels, depth = local[0].shape
-    rows = CHANNEL_BLOCK
-    tile = GROUP * 16
-
-    @pl.loop(0, channels // rows)
-    def _(b):
-        start = pl.multiple_of(b * rows, rows)
-        for g in range(depth // tile):
-            at = pl.ds(pl.multiple_of(b * rows * 16, rows * 16), rows * 16)
-            out[g, at, :] = left_side(local, start, rows, slice(g * tile, (g + 1) * tile))
-
-
-def left_sides(local):
-    channels, depth = local[0].shape
-    vmem = pl.BlockSpec(memory_space=pltpu.VMEM)
-    return pl.pallas_call(
-        left_sides_kernel,
-        in_specs=[vmem] * len(local),
-        out_specs=vmem,
-        out_shape=pltpu.VMEM((depth // (GROUP * 16), channels * 2 * GROUP, 2 * GROUP * 16), jnp.bfloat16),
-        compiler_params=pltpu.CompilerParams(vmem_limit_bytes=VMEM),
-        cost_estimate=COST,
-    )(*local)
-
-
-def lag_kernel(*refs, first, rounds, local_count, has_total, last):
-    table, local, refs = refs[0], refs[1 : 1 + local_count], refs[1 + local_count :]
-    partners, refs = refs[: 2 * len(rounds)], refs[2 * len(rounds) :]
-    depth = partners[0].shape[0]
+def lag_kernel(*refs, first, runs, has_total, last):
+    table, refs = refs[0], refs[1:]
+    locals_, refs = [refs[4 * n : 4 * n + 4] for n in range(runs)], refs[4 * runs :]
+    partners, refs = [refs[4 * n : 4 * n + 4] for n in range(runs)], refs[4 * runs :]
+    depths = [x[0].shape[0] for x in partners]
+    depth = sum(depths)
     total, refs = (refs[0], refs[1:]) if has_total else (None, refs)
     out, cross = refs[:2] if not last else refs[-4:-2]
     rows = CHANNEL_BLOCK
-    width = partners[0].shape[1]
+    width = partners[0][0].shape[1]
     tile = GROUP * 16
     _, lag_count, channels, _ = out.shape
     mine = pl.ds(pl.multiple_of(lax.axis_index("sub") * lag_count, lag_count), lag_count)
     weights = table[mine, 2 * first : 2 * (first + depth // 16)]
     def block(b, slot):
         start = pl.multiple_of(b * rows, rows)
-        for g in range(depth // tile):
-            lanes = slice(g * tile, (g + 1) * tile)
-            if len(local) == 1:
-                left = local[0][g, pl.ds(pl.multiple_of(b * rows * 16, rows * 16), rows * 16), :]
-            else:
-                left = left_side(local, start, rows, lanes)
-            halves = [jnp.concatenate([x[lanes, :] for x in partners[k::2]], axis=1) for k in range(2)]
-            right = jnp.concatenate(halves, axis=0)
-            part = jnp.dot(left, right, preferred_element_type=jnp.float32).astype(jnp.bfloat16)
-            cross[slot, :, g * 2 * GROUP : (g + 1) * 2 * GROUP, :] = part.reshape(rows, 2 * GROUP, part.shape[-1])
+        done = 0
+        for n in range(runs):
+            for g in range(depths[n] // tile):
+                lanes = slice(g * tile, (g + 1) * tile)
+                left = left_side(locals_[n], start, rows, lanes)
+                halves = [jnp.concatenate([x[lanes, :] for x in partners[n][k::2]], axis=1) for k in range(2)]
+                right = jnp.concatenate(halves, axis=0)
+                part = jnp.dot(left, right, preferred_element_type=jnp.float32).astype(jnp.bfloat16)
+                cross[slot, :, done : done + 2 * GROUP, :] = part.reshape(rows, 2 * GROUP, part.shape[-1])
+                done += 2 * GROUP
 
         for low in range(0, rows, 8):
             lagged = [jnp.dot(weights, cross[slot, i], preferred_element_type=jnp.float32) for i in range(low, low + 8)]
             at = pl.ds(pl.multiple_of(start + low, 8), 8)
-            for n, r in enumerate(rounds):
-                stacked = jnp.stack([x[:, n * width : (n + 1) * width] for x in lagged], axis=0)
+            for r in range(ROUNDS):
+                stacked = jnp.stack([x[:, r * width : (r + 1) * width] for x in lagged], axis=0)
                 tile_out = jnp.swapaxes(stacked, 0, 1)
                 if has_total:
                     tile_out = tile_out + total[r, :, at, :]
                 if last:
-                    stage[b, n, :, low : low + 8, :] = tile_out
+                    stage[b, r, :, low : low + 8, :] = tile_out
                 else:
                     out[r, :, at, :] = tile_out
+            if last:
+                store(b, low).start()
 
     if last:
         stage, sems = refs[-2:]
 
-        def store(b):
-            at = pl.ds(pl.multiple_of(b * rows, rows), rows)
-            there = out.at[rounds[0] : rounds[-1] + 1, :, at, :]
-            return pltpu.make_async_copy(stage.at[b], there, sems.at[b])
+        def store(b, low):
+            at = pl.ds(pl.multiple_of(b * rows + low, 8), 8)
+            ready = stage.at[b, :, :, low : low + 8, :]
+            return pltpu.make_async_copy(ready, out.at[:, :, at, :], sems.at[b, low // 8])
 
         @pl.loop(0, channels // rows, step=UNROLL)
         def _(b):
             for n in range(UNROLL):
                 block(b + n, n)
-                store(b + n).start()
 
         for b in range(channels // rows):
-            store(b).wait()
+            for low in range(0, rows, 8):
+                store(b, low).wait()
     else:
 
         @pl.loop(0, channels // rows, step=UNROLL)
@@ -154,44 +129,33 @@
                 block(b + n, n)
 
 
-def add_lags(table, first, local, partners, total, rounds=(0, 1), last=False, result=None):
-    depth, width = partners[0].shape
-    channels = local[0].shape[0] if len(local) > 1 else local[0].shape[1] // (2 * GROUP)
+def add_lags(table, first, locals_, partners, total, last):
+    width = partners[0][0].shape[1]
+    depth = sum(x[0].shape[0] for x in partners)
+    channels = locals_[0][0].shape[0]
     lag_count = table.shape[0] // lax.axis_size("sub")
     block = CHANNEL_BLOCK
     vmem = pl.BlockSpec(memory_space=pltpu.VMEM)
-    hbm = pl.BlockSpec(memory_space=pl.ANY)
-    operands = [table, *local, *partners]
-    in_specs = [vmem] * len(operands)
+    operands = [table, *(x for run in locals_ for x in run), *(x for run in partners for x in run)]
     aliases = {}
     if total is not None:
         if not last:
             aliases = {len(operands): 0}
         operands.append(total)
-        in_specs.append(vmem)
-    if result is not None:
-        aliases = {len(operands): 0}
-        operands.append(result)
-        in_specs.append(hbm)
     shape = (ROUNDS, lag_count, channels, width)
-    scratch = [pltpu.VMEM((UNROLL, block, depth // 8, len(rounds) * width), jnp.bfloat16)]
+    scratch = [pltpu.VMEM((UNROLL, block, depth // 8, ROUNDS * width), jnp.bfloat16)]
     if last:
         blocks = channels // block
-        scratch += [
-            pltpu.VMEM((blocks, len(rounds), lag_count, block, width), jnp.float32),
-            pltpu.SemaphoreType.DMA((blocks,)),
-        ]
+        scratch += [pltpu.VMEM((blocks, ROUNDS, lag_count, block, width), jnp.float32), pltpu.SemaphoreType.DMA((blocks, block // 8))]
     return pl.pallas_call(
-        functools.partial(lag_kernel, first=first, rounds=rounds, local_count=len(local), has_total=total is not None, last=last),
-        in_specs=in_specs,
-        out_specs=hbm if last else vmem,
+        functools.partial(lag_kernel, first=first, runs=len(partners), has_total=total is not None, last=last),
+        in_specs=[vmem] * len(operands),
+        out_specs=pl.BlockSpec(memory_space=pl.ANY) if last else vmem,
         out_shape=jax.ShapeDtypeStruct(shape, jnp.float32) if last else pltpu.VMEM(shape, jnp.float32),
         input_output_aliases=aliases,
         scratch_shapes=scratch,
         compiler_params=pltpu.CompilerParams(vmem_limit_bytes=VMEM),
-        cost_estimate=pl.CostEstimate(
-            flops=int(LAG_FLOPS) * len(rounds) // ROUNDS, bytes_accessed=0, transcendentals=0
-        ),
+        cost_estimate=pl.CostEstimate(flops=int(LAG_FLOPS) * len(partners), bytes_accessed=0, transcendentals=0),
     )(*operands)
 
 
@@ -200,12 +164,13 @@
     for out, size in zip(outs, sizes):
         if size == x.shape[2] and first:
             first = 0
-        for low in range(0, size, 16):
-            at = slice(first + low, first + low + 16)
+        step = 8 if first % 16 or size % 16 else 16
+        for low in range(0, size, step):
+            at = slice(first + low, first + low + step)
             slabs = [x[s, c, at, :].astype(jnp.float32) for c in range(2) for s in range(x.shape[0])]
             turned = jnp.swapaxes(jnp.stack(slabs, axis=0), 0, 1)
-            rows = turned.reshape(16 * len(slabs), x.shape[3]).astype(out.dtype)
-            out[low * len(slabs) : (low + 16) * len(slabs), :] = rows
+            rows = turned.reshape(step * len(slabs), x.shape[3]).astype(out.dtype)
+            out[low * len(slabs) : (low + step) * len(slabs), :] = rows
         first += size
 
 
@@ -304,40 +269,42 @@
         other = ring_shift(whole, "sub", 1)
     local = channels_first(whole, other, [size * whole.shape[0] // bin_count for size in CHUNKS])
 
-    totals = [None]
-    first = 0
-    for n, size in enumerate(CHUNKS):
-        after = [totals[AFTER[n] + 1]] if n in AFTER else []
-        if n == 0:
-            after = [local[0][0], table]
-        if n in EXPAND:
-            m = EXPAND[n]
-            local[m] = [left_sides(local[m])]
-            after = after + local[m]
-        far_own, passed_on = choose(direction, of_pair, mine[n], behind[n], ahead[n], after)
-        if n in NEAR_GATE:
-            passed_on, _ = lax.optimization_barrier((passed_on, totals[NEAR_GATE[n] + 1]))
+    @functools.cache
+    def chosen(n):
+        after = [local[0][0], table] if n == 0 else []
+        if n in AFTER:
+            after = [total_after(AFTER[n])]
+        return choose(direction, of_pair, mine[n], behind[n], ahead[n], after)
+
+    @functools.cache
+    def near(n):
         with jax.named_scope(f"near_{n}"):
-            near_own = pair_swap(passed_on, "blk")
+            return pair_swap(chosen(n)[1], "blk")
+
+    @functools.cache
+    def partners(n):
+        far_own, near_own = chosen(n)[0], near(n)
         with jax.named_scope(f"far_other_half_{n}"):
             far_other = ring_shift(far_own, "sub", 1)
-        ends = n == len(CHUNKS) - 1
-        far_total = None
-        if ends and SPLIT:
-            far_total = add_lags(table, first, local[n], [far_own, far_other], totals[-1], (1,), True)
         if n in GATE:
-            done = far_total if ends and SPLIT and GATE_FAR else totals[GATE[n] + 1]
-            near_own, _ = lax.optimization_barrier((near_own, done))
+            near_own, _ = lax.optimization_barrier((near_own, total_after(GATE[n])))
+        if n in LATE:
+            near_own, _ = lax.optimization_barrier((near_own, chosen(LATE[n])[1]))
         with jax.named_scope(f"near_other_half_{n}"):
             near_other = ring_shift(near_own, "sub", 1)
-        if ends and SPLIT:
-            total = add_lags(table, first, local[n], [near_own, near_other], totals[-1], (0,), True, far_total)
-        else:
-            partners = [near_own, near_other, far_own, far_other]
-            total = add_lags(table, first, local[n], partners, totals[-1], last=ends)
-        totals.append(total)
-        first += size
-    return totals[-1][:, None]
+        return [near_own, near_other, far_own, far_other]
+
+    @functools.cache
+    def total_after(n):
+        at = next(k for k, run in enumerate(RUNS) if n in run)
+        run = RUNS[at]
+        total = total_after(RUNS[at - 1][-1]) if at else None
+        first, last = sum(CHUNKS[: run[0]]), at == len(RUNS) - 1
+        return add_lags(table, first, [local[m] for m in run], [partners(m) for m in run], total, last)
+
+    for n in range(len(CHUNKS)):
+        result = total_after(n)
+    return result[:, None]
 
 
 def solution(mesh):

time: 74.3 us -> 72.7 us (0.978)
  waiting for transfers between devices: 16.5 us -> 14.4 us
    ppermute x5, waiting for transfers between devices: 2.73 us -> 0.54 us  [pair_swap(): return lax.ppermute(x, axis, [(i, i ^ 1) for i in range(size)])]
    pallas_call x4, Pallas kernels: 6.07 us -> 7.03 us  [choose(): pl.pallas_call(choose_kernel, in_specs=[smem, smem] + [hbm] * (3 + len(af...]
    pallas_call x4 -> x3, Pallas kernels: 18.6 us -> 17.7 us  [add_lags(): pl.pallas_call(functools.partial(lag_kernel, first=first, runs=len(partne...]
    ppermute x17, starting transfers between devices: 17.3 us -> 18.1 us  [ring_shift(): return lax.ppermute(x, axis, [(i, (i + by) % size) for i in range(size)])]
where the time goes in v4:
time: 72.7 us; the launch traced here: 72.5 us
  Pallas kernels  27.4 us (38%)
  starting transfers between devices  26.1 us (36%)
  waiting for transfers between devices  14.4 us (20%)
  local copies, waits for them, and re-layouts  2.95 us (4%)
  other arithmetic  1.29 us (2%)
    ppermute x17, starting transfers between devices, ring_shift(): return lax.ppermute(x, axis, [(i, (i + by) % size) for i in range(size)])  18.1 us
    pallas_call x3, Pallas kernels, add_lags(): pl.pallas_call(functools.partial(lag_kernel, first=first, runs=len(partne...  17.7 us
    ppermute x17, waiting for transfers between devices, ring_shift(): return lax.ppermute(x, axis, [(i, (i + by) % size) for i in range(size)])  13.9 us
    ppermute x5, starting transfers between devices, pair_swap(): return lax.ppermute(x, axis, [(i, i ^ 1) for i in range(size)])  7.99 us
    pallas_call x4, Pallas kernels, choose(): pl.pallas_call(choose_kernel, in_specs=[smem, smem] + [hbm] * (3 + len(af...  7.03 us
    unnamed x3, local copies, waits for them, and re-layouts  1.97 us
    pallas_call x1, Pallas kernels, channels_first(): pl.pallas_call(channels_first_kernel, out_shape=[pltpu.VMEM((own.shape[1]...  1.72 us
  transfers between devices with their start and end apart: 22, of which 7 were waited for; matrix products, arithmetic and copies ran while one was open for 4% of the time, Pallas kernels for 29%

profile of v4, /device:TPU:0, one launch (start us, length us, event | category | flops | bytes accessed | tf_op | source)
XLA Modules:
  0.0 72.5 jit_solution(13937271547540955506)
XLA Ops:
  0.0 1.2 %copy-done = bf16[8,2,256,128]{3,2,1,0:T(8,128)(2,1)S(1)} copy-done((bf16[8,2,256,128]{3,2,1,0:T(8,128)(2,1)S(1)}, bf16[8,2,256,128]{3,2,1,0:T(8,128)(2,1)}, u32[]{:S(2)}) %copy-start) | copy-done | bytes 1048600
  1.2 0.1 shard_map.28.outs_0_.mine
  1.4 0.8 %shard_map.29 = (bf16[1024,128]{1,0:T(8,128)(2,1)S(1)}, bf16[1024,128]{1,0:T(8,128)(2,1)S(1)}, bf16[1024,128]{1,0:T(8,128)(2,1)S(1)}, bf16[4096,128]{1,0:T(8,128)(2,1)S(1)}) custom-call(bf16[8,2,256,128]{3,2,1,0:T(8,128)(2,1)S(1)} %copy-done, bf16[1024,128]{1,0:T(8,128)(2,1)S(1)} %shard_map.28.outs_0_.mine), custom_call_target="tpu_custom_call" | custom-call | tf_op jit(solution)/shard_map/pallas_call | solution.py:180
  2.2 0.5 collective-permute-start
  2.7 4.7 %collective-permute-start.5 = (bf16[1024,128]{1,0:T(8,128)(2,1)S(1)}, bf16[1024,128]{1,0:T(8,128)(2,1)}, u32[]{:S(2)}, u32[]{:S(2)}) collective-permute-start(bf16[1024,128]{1,0:T(8,128)(2,1)S(1)} %shard_map.28.outs_0_.mine), channel_id=1, source_target_pairs={{0,12},{2,14},{4,0},{6,2},{8,4},{10,6},{12,8},{14,10},{1,13},{3,15... | collective-permute-start | bytes 786440 | tf_op jit(solution)/shard_map/two_ahead_0/ppermute | solution.py:28
  7.3 0.0 collective-permute-start.4
  7.3 3.8 %collective-permute-start.11 = (bf16[1024,128]{1,0:T(8,128)(2,1)S(1)}, bf16[1024,128]{1,0:T(8,128)(2,1)S(1)}, u32[]{:S(2)}, u32[]{:S(2)}) collective-permute-start(bf16[1024,128]{1,0:T(8,128)(2,1)S(1)} %get-tuple-element.57.mine), channel_id=1, source_target_pairs={{0,12},{2,14},{4,0},{6,2},{8,4},{10,6},{12,8},{14,10},{1,13},{3,15... | collective-permute-start | bytes 786440 | tf_op jit(solution)/shard_map/two_ahead_1/ppermute | solution.py:28
  11.2 0.0 collective-permute-start.10
  11.2 0.7 %copy.12.direction = s32[2,1]{1,0:T(2,128)S(1)} copy(s32[2,1]{0,1:T(1,128)} %param.3) | data formatting | bytes 16 | tf_op args[1]
  11.9 0.6 fusion.4
  12.5 0.7 fusion
  13.2 1.0 %copy.16.rest_1_.refs_0_ = bf16[64,512]{1,0:T(8,128)(2,1)S(1)} copy(bf16[64,512]{0,1:T(8,128)(2,1)} %bitcast.8) | data formatting | bytes 131072 | tf_op jit(solution)/shard_map/reshape | solution.py:45
  14.2 1.6 %collective-permute-start.1 = (s32[1]{0:T(128)}, s32[1]{0:T(128)}, u32[]{:S(2)}, u32[]{:S(2)}) collective-permute-start(s32[1]{0:T(128)} %bitcast.9), channel_id=1, source_target_pairs={{0,2},{2,0},{4,6},{6,4},{8,10},{10,8},{12,14},{14,12},{1,3},{3,1},... | collective-permute-start | bytes 20 | tf_op jit(solution)/shard_map/direction_of_pair/ppermute | solution.py:33
  15.8 1.7 %shard_map.30 = (f32[128,1024]{1,0:T(8,128)S(1)}, f32[128,1024]{1,0:T(8,128)S(1)}, f32[128,1024]{1,0:T(8,128)S(1)}, f32[128,1024]{1,0:T(8,128)S(1)}, f32[128,102...) custom-call(bf16[4096,128]{1,0:T(8,128)(2,1)S(1)} %get-tuple-element, ...), custom_call_target="tpu_custom_call" | custom-call | tf_op jit(solution)/shard_map/pallas_call | solution.py:209
  17.5 0.5 collective-permute-done.1.of_pair
  18.1 2.6 %collective-permute-done.4.behind = bf16[1024,128]{1,0:T(8,128)(2,1)} collective-permute-done((bf16[1024,128]{1,0:T(8,128)(2,1)S(1)}, bf16[1024,128]{1,0:T(8,128)(2,1)}, u32[]{:S(2)}, u32[]{:S(2)}) %collective-permute-start.4) | collective-permute-done | bytes 262176 | tf_op jit(solution)/shard_map/two_behind_0/ppermute | solution.py:28
  20.6 2.2 %shard_map.31 = (bf16[1024,128]{1,0:T(8,128)(2,1)S(1)}, bf16[1024,128]{1,0:T(8,128)(2,1)S(1)}) custom-call(s32[2,1]{1,0:T(2,128)S(1)} %copy.12.direction, s32[1]{0:T(128)} %collective-permute-done.1.of_pair, bf16[1024,128]{1,0:T(8,128)(2,1)S(1)} %shard_map.28.outs_0_.mine, bf16[1024,128]{1,0:T(8,128)(2,1)} %collective-permute-done.4.behind, ...), custom_call_target="tpu_custom_call" | custom-call | tf_op jit(solution)/shard_map/pallas_call | solution.py:242
  22.8 1.6 %collective-permute-start.6 = (bf16[1024,128]{1,0:T(8,128)(2,1)S(1)}, bf16[1024,128]{1,0:T(8,128)(2,1)S(1)}, u32[]{:S(2)}, u32[]{:S(2)}) collective-permute-start(bf16[1024,128]{1,0:T(8,128)(2,1)S(1)} %get-tuple-element.46), channel_id=1, source_target_pairs={{0,2},{2,0},{4,6},{6,4},{8,10},{10,8},{12,14},{14,12},{1,3},{3,1},... | collective-permute-start | bytes 786440 | tf_op jit(solution)/shard_map/near_0/ppermute | solution.py:33
  24.4 2.0 %collective-permute-start.14 = (bf16[1024,128]{1,0:T(8,128)(2,1)S(1)}, bf16[1024,128]{1,0:T(8,128)(2,1)S(1)}, u32[]{:S(2)}, u32[]{:S(2)}) collective-permute-start(bf16[1024,128]{1,0:T(8,128)(2,1)S(1)} %get-tuple-element.59.mine), channel_id=1, source_target_pairs={{0,12},{2,14},{4,0},{6,2},{8,4},{10,6},{12,8},{14,10},{1,13},{3,15... | collective-permute-start | bytes 786440 | tf_op jit(solution)/shard_map/two_ahead_2/ppermute | solution.py:28
  26.4 0.1 collective-permute-start.13
  26.5 0.0 collective-permute-done.11.ahead
  26.5 5.5 %collective-permute-done.10.behind = bf16[1024,128]{1,0:T(8,128)(2,1)} collective-permute-done((bf16[1024,128]{1,0:T(8,128)(2,1)S(1)}, bf16[1024,128]{1,0:T(8,128)(2,1)}, u32[]{:S(2)}, u32[]{:S(2)}) %collective-permute-start.10) | collective-permute-done | bytes 262176 | tf_op jit(solution)/shard_map/two_behind_1/ppermute | solution.py:28
  31.9 2.1 %shard_map.34 = (bf16[1024,128]{1,0:T(8,128)(2,1)S(1)}, bf16[1024,128]{1,0:T(8,128)(2,1)S(1)}) custom-call(s32[2,1]{1,0:T(2,128)S(1)} %copy.12.direction, s32[1]{0:T(128)} %collective-permute-done.1.of_pair, bf16[1024,128]{1,0:T(8,128)(2,1)S(1)} %get-tuple-element.57.mine, bf16[1024,128]{1,0:T(8,128)(2,1)} %collective-permute-done.10.behind, ...), custom_call_target="tpu_custom_call" | custom-call | tf_op jit(solution)/shard_map/pallas_call | solution.py:242
  34.1 1.6 %collective-permute-start.12 = (bf16[1024,128]{1,0:T(8,128)(2,1)S(1)}, bf16[1024,128]{1,0:T(8,128)(2,1)S(1)}, u32[]{:S(2)}, u32[]{:S(2)}) collective-permute-start(bf16[1024,128]{1,0:T(8,128)(2,1)S(1)} %get-tuple-element.58), channel_id=1, source_target_pairs={{0,2},{2,0},{4,6},{6,4},{8,10},{10,8},{12,14},{14,12},{1,3},{3,1},... | collective-permute-start | bytes 786440 | tf_op jit(solution)/shard_map/near_1/ppermute | solution.py:33
  35.7 0.0 collective-permute-start.8
  35.7 0.0 collective-permute-done.6.refs_5_
  35.7 0.5 collective-permute-start.7
  36.2 0.9 %collective-permute-done.14.ahead = bf16[1024,128]{1,0:T(8,128)(2,1)S(1)} collective-permute-done((bf16[1024,128]{1,0:T(8,128)(2,1)S(1)}, bf16[1024,128]{1,0:T(8,128)(2,1)S(1)}, u32[]{:S(2)}, u32[]{:S(2)}) %collective-permute-start.14) | collective-permute-done | bytes 262176 | tf_op jit(solution)/shard_map/two_ahead_2/ppermute | solution.py:28
  37.1 3.7 %collective-permute-start.3 = (bf16[1024,128]{1,0:T(8,128)(2,1)S(1)}, bf16[1024,128]{1,0:T(8,128)(2,1)S(1)}, u32[]{:S(2)}, u32[]{:S(2)}) collective-permute-start(bf16[1024,128]{1,0:T(8,128)(2,1)S(1)} %get-tuple-element.41.mine), channel_id=1, source_target_pairs={{0,12},{2,14},{4,0},{6,2},{8,4},{10,6},{12,8},{14,10},{1,13},{3,15... | collective-permute-start | bytes 786440 | tf_op jit(solution)/shard_map/two_ahead_3/ppermute | solution.py:28
  40.9 2.2 %collective-permute-done.13.behind = bf16[1024,128]{1,0:T(8,128)(2,1)S(1)} collective-permute-done((bf16[1024,128]{1,0:T(8,128)(2,1)S(1)}, bf16[1024,128]{1,0:T(8,128)(2,1)S(1)}, u32[]{:S(2)}, u32[]{:S(2)}) %collective-permute-start.13) | collective-permute-done | bytes 262176 | tf_op jit(solution)/shard_map/two_behind_2/ppermute | solution.py:28
  43.1 1.6 %collective-permute-start.2 = (bf16[1024,128]{1,0:T(8,128)(2,1)S(1)}, bf16[1024,128]{1,0:T(8,128)(2,1)S(1)}, u32[]{:S(2)}, u32[]{:S(2)}) collective-permute-start(bf16[1024,128]{1,0:T(8,128)(2,1)S(1)} %get-tuple-element.41.mine), channel_id=1, source_target_pairs={{0,4},{2,6},{4,8},{6,10},{8,12},{10,14},{12,0},{14,2},{1,5},{3,7},... | collective-permute-start | bytes 786440 | tf_op jit(solution)/shard_map/two_behind_3/ppermute | solution.py:28
  44.7 1.3 %shard_map.35 = (bf16[1024,128]{1,0:T(8,128)(2,1)S(1)}, bf16[1024,128]{1,0:T(8,128)(2,1)S(1)}) custom-call(s32[2,1]{1,0:T(2,128)S(1)} %copy.12.direction, s32[1]{0:T(128)} %collective-permute-done.1.of_pair, bf16[1024,128]{1,0:T(8,128)(2,1)S(1)} %get-tuple-element.59.mine, bf16[1024,128]{1,0:T(8,128)(2,1)S(1)} %collective-permute-done.13.behind, ...), custom_call_target="tpu_custom_call" | custom-call | tf_op jit(solution)/shard_map/pallas_call | solution.py:242
  45.9 0.0 collective-permute-done.12.refs_9_
  45.9 1.6 %collective-permute-start.17 = (bf16[1024,128]{1,0:T(8,128)(2,1)S(1)}, bf16[1024,128]{1,0:T(8,128)(2,1)S(1)}, u32[]{:S(2)}, u32[]{:S(2)}) collective-permute-start(bf16[1024,128]{1,0:T(8,128)(2,1)S(1)} %get-tuple-element.60), channel_id=1, source_target_pairs={{0,2},{2,0},{4,6},{6,4},{8,10},{10,8},{12,14},{14,12},{1,3},{3,1},... | collective-permute-start | bytes 786440 | tf_op jit(solution)/shard_map/near_2/ppermute | solution.py:33
  47.5 0.5 collective-permute-start.19
  48.0 4.2 %shard_map.32.rest_0_.refs_17_ = f32[2,32,128,128]{3,2,1,0:T(8,128)S(1)} custom-call(bf16[64,512]{1,0:T(8,128)(2,1)S(1)} %copy.16.rest_1_.refs_0_, f32[128,1024]{1,0:T(8,128)S(1)} %get-tuple-element.42.rest_0_.refs_1_, f32[128,1024]{1,0:T(8,128)S(1)} %get-tuple-element.43.refs_2_, f32[128,1024]{1,0:T(8,128)S(1)} %get-tuple-element.44.refs_3_, ...), custom_call_target="tpu_custom_call" | custom-call | flops 6000000000 | tf_op jit(solution)/shard_map/pallas_call | solution.py:150
  52.3 0.1 collective-permute-start.15
  52.4 1.5 %collective-permute-done.2.behind = bf16[1024,128]{1,0:T(8,128)(2,1)S(1)} collective-permute-done((bf16[1024,128]{1,0:T(8,128)(2,1)S(1)}, bf16[1024,128]{1,0:T(8,128)(2,1)S(1)}, u32[]{:S(2)}, u32[]{:S(2)}) %collective-permute-start.2) | collective-permute-done | bytes 262176 | tf_op jit(solution)/shard_map/two_behind_3/ppermute | solution.py:28
  53.9 1.4 %shard_map.33 = (bf16[1024,128]{1,0:T(8,128)(2,1)S(1)}, bf16[1024,128]{1,0:T(8,128)(2,1)S(1)}) custom-call(s32[2,1]{1,0:T(2,128)S(1)} %copy.12.direction, s32[1]{0:T(128)} %collective-permute-done.1.of_pair, bf16[1024,128]{1,0:T(8,128)(2,1)S(1)} %get-tuple-element.41.mine, bf16[1024,128]{1,0:T(8,128)(2,1)S(1)} %collective-permute-done.2.behind, ...), custom_call_target="tpu_custom_call" | custom-call | tf_op jit(solution)/shard_map/pallas_call | solution.py:242
  55.3 0.0 collective-permute-done.17.refs_13_
  55.3 0.1 collective-permute-start.18
  55.4 1.6 %collective-permute-start.9 = (bf16[1024,128]{1,0:T(8,128)(2,1)S(1)}, bf16[1024,128]{1,0:T(8,128)(2,1)S(1)}, u32[]{:S(2)}, u32[]{:S(2)}) collective-permute-start(bf16[1024,128]{1,0:T(8,128)(2,1)S(1)} %get-tuple-element.48), channel_id=1, source_target_pairs={{0,2},{2,0},{4,6},{6,4},{8,10},{10,8},{12,14},{14,12},{1,3},{3,1},... | collective-permute-start | bytes 786440 | tf_op jit(solution)/shard_map/near_3/ppermute | solution.py:33
  57.0 0.0 collective-permute-done.16.refs_12_
  57.0 0.2 collective-permute-start.21
  57.2 8.4 %shard_map.36.refs_9_ = f32[2,32,128,128]{3,2,1,0:T(8,128)S(1)} custom-call(bf16[64,512]{1,0:T(8,128)(2,1)S(1)} %copy.16.rest_1_.refs_0_, f32[128,1024]{1,0:T(8,128)S(1)} %get-tuple-element.49.refs_1_, f32[128,1024]{1,0:T(8,128)S(1)} %get-tuple-element.50.refs_2_, f32[128,1024]{1,0:T(8,128)S(1)} %get-tuple-element.51.refs_3_, ...), custom_call_target="tpu_custom_call", output_to_operand_aliasing={{}: (17, {})} | custom-call | flops 12000000000 | tf_op jit(solution)/shard_map/pallas_call | solution.py:150
  65.6 0.4 collective-permute-start.20
  66.0 1.2 %collective-permute-done.20.refs_6_ = bf16[1024,128]{1,0:T(8,128)(2,1)S(1)} collective-permute-done((bf16[1024,128]{1,0:T(8,128)(2,1)S(1)}, bf16[1024,128]{1,0:T(8,128)(2,1)S(1)}, u32[]{:S(2)}, u32[]{:S(2)}) %collective-permute-start.20) | collective-permute-done | bytes 262176 | tf_op jit(solution)/shard_map/near_other_half_3/ppermute | solution.py:28
  67.2 5.2 %shard_map.37 = f32[2,32,128,128]{3,2,1,0:T(8,128)} custom-call(bf16[64,512]{1,0:T(8,128)(2,1)S(1)} %copy.16.rest_1_.refs_0_, f32[128,1024]{1,0:T(8,128)S(1)} %get-tuple-element.37.refs_1_, f32[128,1024]{1,0:T(8,128)S(1)} %get-tuple-element.38.refs_2_, f32[128,1024]{1,0:T(8,128)S(1)} %get-tuple-element.39.refs_3_, ...), custom_call_target="tpu_custom_call" | custom-call | flops 6000000000 | tf_op jit(solution)/shard_map/pallas_call | solution.py:150
  (14 shorter events, 0.0 us)
Async XLA Ops:
  0.0 1.2 %copy-start = (bf16[8,2,256,128]{3,2,1,0:T(8,128)(2,1)S(1)}, bf16[8,2,256,128]{3,2,1,0:T(8,128)(2,1)}, u32[]{:S(2)}) copy-start(bf16[8,2,256,128]{3,2,1,0:T(8,128)(2,1)} %x.3) | copy-start | bytes 3145732
  2.2 12.0 %collective-permute-start = (bf16[4096,128]{1,0:T(8,128)(2,1)S(1)}, bf16[4096,128]{1,0:T(8,128)(2,1)S(1)}, u32[]{:S(2)}, u32[]{:S(2)}) collective-permute-start(bf16[4096,128]{1,0:T(8,128)(2,1)S(1)} %get-tuple-element.36.own), channel_id=1, source_target_pairs={{0,1},{1,0},{2,3},{3,2},{4,5},{5,4},{6,7},{7,6},{8,9},{9,8},{10,11... | collective-permute-start | bytes 3145736 | tf_op jit(solution)/shard_map/my_other_half/ppermute | solution.py:28
  2.7 15.4 %collective-permute-start.5 = (bf16[1024,128]{1,0:T(8,128)(2,1)S(1)}, bf16[1024,128]{1,0:T(8,128)(2,1)}, u32[]{:S(2)}, u32[]{:S(2)}) collective-permute-start(bf16[1024,128]{1,0:T(8,128)(2,1)S(1)} %shard_map.28.outs_0_.mine), channel_id=1, source_target_pairs={{0,12},{2,14},{4,0},{6,2},{8,4},{10,6},{12,8},{14,10},{1,13},{3,15... | collective-permute-start | bytes 786440 | tf_op jit(solution)/shard_map/two_ahead_0/ppermute | solution.py:28
  7.3 13.3 %collective-permute-start.4 = (bf16[1024,128]{1,0:T(8,128)(2,1)S(1)}, bf16[1024,128]{1,0:T(8,128)(2,1)}, u32[]{:S(2)}, u32[]{:S(2)}) collective-permute-start(bf16[1024,128]{1,0:T(8,128)(2,1)S(1)} %shard_map.28.outs_0_.mine), channel_id=1, source_target_pairs={{0,4},{2,6},{4,8},{6,10},{8,12},{10,14},{12,0},{14,2},{1,5},{3,7},... | collective-permute-start | bytes 786440 | tf_op jit(solution)/shard_map/two_behind_0/ppermute | solution.py:28
  7.3 19.1 %collective-permute-start.11 = (bf16[1024,128]{1,0:T(8,128)(2,1)S(1)}, bf16[1024,128]{1,0:T(8,128)(2,1)S(1)}, u32[]{:S(2)}, u32[]{:S(2)}) collective-permute-start(bf16[1024,128]{1,0:T(8,128)(2,1)S(1)} %get-tuple-element.57.mine), channel_id=1, source_target_pairs={{0,12},{2,14},{4,0},{6,2},{8,4},{10,6},{12,8},{14,10},{1,13},{3,15... | collective-permute-start | bytes 786440 | tf_op jit(solution)/shard_map/two_ahead_1/ppermute | solution.py:28
  11.2 20.8 %collective-permute-start.10 = (bf16[1024,128]{1,0:T(8,128)(2,1)S(1)}, bf16[1024,128]{1,0:T(8,128)(2,1)}, u32[]{:S(2)}, u32[]{:S(2)}) collective-permute-start(bf16[1024,128]{1,0:T(8,128)(2,1)S(1)} %get-tuple-element.57.mine), channel_id=1, source_target_pairs={{0,4},{2,6},{4,8},{6,10},{8,12},{10,14},{12,0},{14,2},{1,5},{3,7},... | collective-permute-start | bytes 786440 | tf_op jit(solution)/shard_map/two_behind_1/ppermute | solution.py:28
  14.2 3.8 %collective-permute-start.1 = (s32[1]{0:T(128)}, s32[1]{0:T(128)}, u32[]{:S(2)}, u32[]{:S(2)}) collective-permute-start(s32[1]{0:T(128)} %bitcast.9), channel_id=1, source_target_pairs={{0,2},{2,0},{4,6},{6,4},{8,10},{10,8},{12,14},{14,12},{1,3},{3,1},... | collective-permute-start | bytes 20 | tf_op jit(solution)/shard_map/direction_of_pair/ppermute | solution.py:33
  22.8 12.9 %collective-permute-start.6 = (bf16[1024,128]{1,0:T(8,128)(2,1)S(1)}, bf16[1024,128]{1,0:T(8,128)(2,1)S(1)}, u32[]{:S(2)}, u32[]{:S(2)}) collective-permute-start(bf16[1024,128]{1,0:T(8,128)(2,1)S(1)} %get-tuple-element.46), channel_id=1, source_target_pairs={{0,2},{2,0},{4,6},{6,4},{8,10},{10,8},{12,14},{14,12},{1,3},{3,1},... | collective-permute-start | bytes 786440 | tf_op jit(solution)/shard_map/near_0/ppermute | solution.py:33
  24.4 12.7 %collective-permute-start.14 = (bf16[1024,128]{1,0:T(8,128)(2,1)S(1)}, bf16[1024,128]{1,0:T(8,128)(2,1)S(1)}, u32[]{:S(2)}, u32[]{:S(2)}) collective-permute-start(bf16[1024,128]{1,0:T(8,128)(2,1)S(1)} %get-tuple-element.59.mine), channel_id=1, source_target_pairs={{0,12},{2,14},{4,0},{6,2},{8,4},{10,6},{12,8},{14,10},{1,13},{3,15... | collective-permute-start | bytes 786440 | tf_op jit(solution)/shard_map/two_ahead_2/ppermute | solution.py:28
  26.4 16.7 %collective-permute-start.13 = (bf16[1024,128]{1,0:T(8,128)(2,1)S(1)}, bf16[1024,128]{1,0:T(8,128)(2,1)S(1)}, u32[]{:S(2)}, u32[]{:S(2)}) collective-permute-start(bf16[1024,128]{1,0:T(8,128)(2,1)S(1)} %get-tuple-element.59.mine), channel_id=1, source_target_pairs={{0,4},{2,6},{4,8},{6,10},{8,12},{10,14},{12,0},{14,2},{1,5},{3,7},... | collective-permute-start | bytes 786440 | tf_op jit(solution)/shard_map/two_behind_2/ppermute | solution.py:28
  34.1 11.9 %collective-permute-start.12 = (bf16[1024,128]{1,0:T(8,128)(2,1)S(1)}, bf16[1024,128]{1,0:T(8,128)(2,1)S(1)}, u32[]{:S(2)}, u32[]{:S(2)}) collective-permute-start(bf16[1024,128]{1,0:T(8,128)(2,1)S(1)} %get-tuple-element.58), channel_id=1, source_target_pairs={{0,2},{2,0},{4,6},{6,4},{8,10},{10,8},{12,14},{14,12},{1,3},{3,1},... | collective-permute-start | bytes 786440 | tf_op jit(solution)/shard_map/near_1/ppermute | solution.py:33
  35.7 11.8 %collective-permute-start.8 = (bf16[1024,128]{1,0:T(8,128)(2,1)S(1)}, bf16[1024,128]{1,0:T(8,128)(2,1)S(1)}, u32[]{:S(2)}, u32[]{:S(2)}) collective-permute-start(bf16[1024,128]{1,0:T(8,128)(2,1)S(1)} %get-tuple-element.47.refs_7_), channel_id=1, source_target_pairs={{0,1},{1,0},{2,3},{3,2},{4,5},{5,4},{6,7},{7,6},{8,9},{9,8},{10,11... | collective-permute-start | bytes 786440 | tf_op jit(solution)/shard_map/far_other_half_0/ppermute | solution.py:28
  35.7 11.8 %collective-permute-start.7 = (bf16[1024,128]{1,0:T(8,128)(2,1)S(1)}, bf16[1024,128]{1,0:T(8,128)(2,1)S(1)}, u32[]{:S(2)}, u32[]{:S(2)}) collective-permute-start(bf16[1024,128]{1,0:T(8,128)(2,1)S(1)} %collective-permute-done.6.refs_5_), channel_id=1, source_target_pairs={{0,1},{1,0},{2,3},{3,2},{4,5},{5,4},{6,7},{7,6},{8,9},{9,8},{10,11... | collective-permute-start | bytes 786440 | tf_op jit(solution)/shard_map/near_other_half_0/ppermute | solution.py:28
  37.1 15.1 %collective-permute-start.3 = (bf16[1024,128]{1,0:T(8,128)(2,1)S(1)}, bf16[1024,128]{1,0:T(8,128)(2,1)S(1)}, u32[]{:S(2)}, u32[]{:S(2)}) collective-permute-start(bf16[1024,128]{1,0:T(8,128)(2,1)S(1)} %get-tuple-element.41.mine), channel_id=1, source_target_pairs={{0,12},{2,14},{4,0},{6,2},{8,4},{10,6},{12,8},{14,10},{1,13},{3,15... | collective-permute-start | bytes 786440 | tf_op jit(solution)/shard_map/two_ahead_3/ppermute | solution.py:28
  43.1 10.8 %collective-permute-start.2 = (bf16[1024,128]{1,0:T(8,128)(2,1)S(1)}, bf16[1024,128]{1,0:T(8,128)(2,1)S(1)}, u32[]{:S(2)}, u32[]{:S(2)}) collective-permute-start(bf16[1024,128]{1,0:T(8,128)(2,1)S(1)} %get-tuple-element.41.mine), channel_id=1, source_target_pairs={{0,4},{2,6},{4,8},{6,10},{8,12},{10,14},{12,0},{14,2},{1,5},{3,7},... | collective-permute-start | bytes 786440 | tf_op jit(solution)/shard_map/two_behind_3/ppermute | solution.py:28
  45.9 9.4 %collective-permute-start.17 = (bf16[1024,128]{1,0:T(8,128)(2,1)S(1)}, bf16[1024,128]{1,0:T(8,128)(2,1)S(1)}, u32[]{:S(2)}, u32[]{:S(2)}) collective-permute-start(bf16[1024,128]{1,0:T(8,128)(2,1)S(1)} %get-tuple-element.60), channel_id=1, source_target_pairs={{0,2},{2,0},{4,6},{6,4},{8,10},{10,8},{12,14},{14,12},{1,3},{3,1},... | collective-permute-start | bytes 786440 | tf_op jit(solution)/shard_map/near_2/ppermute | solution.py:33
  47.5 9.5 %collective-permute-start.16 = (bf16[1024,128]{1,0:T(8,128)(2,1)S(1)}, bf16[1024,128]{1,0:T(8,128)(2,1)S(1)}, u32[]{:S(2)}, u32[]{:S(2)}) collective-permute-start(bf16[1024,128]{1,0:T(8,128)(2,1)S(1)} %get-tuple-element.62.refs_11_), channel_id=1, source_target_pairs={{0,1},{1,0},{2,3},{3,2},{4,5},{5,4},{6,7},{7,6},{8,9},{9,8},{10,11... | collective-permute-start | bytes 786440 | tf_op jit(solution)/shard_map/far_other_half_1/ppermute | solution.py:28
  47.5 9.6 %collective-permute-start.19 = (bf16[1024,128]{1,0:T(8,128)(2,1)S(1)}, bf16[1024,128]{1,0:T(8,128)(2,1)S(1)}, u32[]{:S(2)}, u32[]{:S(2)}) collective-permute-start(bf16[1024,128]{1,0:T(8,128)(2,1)S(1)} %get-tuple-element.64.refs_15_), channel_id=1, source_target_pairs={{0,1},{1,0},{2,3},{3,2},{4,5},{5,4},{6,7},{7,6},{8,9},{9,8},{10,11... | collective-permute-start | bytes 786440 | tf_op jit(solution)/shard_map/far_other_half_2/ppermute | solution.py:28
  52.3 4.9 %collective-permute-start.15 = (bf16[1024,128]{1,0:T(8,128)(2,1)S(1)}, bf16[1024,128]{1,0:T(8,128)(2,1)S(1)}, u32[]{:S(2)}, u32[]{:S(2)}) collective-permute-start(bf16[1024,128]{1,0:T(8,128)(2,1)S(1)} %collective-permute-done.12.refs_9_), channel_id=1, source_target_pairs={{0,1},{1,0},{2,3},{3,2},{4,5},{5,4},{6,7},{7,6},{8,9},{9,8},{10,11... | collective-permute-start | bytes 786440 | tf_op jit(solution)/shard_map/near_other_half_1/ppermute | solution.py:28
  55.3 1.8 %collective-permute-start.18 = (bf16[1024,128]{1,0:T(8,128)(2,1)S(1)}, bf16[1024,128]{1,0:T(8,128)(2,1)S(1)}, u32[]{:S(2)}, u32[]{:S(2)}) collective-permute-start(bf16[1024,128]{1,0:T(8,128)(2,1)S(1)} %collective-permute-done.17.refs_13_), channel_id=1, source_target_pairs={{0,1},{1,0},{2,3},{3,2},{4,5},{5,4},{6,7},{7,6},{8,9},{9,8},{10,11... | collective-permute-start | bytes 786440 | tf_op jit(solution)/shard_map/near_other_half_2/ppermute | solution.py:28
  55.4 10.1 %collective-permute-start.9 = (bf16[1024,128]{1,0:T(8,128)(2,1)S(1)}, bf16[1024,128]{1,0:T(8,128)(2,1)S(1)}, u32[]{:S(2)}, u32[]{:S(2)}) collective-permute-start(bf16[1024,128]{1,0:T(8,128)(2,1)S(1)} %get-tuple-element.48), channel_id=1, source_target_pairs={{0,2},{2,0},{4,6},{6,4},{8,10},{10,8},{12,14},{14,12},{1,3},{3,1},... | collective-permute-start | bytes 786440 | tf_op jit(solution)/shard_map/near_3/ppermute | solution.py:33
  57.0 9.0 %collective-permute-start.21 = (bf16[1024,128]{1,0:T(8,128)(2,1)S(1)}, bf16[1024,128]{1,0:T(8,128)(2,1)S(1)}, u32[]{:S(2)}, u32[]{:S(2)}) collective-permute-start(bf16[1024,128]{1,0:T(8,128)(2,1)S(1)} %get-tuple-element.66.refs_7_), channel_id=1, source_target_pairs={{0,1},{1,0},{2,3},{3,2},{4,5},{5,4},{6,7},{7,6},{8,9},{9,8},{10,11... | collective-permute-start | bytes 786440 | tf_op jit(solution)/shard_map/far_other_half_3/ppermute | solution.py:28
  65.6 1.6 %collective-permute-start.20 = (bf16[1024,128]{1,0:T(8,128)(2,1)S(1)}, bf16[1024,128]{1,0:T(8,128)(2,1)S(1)}, u32[]{:S(2)}, u32[]{:S(2)}) collective-permute-start(bf16[1024,128]{1,0:T(8,128)(2,1)S(1)} %collective-permute-done.9.refs_5_), channel_id=1, source_target_pairs={{0,1},{1,0},{2,3},{3,2},{4,5},{5,4},{6,7},{7,6},{8,9},{9,8},{10,11... | collective-permute-start | bytes 786440 | tf_op jit(solution)/shard_map/near_other_half_3/ppermute | solution.py:28

commit v5 on v4

--- a/solution.py
+++ b/solution.py
@@ -11,8 +11,8 @@
 LAGS = 64
 ROUNDS = 2
 GROUP = 8
-CHANNEL_BLOCK = 32
-UNROLL = 2
+CHANNEL_BLOCK = 64
+UNROLL = 1
 CHUNKS = (64, 64, 64, 64)
 VMEM = 20 * 2**20
 AFTER = {3: 0}
@@ -221,19 +221,31 @@
     far, near, held, sems = rest[-4:]
     odd = lax.axis_index("blk") % 2
 
-    def fetch(source, n):
-        return pltpu.make_async_copy(source, held.at[n], sems.at[n])
-
-    pl.when(direction[1, 0] == 1)(lambda: fetch(ahead, 0).start())
-    pl.when(direction[1, 0] != 1)(lambda: fetch(behind, 0).start())
-    pl.when(of_pair[0] == odd)(lambda: fetch(mine, 1).start())
-    pl.when((of_pair[0] != odd) & (odd == 1))(lambda: fetch(behind, 1).start())
-    pl.when((of_pair[0] != odd) & (odd == 0))(lambda: fetch(ahead, 1).start())
-    for n, out in enumerate((far, near)):
-        fetch(mine, n).wait()
-        pltpu.make_async_copy(held.at[n], out, sems.at[n]).start()
-    for n, out in enumerate((far, near)):
-        pltpu.make_async_copy(held.at[n], out, sems.at[n]).wait()
+    half = mine.shape[0] // 2
+    pieces = [(n, k) for n in range(2) for k in range(2)]
+
+    def fetch(source, n, k):
+        at = slice(k * half, (k + 1) * half)
+        return pltpu.make_async_copy(source.at[at, :], held.at[n, at, :], sems.at[n, k])
+
+    def store(n, k):
+        at = slice(k * half, (k + 1) * half)
+        return pltpu.make_async_copy(held.at[n, at, :], (far, near)[n].at[at, :], sems.at[n, k])
+
+    def fetch_both(source, n):
+        for k in range(2):
+            fetch(source, n, k).start()
+
+    pl.when(direction[1, 0] == 1)(lambda: fetch_both(ahead, 0))
+    pl.when(direction[1, 0] != 1)(lambda: fetch_both(behind, 0))
+    pl.when(of_pair[0] == odd)(lambda: fetch_both(mine, 1))
+    pl.when((of_pair[0] != odd) & (odd == 1))(lambda: fetch_both(behind, 1))
+    pl.when((of_pair[0] != odd) & (odd == 0))(lambda: fetch_both(ahead, 1))
+    for n, k in pieces:
+        fetch(mine, n, k).wait()
+        store(n, k).start()
+    for n, k in pieces:
+        store(n, k).wait()
 
 
 def choose(direction, of_pair, mine, behind, ahead, after):
@@ -244,7 +256,7 @@
         in_specs=[smem, smem] + [hbm] * (3 + len(after)),
         out_specs=[hbm, hbm],
         out_shape=[jax.ShapeDtypeStruct(mine.shape, mine.dtype)] * 2,
-        scratch_shapes=[pltpu.VMEM((2, *mine.shape), mine.dtype), pltpu.SemaphoreType.DMA((2,))],
+        scratch_shapes=[pltpu.VMEM((2, *mine.shape), mine.dtype), pltpu.SemaphoreType.DMA((2, 2))],
         compiler_params=pltpu.CompilerParams(vmem_limit_bytes=VMEM),
         cost_estimate=COST,
     )(direction, of_pair, mine, behind, ahead, *after)

time: 72.7 us -> 74 us (1.018)
  Pallas kernels: 27.4 us -> 30.9 us
  waiting for transfers between devices: 14.4 us -> 12.4 us
    pallas_call x4, Pallas kernels: 7.03 us -> 10.7 us  [choose(): pl.pallas_call(choose_kernel, in_specs=[smem, smem] + [hbm] * (3 + len(af...]
    ppermute x17, waiting for transfers between devices: 13.9 us -> 11.8 us  [ring_shift(): return lax.ppermute(x, axis, [(i, (i + by) % size) for i in range(size)])]
  transfers between devices with their start and end apart: 22 -> 22, of which waited for: 7 -> 7; matrix products, arithmetic and copies ran while one was open for 4% -> 4% of each run, Pallas kernels for 29% -> 34%
where the time goes in v5:
time: 74 us; the launch traced here: 73.7 us
  Pallas kernels  30.9 us (42%)
  starting transfers between devices  25.9 us (35%)
  waiting for transfers between devices  12.4 us (17%)
  local copies, waits for them, and re-layouts  2.95 us (4%)
  other arithmetic  1.29 us (2%)
    ppermute x17, starting transfers between devices, ring_shift(): return lax.ppermute(x, axis, [(i, (i + by) % size) for i in range(size)])  18.1 us
    pallas_call x3, Pallas kernels, add_lags(): pl.pallas_call(functools.partial(lag_kernel, first=first, runs=len(partne...  17.5 us
    ppermute x17, waiting for transfers between devices, ring_shift(): return lax.ppermute(x, axis, [(i, (i + by) % size) for i in range(size)])  11.8 us
    pallas_call x4, Pallas kernels, choose(): pl.pallas_call(choose_kernel, in_specs=[smem, smem] + [hbm] * (3 + len(af...  10.7 us
    ppermute x5, starting transfers between devices, pair_swap(): return lax.ppermute(x, axis, [(i, i ^ 1) for i in range(size)])  7.81 us
    unnamed x3, local copies, waits for them, and re-layouts  1.97 us
    pallas_call x1, Pallas kernels, channels_first(): pl.pallas_call(channels_first_kernel, out_shape=[pltpu.VMEM((own.shape[1]...  1.72 us
  transfers between devices with their start and end apart: 22, of which 7 were waited for; matrix products, arithmetic and copies ran while one was open for 4% of the time, Pallas kernels for 34%

profile of v5, /device:TPU:0, one launch (start us, length us, event | category | flops | bytes accessed | tf_op | source)
XLA Modules:
  0.0 73.7 jit_solution(12915810901214932238)
XLA Ops:
  0.0 1.2 %copy-done = bf16[8,2,256,128]{3,2,1,0:T(8,128)(2,1)S(1)} copy-done((bf16[8,2,256,128]{3,2,1,0:T(8,128)(2,1)S(1)}, bf16[8,2,256,128]{3,2,1,0:T(8,128)(2,1)}, u32[]{:S(2)}) %copy-start) | copy-done | bytes 1048600
  1.2 0.1 shard_map.28.outs_0_.mine
  1.4 0.8 %shard_map.29 = (bf16[1024,128]{1,0:T(8,128)(2,1)S(1)}, bf16[1024,128]{1,0:T(8,128)(2,1)S(1)}, bf16[1024,128]{1,0:T(8,128)(2,1)S(1)}, bf16[4096,128]{1,0:T(8,128)(2,1)S(1)}) custom-call(bf16[8,2,256,128]{3,2,1,0:T(8,128)(2,1)S(1)} %copy-done, bf16[1024,128]{1,0:T(8,128)(2,1)S(1)} %shard_map.28.outs_0_.mine), custom_call_target="tpu_custom_call" | custom-call | tf_op jit(solution)/shard_map/pallas_call | solution.py:180
  2.2 0.5 collective-permute-start
  2.7 4.7 %collective-permute-start.5 = (bf16[1024,128]{1,0:T(8,128)(2,1)S(1)}, bf16[1024,128]{1,0:T(8,128)(2,1)}, u32[]{:S(2)}, u32[]{:S(2)}) collective-permute-start(bf16[1024,128]{1,0:T(8,128)(2,1)S(1)} %shard_map.28.outs_0_.mine), channel_id=1, source_target_pairs={{0,12},{2,14},{4,0},{6,2},{8,4},{10,6},{12,8},{14,10},{1,13},{3,15... | collective-permute-start | bytes 786440 | tf_op jit(solution)/shard_map/two_ahead_0/ppermute | solution.py:28
  7.3 3.8 %collective-permute-start.11 = (bf16[1024,128]{1,0:T(8,128)(2,1)S(1)}, bf16[1024,128]{1,0:T(8,128)(2,1)S(1)}, u32[]{:S(2)}, u32[]{:S(2)}) collective-permute-start(bf16[1024,128]{1,0:T(8,128)(2,1)S(1)} %get-tuple-element.57.mine), channel_id=1, source_target_pairs={{0,12},{2,14},{4,0},{6,2},{8,4},{10,6},{12,8},{14,10},{1,13},{3,15... | collective-permute-start | bytes 786440 | tf_op jit(solution)/shard_map/two_ahead_1/ppermute | solution.py:28
  11.2 0.0 collective-permute-start.10
  11.2 0.7 %copy.12.direction = s32[2,1]{1,0:T(2,128)S(1)} copy(s32[2,1]{0,1:T(1,128)} %param.3) | data formatting | bytes 16 | tf_op args[1]
  11.9 0.6 fusion.4
  12.5 0.7 fusion
  13.2 1.0 %copy.16.rest_1_.refs_0_ = bf16[64,512]{1,0:T(8,128)(2,1)S(1)} copy(bf16[64,512]{0,1:T(8,128)(2,1)} %bitcast.8) | data formatting | bytes 131072 | tf_op jit(solution)/shard_map/reshape | solution.py:45
  14.2 0.0 collective-permute-done.other
  14.2 1.6 %collective-permute-start.1 = (s32[1]{0:T(128)}, s32[1]{0:T(128)}, u32[]{:S(2)}, u32[]{:S(2)}) collective-permute-start(s32[1]{0:T(128)} %bitcast.9), channel_id=1, source_target_pairs={{0,2},{2,0},{4,6},{6,4},{8,10},{10,8},{12,14},{14,12},{1,3},{3,1},... | collective-permute-start | bytes 20 | tf_op jit(solution)/shard_map/direction_of_pair/ppermute | solution.py:33
  15.8 1.7 %shard_map.30 = (f32[128,1024]{1,0:T(8,128)S(1)}, f32[128,1024]{1,0:T(8,128)S(1)}, f32[128,1024]{1,0:T(8,128)S(1)}, f32[128,1024]{1,0:T(8,128)S(1)}, f32[128,102...) custom-call(bf16[4096,128]{1,0:T(8,128)(2,1)S(1)} %get-tuple-element, ...), custom_call_target="tpu_custom_call" | custom-call | tf_op jit(solution)/shard_map/pallas_call | solution.py:209
  17.5 0.5 collective-permute-done.1.of_pair
  18.1 2.6 %collective-permute-done.4.behind = bf16[1024,128]{1,0:T(8,128)(2,1)} collective-permute-done((bf16[1024,128]{1,0:T(8,128)(2,1)S(1)}, bf16[1024,128]{1,0:T(8,128)(2,1)}, u32[]{:S(2)}, u32[]{:S(2)}) %collective-permute-start.4) | collective-permute-done | bytes 262176 | tf_op jit(solution)/shard_map/two_behind_0/ppermute | solution.py:28
  20.6 2.7 %shard_map.31 = (bf16[1024,128]{1,0:T(8,128)(2,1)S(1)}, bf16[1024,128]{1,0:T(8,128)(2,1)S(1)}) custom-call(s32[2,1]{1,0:T(2,128)S(1)} %copy.12.direction, s32[1]{0:T(128)} %collective-permute-done.1.of_pair, bf16[1024,128]{1,0:T(8,128)(2,1)S(1)} %shard_map.28.outs_0_.mine, bf16[1024,128]{1,0:T(8,128)(2,1)} %collective-permute-done.4.behind, ...), custom_call_target="tpu_custom_call" | custom-call | tf_op jit(solution)/shard_map/pallas_call | solution.py:254
  23.4 1.6 %collective-permute-start.6 = (bf16[1024,128]{1,0:T(8,128)(2,1)S(1)}, bf16[1024,128]{1,0:T(8,128)(2,1)S(1)}, u32[]{:S(2)}, u32[]{:S(2)}) collective-permute-start(bf16[1024,128]{1,0:T(8,128)(2,1)S(1)} %get-tuple-element.46), channel_id=1, source_target_pairs={{0,2},{2,0},{4,6},{6,4},{8,10},{10,8},{12,14},{14,12},{1,3},{3,1},... | collective-permute-start | bytes 786440 | tf_op jit(solution)/shard_map/near_0/ppermute | solution.py:33
  24.9 2.0 %collective-permute-start.14 = (bf16[1024,128]{1,0:T(8,128)(2,1)S(1)}, bf16[1024,128]{1,0:T(8,128)(2,1)S(1)}, u32[]{:S(2)}, u32[]{:S(2)}) collective-permute-start(bf16[1024,128]{1,0:T(8,128)(2,1)S(1)} %get-tuple-element.59.mine), channel_id=1, source_target_pairs={{0,12},{2,14},{4,0},{6,2},{8,4},{10,6},{12,8},{14,10},{1,13},{3,15... | collective-permute-start | bytes 786440 | tf_op jit(solution)/shard_map/two_ahead_2/ppermute | solution.py:28
  27.0 0.0 collective-permute-start.13
  27.0 0.0 collective-permute-done.11.ahead
  27.0 4.9 %collective-permute-done.10.behind = bf16[1024,128]{1,0:T(8,128)(2,1)} collective-permute-done((bf16[1024,128]{1,0:T(8,128)(2,1)S(1)}, bf16[1024,128]{1,0:T(8,128)(2,1)}, u32[]{:S(2)}, u32[]{:S(2)}) %collective-permute-start.10) | collective-permute-done | bytes 262176 | tf_op jit(solution)/shard_map/two_behind_1/ppermute | solution.py:28
  31.9 2.7 %shard_map.34 = (bf16[1024,128]{1,0:T(8,128)(2,1)S(1)}, bf16[1024,128]{1,0:T(8,128)(2,1)S(1)}) custom-call(s32[2,1]{1,0:T(2,128)S(1)} %copy.12.direction, s32[1]{0:T(128)} %collective-permute-done.1.of_pair, bf16[1024,128]{1,0:T(8,128)(2,1)S(1)} %get-tuple-element.57.mine, bf16[1024,128]{1,0:T(8,128)(2,1)} %collective-permute-done.10.behind, ...), custom_call_target="tpu_custom_call" | custom-call | tf_op jit(solution)/shard_map/pallas_call | solution.py:254
  34.6 1.6 %collective-permute-start.12 = (bf16[1024,128]{1,0:T(8,128)(2,1)S(1)}, bf16[1024,128]{1,0:T(8,128)(2,1)S(1)}, u32[]{:S(2)}, u32[]{:S(2)}) collective-permute-start(bf16[1024,128]{1,0:T(8,128)(2,1)S(1)} %get-tuple-element.58), channel_id=1, source_target_pairs={{0,2},{2,0},{4,6},{6,4},{8,10},{10,8},{12,14},{14,12},{1,3},{3,1},... | collective-permute-start | bytes 786440 | tf_op jit(solution)/shard_map/near_1/ppermute | solution.py:33
  36.2 0.5 collective-permute-start.7
  36.7 0.6 collective-permute-done.14.ahead
  37.3 3.5 %collective-permute-start.3 = (bf16[1024,128]{1,0:T(8,128)(2,1)S(1)}, bf16[1024,128]{1,0:T(8,128)(2,1)S(1)}, u32[]{:S(2)}, u32[]{:S(2)}) collective-permute-start(bf16[1024,128]{1,0:T(8,128)(2,1)S(1)} %get-tuple-element.41.mine), channel_id=1, source_target_pairs={{0,12},{2,14},{4,0},{6,2},{8,4},{10,6},{12,8},{14,10},{1,13},{3,15... | collective-permute-start | bytes 786440 | tf_op jit(solution)/shard_map/two_ahead_3/ppermute | solution.py:28
  40.9 2.2 %collective-permute-done.13.behind = bf16[1024,128]{1,0:T(8,128)(2,1)S(1)} collective-permute-done((bf16[1024,128]{1,0:T(8,128)(2,1)S(1)}, bf16[1024,128]{1,0:T(8,128)(2,1)S(1)}, u32[]{:S(2)}, u32[]{:S(2)}) %collective-permute-start.13) | collective-permute-done | bytes 262176 | tf_op jit(solution)/shard_map/two_behind_2/ppermute | solution.py:28
  43.1 1.6 %collective-permute-start.2 = (bf16[1024,128]{1,0:T(8,128)(2,1)S(1)}, bf16[1024,128]{1,0:T(8,128)(2,1)S(1)}, u32[]{:S(2)}, u32[]{:S(2)}) collective-permute-start(bf16[1024,128]{1,0:T(8,128)(2,1)S(1)} %get-tuple-element.41.mine), channel_id=1, source_target_pairs={{0,4},{2,6},{4,8},{6,10},{8,12},{10,14},{12,0},{14,2},{1,5},{3,7},... | collective-permute-start | bytes 786440 | tf_op jit(solution)/shard_map/two_behind_3/ppermute | solution.py:28
  44.7 2.6 %shard_map.35 = (bf16[1024,128]{1,0:T(8,128)(2,1)S(1)}, bf16[1024,128]{1,0:T(8,128)(2,1)S(1)}) custom-call(s32[2,1]{1,0:T(2,128)S(1)} %copy.12.direction, s32[1]{0:T(128)} %collective-permute-done.1.of_pair, bf16[1024,128]{1,0:T(8,128)(2,1)S(1)} %get-tuple-element.59.mine, bf16[1024,128]{1,0:T(8,128)(2,1)S(1)} %collective-permute-done.13.behind, ...), custom_call_target="tpu_custom_call" | custom-call | tf_op jit(solution)/shard_map/pallas_call | solution.py:254
  47.2 1.6 %collective-permute-start.17 = (bf16[1024,128]{1,0:T(8,128)(2,1)S(1)}, bf16[1024,128]{1,0:T(8,128)(2,1)S(1)}, u32[]{:S(2)}, u32[]{:S(2)}) collective-permute-start(bf16[1024,128]{1,0:T(8,128)(2,1)S(1)} %get-tuple-element.60), channel_id=1, source_target_pairs={{0,2},{2,0},{4,6},{6,4},{8,10},{10,8},{12,14},{14,12},{1,3},{3,1},... | collective-permute-start | bytes 786440 | tf_op jit(solution)/shard_map/near_2/ppermute | solution.py:33
  48.8 0.0 collective-permute-done.8.refs_8_
  48.8 0.0 collective-permute-start.16
  48.8 0.5 collective-permute-start.19
  49.3 4.1 %shard_map.32.rest_0_.refs_17_ = f32[2,32,128,128]{3,2,1,0:T(8,128)S(1)} custom-call(bf16[64,512]{1,0:T(8,128)(2,1)S(1)} %copy.16.rest_1_.refs_0_, f32[128,1024]{1,0:T(8,128)S(1)} %get-tuple-element.42.rest_0_.refs_1_, f32[128,1024]{1,0:T(8,128)S(1)} %get-tuple-element.43.refs_2_, f32[128,1024]{1,0:T(8,128)S(1)} %get-tuple-element.44.refs_3_, ...), custom_call_target="tpu_custom_call" | custom-call | flops 6000000000 | tf_op jit(solution)/shard_map/pallas_call | solution.py:150
  53.4 0.0 collective-permute-done.3.ahead
  53.4 0.1 collective-permute-start.15
  53.6 0.3 collective-permute-done.2.behind
  53.9 2.7 %shard_map.33 = (bf16[1024,128]{1,0:T(8,128)(2,1)S(1)}, bf16[1024,128]{1,0:T(8,128)(2,1)S(1)}) custom-call(s32[2,1]{1,0:T(2,128)S(1)} %copy.12.direction, s32[1]{0:T(128)} %collective-permute-done.1.of_pair, bf16[1024,128]{1,0:T(8,128)(2,1)S(1)} %get-tuple-element.41.mine, bf16[1024,128]{1,0:T(8,128)(2,1)S(1)} %collective-permute-done.2.behind, ...), custom_call_target="tpu_custom_call" | custom-call | tf_op jit(solution)/shard_map/pallas_call | solution.py:254
  56.6 0.0 collective-permute-done.17.refs_13_
  56.6 0.2 collective-permute-start.18
  56.8 1.5 %collective-permute-start.9 = (bf16[1024,128]{1,0:T(8,128)(2,1)S(1)}, bf16[1024,128]{1,0:T(8,128)(2,1)S(1)}, u32[]{:S(2)}, u32[]{:S(2)}) collective-permute-start(bf16[1024,128]{1,0:T(8,128)(2,1)S(1)} %get-tuple-element.48), channel_id=1, source_target_pairs={{0,2},{2,0},{4,6},{6,4},{8,10},{10,8},{12,14},{14,12},{1,3},{3,1},... | collective-permute-start | bytes 786440 | tf_op jit(solution)/shard_map/near_3/ppermute | solution.py:33
  58.3 0.0 collective-permute-done.16.refs_12_
  58.3 0.2 collective-permute-start.21
  58.5 8.3 %shard_map.36.refs_9_ = f32[2,32,128,128]{3,2,1,0:T(8,128)S(1)} custom-call(bf16[64,512]{1,0:T(8,128)(2,1)S(1)} %copy.16.rest_1_.refs_0_, f32[128,1024]{1,0:T(8,128)S(1)} %get-tuple-element.49.refs_1_, f32[128,1024]{1,0:T(8,128)S(1)} %get-tuple-element.50.refs_2_, f32[128,1024]{1,0:T(8,128)S(1)} %get-tuple-element.51.refs_3_, ...), custom_call_target="tpu_custom_call", output_to_operand_aliasing={{}: (17, {})} | custom-call | flops 12000000000 | tf_op jit(solution)/shard_map/pallas_call | solution.py:150
  66.8 0.4 collective-permute-start.20
  67.2 1.2 %collective-permute-done.20.refs_6_ = bf16[1024,128]{1,0:T(8,128)(2,1)S(1)} collective-permute-done((bf16[1024,128]{1,0:T(8,128)(2,1)S(1)}, bf16[1024,128]{1,0:T(8,128)(2,1)S(1)}, u32[]{:S(2)}, u32[]{:S(2)}) %collective-permute-start.20) | collective-permute-done | bytes 262176 | tf_op jit(solution)/shard_map/near_other_half_3/ppermute | solution.py:28
  68.4 5.2 %shard_map.37 = f32[2,32,128,128]{3,2,1,0:T(8,128)} custom-call(bf16[64,512]{1,0:T(8,128)(2,1)S(1)} %copy.16.rest_1_.refs_0_, f32[128,1024]{1,0:T(8,128)S(1)} %get-tuple-element.37.refs_1_, f32[128,1024]{1,0:T(8,128)S(1)} %get-tuple-element.38.refs_2_, f32[128,1024]{1,0:T(8,128)S(1)} %get-tuple-element.39.refs_3_, ...), custom_call_target="tpu_custom_call" | custom-call | flops 6000000000 | tf_op jit(solution)/shard_map/pallas_call | solution.py:150
  (14 shorter events, 0.0 us)
Async XLA Ops:
  0.0 1.2 %copy-start = (bf16[8,2,256,128]{3,2,1,0:T(8,128)(2,1)S(1)}, bf16[8,2,256,128]{3,2,1,0:T(8,128)(2,1)}, u32[]{:S(2)}) copy-start(bf16[8,2,256,128]{3,2,1,0:T(8,128)(2,1)} %x.3) | copy-start | bytes 3145732
  2.2 12.0 %collective-permute-start = (bf16[4096,128]{1,0:T(8,128)(2,1)S(1)}, bf16[4096,128]{1,0:T(8,128)(2,1)S(1)}, u32[]{:S(2)}, u32[]{:S(2)}) collective-permute-start(bf16[4096,128]{1,0:T(8,128)(2,1)S(1)} %get-tuple-element.36.own), channel_id=1, source_target_pairs={{0,1},{1,0},{2,3},{3,2},{4,5},{5,4},{6,7},{7,6},{8,9},{9,8},{10,11... | collective-permute-start | bytes 3145736 | tf_op jit(solution)/shard_map/my_other_half/ppermute | solution.py:28
  2.7 15.4 %collective-permute-start.5 = (bf16[1024,128]{1,0:T(8,128)(2,1)S(1)}, bf16[1024,128]{1,0:T(8,128)(2,1)}, u32[]{:S(2)}, u32[]{:S(2)}) collective-permute-start(bf16[1024,128]{1,0:T(8,128)(2,1)S(1)} %shard_map.28.outs_0_.mine), channel_id=1, source_target_pairs={{0,12},{2,14},{4,0},{6,2},{8,4},{10,6},{12,8},{14,10},{1,13},{3,15... | collective-permute-start | bytes 786440 | tf_op jit(solution)/shard_map/two_ahead_0/ppermute | solution.py:28
  7.3 13.3 %collective-permute-start.4 = (bf16[1024,128]{1,0:T(8,128)(2,1)S(1)}, bf16[1024,128]{1,0:T(8,128)(2,1)}, u32[]{:S(2)}, u32[]{:S(2)}) collective-permute-start(bf16[1024,128]{1,0:T(8,128)(2,1)S(1)} %shard_map.28.outs_0_.mine), channel_id=1, source_target_pairs={{0,4},{2,6},{4,8},{6,10},{8,12},{10,14},{12,0},{14,2},{1,5},{3,7},... | collective-permute-start | bytes 786440 | tf_op jit(solution)/shard_map/two_behind_0/ppermute | solution.py:28
  7.3 19.6 %collective-permute-start.11 = (bf16[1024,128]{1,0:T(8,128)(2,1)S(1)}, bf16[1024,128]{1,0:T(8,128)(2,1)S(1)}, u32[]{:S(2)}, u32[]{:S(2)}) collective-permute-start(bf16[1024,128]{1,0:T(8,128)(2,1)S(1)} %get-tuple-element.57.mine), channel_id=1, source_target_pairs={{0,12},{2,14},{4,0},{6,2},{8,4},{10,6},{12,8},{14,10},{1,13},{3,15... | collective-permute-start | bytes 786440 | tf_op jit(solution)/shard_map/two_ahead_1/ppermute | solution.py:28
  11.2 20.8 %collective-permute-start.10 = (bf16[1024,128]{1,0:T(8,128)(2,1)S(1)}, bf16[1024,128]{1,0:T(8,128)(2,1)}, u32[]{:S(2)}, u32[]{:S(2)}) collective-permute-start(bf16[1024,128]{1,0:T(8,128)(2,1)S(1)} %get-tuple-element.57.mine), channel_id=1, source_target_pairs={{0,4},{2,6},{4,8},{6,10},{8,12},{10,14},{12,0},{14,2},{1,5},{3,7},... | collective-permute-start | bytes 786440 | tf_op jit(solution)/shard_map/two_behind_1/ppermute | solution.py:28
  14.2 3.8 %collective-permute-start.1 = (s32[1]{0:T(128)}, s32[1]{0:T(128)}, u32[]{:S(2)}, u32[]{:S(2)}) collective-permute-start(s32[1]{0:T(128)} %bitcast.9), channel_id=1, source_target_pairs={{0,2},{2,0},{4,6},{6,4},{8,10},{10,8},{12,14},{14,12},{1,3},{3,1},... | collective-permute-start | bytes 20 | tf_op jit(solution)/shard_map/direction_of_pair/ppermute | solution.py:33
  23.4 12.9 %collective-permute-start.6 = (bf16[1024,128]{1,0:T(8,128)(2,1)S(1)}, bf16[1024,128]{1,0:T(8,128)(2,1)S(1)}, u32[]{:S(2)}, u32[]{:S(2)}) collective-permute-start(bf16[1024,128]{1,0:T(8,128)(2,1)S(1)} %get-tuple-element.46), channel_id=1, source_target_pairs={{0,2},{2,0},{4,6},{6,4},{8,10},{10,8},{12,14},{14,12},{1,3},{3,1},... | collective-permute-start | bytes 786440 | tf_op jit(solution)/shard_map/near_0/ppermute | solution.py:33
  24.9 12.4 %collective-permute-start.14 = (bf16[1024,128]{1,0:T(8,128)(2,1)S(1)}, bf16[1024,128]{1,0:T(8,128)(2,1)S(1)}, u32[]{:S(2)}, u32[]{:S(2)}) collective-permute-start(bf16[1024,128]{1,0:T(8,128)(2,1)S(1)} %get-tuple-element.59.mine), channel_id=1, source_target_pairs={{0,12},{2,14},{4,0},{6,2},{8,4},{10,6},{12,8},{14,10},{1,13},{3,15... | collective-permute-start | bytes 786440 | tf_op jit(solution)/shard_map/two_ahead_2/ppermute | solution.py:28
  27.0 16.1 %collective-permute-start.13 = (bf16[1024,128]{1,0:T(8,128)(2,1)S(1)}, bf16[1024,128]{1,0:T(8,128)(2,1)S(1)}, u32[]{:S(2)}, u32[]{:S(2)}) collective-permute-start(bf16[1024,128]{1,0:T(8,128)(2,1)S(1)} %get-tuple-element.59.mine), channel_id=1, source_target_pairs={{0,4},{2,6},{4,8},{6,10},{8,12},{10,14},{12,0},{14,2},{1,5},{3,7},... | collective-permute-start | bytes 786440 | tf_op jit(solution)/shard_map/two_behind_2/ppermute | solution.py:28
  34.6 12.6 %collective-permute-start.12 = (bf16[1024,128]{1,0:T(8,128)(2,1)S(1)}, bf16[1024,128]{1,0:T(8,128)(2,1)S(1)}, u32[]{:S(2)}, u32[]{:S(2)}) collective-permute-start(bf16[1024,128]{1,0:T(8,128)(2,1)S(1)} %get-tuple-element.58), channel_id=1, source_target_pairs={{0,2},{2,0},{4,6},{6,4},{8,10},{10,8},{12,14},{14,12},{1,3},{3,1},... | collective-permute-start | bytes 786440 | tf_op jit(solution)/shard_map/near_1/ppermute | solution.py:33
  36.2 12.6 %collective-permute-start.8 = (bf16[1024,128]{1,0:T(8,128)(2,1)S(1)}, bf16[1024,128]{1,0:T(8,128)(2,1)S(1)}, u32[]{:S(2)}, u32[]{:S(2)}) collective-permute-start(bf16[1024,128]{1,0:T(8,128)(2,1)S(1)} %get-tuple-element.47.refs_7_), channel_id=1, source_target_pairs={{0,1},{1,0},{2,3},{3,2},{4,5},{5,4},{6,7},{7,6},{8,9},{9,8},{10,11... | collective-permute-start | bytes 786440 | tf_op jit(solution)/shard_map/far_other_half_0/ppermute | solution.py:28
  36.2 12.6 %collective-permute-start.7 = (bf16[1024,128]{1,0:T(8,128)(2,1)S(1)}, bf16[1024,128]{1,0:T(8,128)(2,1)S(1)}, u32[]{:S(2)}, u32[]{:S(2)}) collective-permute-start(bf16[1024,128]{1,0:T(8,128)(2,1)S(1)} %collective-permute-done.6.refs_5_), channel_id=1, source_target_pairs={{0,1},{1,0},{2,3},{3,2},{4,5},{5,4},{6,7},{7,6},{8,9},{9,8},{10,11... | collective-permute-start | bytes 786440 | tf_op jit(solution)/shard_map/near_other_half_0/ppermute | solution.py:28
  37.3 16.1 %collective-permute-start.3 = (bf16[1024,128]{1,0:T(8,128)(2,1)S(1)}, bf16[1024,128]{1,0:T(8,128)(2,1)S(1)}, u32[]{:S(2)}, u32[]{:S(2)}) collective-permute-start(bf16[1024,128]{1,0:T(8,128)(2,1)S(1)} %get-tuple-element.41.mine), channel_id=1, source_target_pairs={{0,12},{2,14},{4,0},{6,2},{8,4},{10,6},{12,8},{14,10},{1,13},{3,15... | collective-permute-start | bytes 786440 | tf_op jit(solution)/shard_map/two_ahead_3/ppermute | solution.py:28
  43.1 10.8 %collective-permute-start.2 = (bf16[1024,128]{1,0:T(8,128)(2,1)S(1)}, bf16[1024,128]{1,0:T(8,128)(2,1)S(1)}, u32[]{:S(2)}, u32[]{:S(2)}) collective-permute-start(bf16[1024,128]{1,0:T(8,128)(2,1)S(1)} %get-tuple-element.41.mine), channel_id=1, source_target_pairs={{0,4},{2,6},{4,8},{6,10},{8,12},{10,14},{12,0},{14,2},{1,5},{3,7},... | collective-permute-start | bytes 786440 | tf_op jit(solution)/shard_map/two_behind_3/ppermute | solution.py:28
  47.2 9.4 %collective-permute-start.17 = (bf16[1024,128]{1,0:T(8,128)(2,1)S(1)}, bf16[1024,128]{1,0:T(8,128)(2,1)S(1)}, u32[]{:S(2)}, u32[]{:S(2)}) collective-permute-start(bf16[1024,128]{1,0:T(8,128)(2,1)S(1)} %get-tuple-element.60), channel_id=1, source_target_pairs={{0,2},{2,0},{4,6},{6,4},{8,10},{10,8},{12,14},{14,12},{1,3},{3,1},... | collective-permute-start | bytes 786440 | tf_op jit(solution)/shard_map/near_2/ppermute | solution.py:33
  48.8 9.5 %collective-permute-start.16 = (bf16[1024,128]{1,0:T(8,128)(2,1)S(1)}, bf16[1024,128]{1,0:T(8,128)(2,1)S(1)}, u32[]{:S(2)}, u32[]{:S(2)}) collective-permute-start(bf16[1024,128]{1,0:T(8,128)(2,1)S(1)} %get-tuple-element.62.refs_11_), channel_id=1, source_target_pairs={{0,1},{1,0},{2,3},{3,2},{4,5},{5,4},{6,7},{7,6},{8,9},{9,8},{10,11... | collective-permute-start | bytes 786440 | tf_op jit(solution)/shard_map/far_other_half_1/ppermute | solution.py:28
  48.8 9.6 %collective-permute-start.19 = (bf16[1024,128]{1,0:T(8,128)(2,1)S(1)}, bf16[1024,128]{1,0:T(8,128)(2,1)S(1)}, u32[]{:S(2)}, u32[]{:S(2)}) collective-permute-start(bf16[1024,128]{1,0:T(8,128)(2,1)S(1)} %get-tuple-element.64.refs_15_), channel_id=1, source_target_pairs={{0,1},{1,0},{2,3},{3,2},{4,5},{5,4},{6,7},{7,6},{8,9},{9,8},{10,11... | collective-permute-start | bytes 786440 | tf_op jit(solution)/shard_map/far_other_half_2/ppermute | solution.py:28
  53.4 5.0 %collective-permute-start.15 = (bf16[1024,128]{1,0:T(8,128)(2,1)S(1)}, bf16[1024,128]{1,0:T(8,128)(2,1)S(1)}, u32[]{:S(2)}, u32[]{:S(2)}) collective-permute-start(bf16[1024,128]{1,0:T(8,128)(2,1)S(1)} %collective-permute-done.12.refs_9_), channel_id=1, source_target_pairs={{0,1},{1,0},{2,3},{3,2},{4,5},{5,4},{6,7},{7,6},{8,9},{9,8},{10,11... | collective-permute-start | bytes 786440 | tf_op jit(solution)/shard_map/near_other_half_1/ppermute | solution.py:28
  56.6 1.9 %collective-permute-start.18 = (bf16[1024,128]{1,0:T(8,128)(2,1)S(1)}, bf16[1024,128]{1,0:T(8,128)(2,1)S(1)}, u32[]{:S(2)}, u32[]{:S(2)}) collective-permute-start(bf16[1024,128]{1,0:T(8,128)(2,1)S(1)} %collective-permute-done.17.refs_13_), channel_id=1, source_target_pairs={{0,1},{1,0},{2,3},{3,2},{4,5},{5,4},{6,7},{7,6},{8,9},{9,8},{10,11... | collective-permute-start | bytes 786440 | tf_op jit(solution)/shard_map/near_other_half_2/ppermute | solution.py:28
  56.8 9.9 %collective-permute-start.9 = (bf16[1024,128]{1,0:T(8,128)(2,1)S(1)}, bf16[1024,128]{1,0:T(8,128)(2,1)S(1)}, u32[]{:S(2)}, u32[]{:S(2)}) collective-permute-start(bf16[1024,128]{1,0:T(8,128)(2,1)S(1)} %get-tuple-element.48), channel_id=1, source_target_pairs={{0,2},{2,0},{4,6},{6,4},{8,10},{10,8},{12,14},{14,12},{1,3},{3,1},... | collective-permute-start | bytes 786440 | tf_op jit(solution)/shard_map/near_3/ppermute | solution.py:33
  58.3 8.9 %collective-permute-start.21 = (bf16[1024,128]{1,0:T(8,128)(2,1)S(1)}, bf16[1024,128]{1,0:T(8,128)(2,1)S(1)}, u32[]{:S(2)}, u32[]{:S(2)}) collective-permute-start(bf16[1024,128]{1,0:T(8,128)(2,1)S(1)} %get-tuple-element.66.refs_7_), channel_id=1, source_target_pairs={{0,1},{1,0},{2,3},{3,2},{4,5},{5,4},{6,7},{7,6},{8,9},{9,8},{10,11... | collective-permute-start | bytes 786440 | tf_op jit(solution)/shard_map/far_other_half_3/ppermute | solution.py:28
  66.8 1.6 %collective-permute-start.20 = (bf16[1024,128]{1,0:T(8,128)(2,1)S(1)}, bf16[1024,128]{1,0:T(8,128)(2,1)S(1)}, u32[]{:S(2)}, u32[]{:S(2)}) collective-permute-start(bf16[1024,128]{1,0:T(8,128)(2,1)S(1)} %collective-permute-done.9.refs_5_), channel_id=1, source_target_pairs={{0,1},{1,0},{2,3},{3,2},{4,5},{5,4},{6,7},{7,6},{8,9},{9,8},{10,11... | collective-permute-start | bytes 786440 | tf_op jit(solution)/shard_map/near_other_half_3/ppermute | solution.py:28
